TPU v7x, 32 devices: a whole 2x2x4 slice. The times are simulated.
32 devices in a mesh: replica: 4 (over y, x), fsdp: 4 (over z), tensor: 2 (over core).
Axes of the slice: x: 2, y: 2, z: 4, core: 2. Of those that a mesh axis runs over, the one named last changes fastest.
Arguments:
- tokens: bfloat16 [4, 16, 4096], P('replica', ('fsdp', 'tensor')), may hold values from -6 to 6
- d_out: bfloat16 [4, 16, 4096], P('replica', ('fsdp', 'tensor')), may hold values from -6 to 6
- w_gate: bfloat16 [4096, 15360], P(None, ('fsdp', 'tensor')), may hold values from -0.09375 to 0.09375
- w_up: bfloat16 [4096, 15360], P(None, ('fsdp', 'tensor')), may hold values from -0.09375 to 0.09375
- w_down: bfloat16 [15360, 4096], P(('fsdp', 'tensor')), may hold values from -0.046875 to 0.046875
- failed: int32 [8], P(('fsdp', 'tensor')), may hold values from 0 to 3
- master: float32 [2, 15360, 4096], P(None, ('fsdp', 'tensor'), 'replica'), may hold values from -6 to 6
- moment1: float32 [2, 15360, 4096], P(None, ('fsdp', 'tensor'), 'replica'), may hold values from -4 to 4
- moment2: float32 [2, 15360, 4096], P(None, ('fsdp', 'tensor'), 'replica'), may hold values from 0.1 to 1
Outputs:
- d_tokens: bfloat16 [4, 16, 4096], P('replica', ('fsdp', 'tensor'))
- master_new: float32 [15360, 4096], P(('fsdp', 'tensor'), 'replica')
- moment1_new: float32 [15360, 4096], P(('fsdp', 'tensor'), 'replica')
- moment2_new: float32 [15360, 4096], P(('fsdp', 'tensor'), 'replica')
All inputs are finite; a program needn't handle non-finite values.
Results may differ from a plain program's by a relative error of at most 0.0049.
Values may be sent and summed in bfloat16 or wider, within the bound.
No kernel may reach another device: no remote copies, remote signals or barrier semaphores. Data moves between devices by JAX's collectives and lax.ppermute only.
A program may use at most 256 MiB of HBM per device.

v0:
```python
import jax
import jax.numpy as jnp
from jax import lax
from jax.sharding import PartitionSpec as P


def from_behind(block, axis, distance):
    devices = range(lax.axis_size(axis))
    route = [((i - distance) % len(devices), i) for i in devices]
    return lax.ppermute(block, axis, route)


def per_device(tokens, d_out, w_gate, w_up, w_down, failed, master, moment1, moment2):
    rows = tokens[0]
    grads_out = d_out[0]
    replicas = lax.axis_size("replica")
    row_piece = lax.all_gather(rows, ("fsdp", "tensor"), axis=0, tiled=True)
    out_piece = lax.all_gather(grads_out, ("fsdp", "tensor"), axis=0, tiled=True)
    gate = jnp.dot(row_piece, w_gate, preferred_element_type=jnp.float32)
    up = jnp.dot(row_piece, w_up, preferred_element_type=jnp.float32)
    sig = 1.0 / (1.0 + jnp.exp(-gate))
    hidden = (gate * sig * up).astype(jnp.bfloat16)
    d_hidden = lax.dot_general(
        out_piece, w_down, (((1,), (1,)), ((), ())), preferred_element_type=jnp.float32
    )
    d_gate = (d_hidden * up * sig * (1.0 + gate * (1.0 - sig))).astype(jnp.bfloat16)
    d_up = (d_hidden * gate * sig).astype(jnp.bfloat16)
    hidden, d_gate, d_up = (hidden, d_gate, d_up)
    grad_down = lax.dot_general(
        hidden, out_piece, (((0,), (0,)), ((), ())), preferred_element_type=jnp.float32
    )
    d_rows = lax.dot_general(
        d_gate, w_gate, (((1,), (1,)), ((), ())), preferred_element_type=jnp.float32
    )
    partial_value = d_rows + lax.dot_general(
        d_up, w_up, (((1,), (1,)), ((), ())), preferred_element_type=jnp.float32
    )
    folded = (grad_down, partial_value)
    grad_down = folded[0]
    d_rows = lax.psum_scatter(folded[1], ("fsdp", "tensor"), scatter_dimension=0, tiled=True)
    d_tokens = d_rows.astype(jnp.bfloat16)[None]
    failed_id = failed[0]
    own_index = lax.axis_index("replica")
    keep = (own_index != failed_id).astype(jnp.float32)
    grad = lax.psum_scatter(grad_down * keep, "replica", scatter_dimension=1, tiled=True) / (
        replicas - 1.0
    )
    backup = from_behind((master[1], moment1[1], moment2[1]), "replica", -1)
    lost = own_index == failed_id
    master_old = jnp.where(lost, backup[0], master[0])
    first_old = jnp.where(lost, backup[1], moment1[0])
    second_old = jnp.where(lost, backup[2], moment2[0])
    first_new = 0.9 * first_old + 0.1 * grad
    second_new = 0.95 * second_old + 0.05 * grad * grad
    master_new = master_old - 0.01 * first_new / (jnp.sqrt(second_new) + 1e-08)
    return (d_tokens, master_new, first_new, second_new)


def solution(mesh):
    placed = (
        P("replica", ("fsdp", "tensor"), None),
        P("replica", ("fsdp", "tensor"), None),
        P(None, ("fsdp", "tensor")),
        P(None, ("fsdp", "tensor")),
        P(("fsdp", "tensor"), None),
        P(("fsdp", "tensor")),
        P(None, ("fsdp", "tensor"), "replica"),
        P(None, ("fsdp", "tensor"), "replica"),
        P(None, ("fsdp", "tensor"), "replica"),
    )
    return jax.shard_map(
        per_device,
        mesh=mesh,
        in_specs=placed,
        out_specs=(
            P("replica", ("fsdp", "tensor"), None),
            P(("fsdp", "tensor"), "replica"),
            P(("fsdp", "tensor"), "replica"),
            P(("fsdp", "tensor"), "replica"),
        ),
        check_vma=False,
    )
```

profile of v0, /device:TPU:0, one launch (start us, length us, event | category | flops | bytes accessed | tf_op | source)
XLA Modules:
  0.0 870.2 jit_solution(10824514009610968534)
XLA Ops:
  7.2 0.0 reduce-scatter.2.cloned.1.call-start
  7.2 0.7 copy.16
  8.0 15.9 %all-gather.1 = bf16[1,16,4096]{2,0,1:T(2,128)(2,1)S(1)} all-gather(bf16[1,2,4096]{2,0,1:T(2,128)(2,1)S(1)} %copy.16), channel_id=3, replica_groups=mesh['replica'=4,'fsdp'=4,'tensor'=2] {'fsdp','tensor'}, dimensions={1}, use_global_device_ids=true | all-gather | bytes 147456 | tf_op jit(solution)/shard_map/all_gather | solution.py:17
  23.8 0.7 copy.15
  24.6 14.2 %all-gather = bf16[1,16,4096]{2,0,1:T(2,128)(2,1)S(1)} all-gather(bf16[1,2,4096]{2,0,1:T(2,128)(2,1)S(1)} %copy.15), channel_id=2, replica_groups=mesh['replica'=4,'fsdp'=4,'tensor'=2] {'fsdp','tensor'}, dimensions={1}, use_global_device_ids=true | all-gather | bytes 147456 | tf_op jit(solution)/shard_map/all_gather | solution.py:18
  38.8 0.0 copy-start
  38.8 7.8 fusion.5
  46.6 2.1 copy-done
  48.7 2.2 fusion.7
  51.6 12.4 %broadcast_multiply_fusion = f32[1920,4096]{1,0:T(8,128)} fusion(f32[]{:T(128)S(6)} %convert_element_type.19, f32[16,1920]{1,0:T(8,128)S(1)} %fusion.7, f32[16,1920]{1,0:T(8,128)S(1)} %fusion.5, bf16[1,16,4096]{2,0,1:T(2,128)(2,1)S(1)} %all-gather), kind=kOutput, calls=%fused_computation | convolution fusion | flops 259706880 | bytes 31834116 | tf_op jit(solution)/shard_map/dot_general | solution.py:29
  64.0 0.0 reduce-scatter.2.cloned.1.call-update
  64.1 0.0 slice-start
  64.1 0.0 slice-start.1
  64.1 8.3 slice_bitcast_fusion.2
  72.3 0.0 slice-start.2
  72.3 0.0 slice-start.3
  72.3 2.3 collective-permute-start
  74.7 8.4 slice_bitcast_fusion.1
  83.0 1.1 collective-permute-start.1
  84.1 0.0 slice-done
  84.1 0.0 slice-done.1
  84.1 0.0 slice-done.2
  84.1 0.0 slice-done.3
  84.2 4.0 slice_bitcast_fusion
  88.2 1.3 collective-permute-start.2
  89.4 9.6 %fusion.10 = f32[16,1920]{1,0:T(8,128)S(1)} fusion(bf16[1920,4096]{1,0:T(8,128)(2,1)} %param.13, bf16[1,16,4096]{2,0,1:T(2,128)(2,1)S(1)} %all-gather), kind=kOutput, calls=%fused_computation.18 | convolution fusion | flops 251658240 | bytes 15982592 | tf_op jit(solution)/shard_map/dot_general | solution.py:23
  99.1 9.6 %fusion.12 = f32[16,4096]{1,0:T(8,128)S(1)} fusion(bf16[4096,1920]{1,0:T(8,128)(2,1)} %param.11, f32[16,1920]{1,0:T(8,128)S(1)} %fusion.5, f32[16,1920]{1,0:T(8,128)S(1)} %fusion.10, f32[16,1920]{1,0:T(8,128)S(1)} %fusion.7), kind=kOutput, calls=%fused_computation.24 | convolution fusion | flops 251965440 | bytes 16359424 | tf_op jit(solution)/shard_map/dot_general | solution.py:32
  108.7 0.0 copy-start.1
  108.7 9.7 %convolution_add_fusion = f32[16,4096]{1,0:T(8,128)S(1)} fusion(f32[16,4096]{1,0:T(8,128)S(1)} %fusion.12, bf16[4096,1920]{1,0:T(8,128)(2,1)} %param.12, f32[16,1920]{1,0:T(8,128)S(1)} %fusion.10, f32[16,1920]{1,0:T(8,128)S(1)} %fusion.5), kind=kOutput, calls=%fused_computation.12 | convolution fusion | flops 251908096 | bytes 16498688 | tf_op jit(solution)/shard_map/dot_general | solution.py:35
  118.4 0.0 copy-done.1
  118.4 0.6 dynamic-slice
  119.6 31.9 %all-reduce.2 = bf16[16,4096]{1,0:T(8,128)(2,1)S(1)} all-reduce(f32[16,4096]{1,0:T(8,128)S(1)} %convolution_add_fusion), channel_id=4, replica_groups=mesh['replica'=4,'fsdp'=4,'tensor'=2] {'fsdp','tensor'}, use_global_device_ids=true, to_apply=%region_0.0.clone | all-reduce | flops 65536 | bytes 393216
  151.5 0.6 fusion.20
  152.2 259.1 %collective-permute-done = f32[1920,1024]{1,0:T(8,128)} collective-permute-done((f32[1920,1024]{1,0:T(8,128)}, f32[1920,1024]{1,0:T(8,128)}, u32[]{:S(2)}, u32[]{:S(2)}) %collective-permute-start) | collective-permute-done | bytes 7864352 | tf_op jit(solution)/shard_map/ppermute | solution.py:10
  411.3 168.5 %collective-permute-done.1 = f32[1920,1024]{1,0:T(8,128)} collective-permute-done((f32[1920,1024]{1,0:T(8,128)}, f32[1920,1024]{1,0:T(8,128)}, u32[]{:S(2)}, u32[]{:S(2)}) %collective-permute-start.1) | collective-permute-done | bytes 7864352 | tf_op jit(solution)/shard_map/ppermute | solution.py:10
  579.8 168.3 %collective-permute-done.2 = f32[1920,1024]{1,0:T(8,128)} collective-permute-done((f32[1920,1024]{1,0:T(8,128)}, f32[1920,1024]{1,0:T(8,128)}, u32[]{:S(2)}, u32[]{:S(2)}) %collective-permute-start.2) | collective-permute-done | bytes 7864352 | tf_op jit(solution)/shard_map/ppermute | solution.py:10
  748.1 92.8 %reduce-scatter.2.cloned.1.call-done = f32[1920,1024]{1,0:T(8,128)} async-done(((f32[1920,4096]{1,0:T(8,128)}), f32[1920,1024]{1,0:T(8,128)}) %reduce-scatter.2.cloned.1.call-update) | async-done | bytes 7864336 | tf_op jit(solution)/shard_map/reduce_scatter | solution.py:45
  840.9 22.5 %fusion.4 = (f32[1920,1024]{1,0:T(8,128)}, f32[1920,1024]{1,0:T(8,128)}, f32[1920,1024]{1,0:T(8,128)}) fusion(f32[1920,1024]{1,0:T(8,128)} %collective-permute-done, f32[2,1920,1024]{2,1,0:T(8,128)} %param.15, pred[]{:T(512)S(6)} %eq.3, f32[1920,1024]{1,0:T(8,128)} %reduce-scatter.2.cloned.1.call-done, f32[1920,1024]{1,0:T(8,128)} %collective-permute-done.1, ...), kind=kLoop, calls=%fused_computation.8 | loop fusion | flops 29491200 | bytes 78643200 | tf_op jit(solution)/shard_map/sub | solution.py:55
  (1 shorter events, 0.0 us)
Async XLA Ops:
  7.2 833.8 %reduce-scatter.2.cloned.1.call-start = ((), (), s32[]{:S(2)}) async-start(), calls=%async_computation.1 | async-start | bytes 39321600 | tf_op jit(solution)/shard_map/reduce_scatter | solution.py:45
  38.8 9.9 %copy-start = (bf16[4096,1920]{1,0:T(8,128)(2,1)S(1)}, bf16[4096,1920]{1,0:T(8,128)(2,1)}, u32[]{:S(2)}) copy-start(bf16[4096,1920]{1,0:T(8,128)(2,1)} %param.12) | copy-start | bytes 47185924
  64.1 20.1 %slice-start = ((s8[15728640]{0:T(1024)(128)(4,1)}), s8[4194304]{0:T(1024)(128)(4,1)S(1)}, s32[]{:S(2)}) async-start(s8[15728640]{0:T(1024)(128)(4,1)} %bitcast.45), calls=%async_computation.2 | async-start | bytes 8388608
  64.1 20.1 %slice-start.1 = ((s8[15728640]{0:T(1024)(128)(4,1)}), s8[4194304]{0:T(1024)(128)(4,1)S(1)}, s32[]{:S(2)}) async-start(s8[15728640]{0:T(1024)(128)(4,1)} %bitcast.45), calls=%async_computation.3 | async-start | bytes 8388608
  72.3 11.8 %slice-start.2 = ((s8[15728640]{0:T(1024)(128)(4,1)}), s8[4194304]{0:T(1024)(128)(4,1)S(1)}, s32[]{:S(2)}) async-start(s8[15728640]{0:T(1024)(128)(4,1)} %bitcast.45), calls=%async_computation.4 | async-start | bytes 8388608
  72.3 11.8 %slice-start.3 = ((s8[15728640]{0:T(1024)(128)(4,1)}), s8[3145728]{0:T(1024)(128)(4,1)S(1)}, s32[]{:S(2)}) async-start(s8[15728640]{0:T(1024)(128)(4,1)} %bitcast.45), calls=%async_computation.5 | async-start | bytes 6291456
  72.3 339.0 %collective-permute-start = (f32[1920,1024]{1,0:T(8,128)}, f32[1920,1024]{1,0:T(8,128)}, u32[]{:S(2)}, u32[]{:S(2)}) collective-permute-start(f32[1920,1024]{1,0:T(8,128)} %slice_bitcast_fusion.2), channel_id=1, source_target_pairs={{8,0},{16,8},{24,16},{0,24},{9,1},{17,9},{25,17},{1,25},{10,2},{18... | collective-permute-start | bytes 23592968 | tf_op jit(solution)/shard_map/ppermute | solution.py:10
  83.0 496.8 %collective-permute-start.1 = (f32[1920,1024]{1,0:T(8,128)}, f32[1920,1024]{1,0:T(8,128)}, u32[]{:S(2)}, u32[]{:S(2)}) collective-permute-start(f32[1920,1024]{1,0:T(8,128)} %slice_bitcast_fusion.1), channel_id=1, source_target_pairs={{8,0},{16,8},{24,16},{0,24},{9,1},{17,9},{25,17},{1,25},{10,2},{18... | collective-permute-start | bytes 23592968 | tf_op jit(solution)/shard_map/ppermute | solution.py:10
  88.2 660.0 %collective-permute-start.2 = (f32[1920,1024]{1,0:T(8,128)}, f32[1920,1024]{1,0:T(8,128)}, u32[]{:S(2)}, u32[]{:S(2)}) collective-permute-start(f32[1920,1024]{1,0:T(8,128)} %slice_bitcast_fusion), channel_id=1, source_target_pairs={{8,0},{16,8},{24,16},{0,24},{9,1},{17,9},{25,17},{1,25},{10,2},{18... | collective-permute-start | bytes 23592968 | tf_op jit(solution)/shard_map/ppermute | solution.py:10
  108.7 9.7 %copy-start.1 = (u32[32]{0:T(128)S(1)}, u32[32]{0:T(128)}, u32[]{:S(2)}) copy-start(u32[32]{0:T(128)} %constant.29) | copy-start | bytes 388
Sparse Core Ops, SparseCore 0:
  64.2 776.7 reduce-scatter.1
where the time goes:
time: 875 us; the launch traced here: 870 us
  waiting for transfers between devices  689 us (79%)
  blocking collectives  62 us (7%)
  matrix products  51.4 us (6%)
  local copies, waits for them, and re-layouts  25.5 us (3%)
  other arithmetic  22.5 us (3%)
  between operations  15.4 us (2%)
    ppermute x3, waiting for transfers between devices, from_behind(): return lax.ppermute(block, axis, route)  596 us
    reduce_scatter x1, waiting for transfers between devices, per_device(): lax.psum_scatter(grad_down * keep, 'replica', scatter_dimension=1, tiled=...  92.8 us
    unnamed x1, blocking collectives  31.9 us
    sub x1, other arithmetic, per_device(): master_new = master_old - 0.01 * first_new / (jnp.sqrt(second_new) + 1e-08)  22.5 us
    squeeze x3, local copies, waits for them, and re-layouts, per_device(): backup = from_behind((master[1], moment1[1], moment2[1]), 'replica', -1)  20.6 us
  transfers between devices with their start and end apart: 4, of which 4 were waited for; matrix products, arithmetic and copies ran while one was open for 6% of the time, Pallas kernels for 0%

commit v1 on v0

v1 whole, which is shorter than its diff:
```python
import functools

import jax
import jax.numpy as jnp
from jax import lax
from jax.experimental import pallas as pl
from jax.experimental.pallas import tpu as pltpu
from jax.sharding import PartitionSpec as P

BF16, F32 = jnp.bfloat16, jnp.float32
LAG = 2
MOST_CHUNKS = 20
TILE = 16
VMEM = 48 << 20


def ring_order(n):
    return [0, 1, 3, 2] if n == 4 else list(range(n))


def largest(options, default):
    options = list(options)
    return max(options) if options else default


def updated(first_old, second_old, master_old, grad):
    first_new = 0.9 * first_old + 0.1 * grad
    second_new = 0.95 * second_old + 0.05 * grad * grad
    master_new = master_old - 0.01 * first_new / (jnp.sqrt(second_new) + 1e-08)
    return master_new, first_new, second_new


def pack_body(flag, *refs):
    ahead, behind = refs[0:3], refs[3:6]
    sends = refs[-2:]
    got = refs[6:-2]
    for own, send, seen in zip((ahead, behind), sends, got or (None, None)):
        if seen is None:
            for k in range(3):
                send[k] = own[k][0].astype(BF16)
        else:

            @pl.when(flag[0] == 1)
            def _(own=own, send=send):
                for k in range(3):
                    send[k] = own[k][0].astype(BF16)

            @pl.when(flag[0] == 0)
            def _(send=send, seen=seen):
                send[...] = seen[...]


def pack(is_source, state, got, chunk_ahead, chunk_behind, chunk):
    width = state[0].shape[2]
    half = chunk // 2 if chunk % (2 * TILE) == 0 else chunk
    pieces = chunk // half

    def own(index):
        return pl.BlockSpec((1, half, width), lambda i, s: (1, index * pieces + i, 0))

    moved = pl.BlockSpec((3, half, width), lambda i, s: (0, i, 0))
    shape = jax.ShapeDtypeStruct((3, chunk, width), BF16)
    return pl.pallas_call(
        pack_body,
        grid_spec=pltpu.PrefetchScalarGridSpec(
            num_scalar_prefetch=1,
            grid=(pieces,),
            in_specs=[own(chunk_ahead)] * 3 + [own(chunk_behind)] * 3 + [moved] * len(got),
            out_specs=[moved, moved],
        ),
        out_shape=[shape, shape],
        compiler_params=pltpu.CompilerParams(vmem_limit_bytes=VMEM),
        cost_estimate=pl.CostEstimate(
            flops=0, bytes_accessed=2 * 3 * chunk * width * 8, transcendentals=0
        ),
        name="pack",
    )(is_source, *state, *state, *got)


def update_body(hid_ref, out_ref, m_ref, a_ref, b_ref, m_new, a_new, b_new, *, scale):
    grad = jnp.dot(hid_ref[...], out_ref[...], preferred_element_type=F32) * scale
    m_new[...], a_new[...], b_new[...] = updated(a_ref[0], b_ref[0], m_ref[0], grad)


def update(hidden_t, outs, state, scale):
    _, rows, width = state[0].shape
    depth = hidden_t.shape[1]
    block = largest((b for b in range(TILE, 193, TILE) if rows % b == 0), rows)
    spec = pl.BlockSpec((1, block, width), lambda i: (0, i, 0))
    out = pl.BlockSpec((block, width), lambda i: (i, 0))
    shape = jax.ShapeDtypeStruct((rows, width), F32)
    return pl.pallas_call(
        functools.partial(update_body, scale=scale),
        grid=(rows // block,),
        in_specs=[
            pl.BlockSpec((block, depth), lambda i: (i, 0)),
            pl.BlockSpec((depth, width), lambda i: (0, 0)),
            spec,
            spec,
            spec,
        ],
        out_specs=[out] * 3,
        out_shape=[shape] * 3,
        compiler_params=pltpu.CompilerParams(vmem_limit_bytes=VMEM),
        cost_estimate=pl.CostEstimate(
            flops=2 * rows * width * depth,
            bytes_accessed=6 * rows * width * 4,
            transcendentals=2 * rows * width,
        ),
        name="update",
    )(hidden_t, outs, *state)


def patch_body(info, hid_ref, out_ref, *refs, arrivals, chunks, n, scale):
    count = len(arrivals)
    got = refs[:count]
    news = refs[count + 3 : count + 6]
    held, made, in_sem, out_sem = refs[count + 6 :]
    chunk = held.shape[2]
    part = largest((p for p in (16, 32) if chunk % p == 0), chunk)
    ahead = info[1]
    lag_of = {True: LAG * (ahead - 1), False: LAG * (n - ahead - 1)}

    def fetch(j):
        return pltpu.make_async_copy(got[j], held.at[j % 2], in_sem.at[j % 2])

    def first_row(j):
        step, forward = arrivals[j]
        place = step - lag_of[forward]
        if not forward:
            place = chunks - 1 - place
        return pl.multiple_of(jnp.clip(place, 0, chunks - 1) * chunk, TILE)

    def store(j, k):
        return pltpu.make_async_copy(
            made.at[j % 2, k], news[k].at[pl.ds(first_row(j), chunk)], out_sem.at[j % 2, k]
        )

    def valid(j):
        step, forward = arrivals[j]
        return step >= lag_of[forward]

    def finish(j):
        @pl.when(valid(j))
        def _():
            for k in range(3):
                store(j, k).wait()

    @pl.when(info[0] == 1)
    def _():
        fetch(0).start()
        for j in range(count):
            slot = j % 2
            if j + 1 < count:
                fetch(j + 1).start()
            fetch(j).wait()
            if j >= 2:
                finish(j - 2)

            @pl.when(valid(j))
            def _(j=j, slot=slot):
                first = first_row(j)

                @pl.loop(0, chunk // part)
                def _(i):
                    base = pl.multiple_of(i * part, part)
                    here = pl.ds(base, part)
                    units = hid_ref[pl.ds(pl.multiple_of(first + base, TILE), part)]
                    grad = jnp.dot(units, out_ref[...], preferred_element_type=F32) * scale
                    old = [held[slot, k, here].astype(F32) for k in range(3)]
                    new = updated(old[1], old[2], old[0], grad)
                    for k in range(3):
                        made[slot, k, here] = new[k]

                for k in range(3):
                    store(j, k).start()

        for j in range(max(count - 2, 0), count):
            finish(j)


def patch(info, hidden_t, outs, got, arrivals, news, chunks, n, scale):
    rows, width = news[0].shape
    chunk = rows // chunks
    count = len(got)
    any_spec = pl.BlockSpec(memory_space=pl.ANY)
    whole = pl.BlockSpec(memory_space=pltpu.VMEM)
    shape = jax.ShapeDtypeStruct((rows, width), F32)
    return pl.pallas_call(
        functools.partial(patch_body, arrivals=arrivals, chunks=chunks, n=n, scale=scale),
        in_specs=[pl.BlockSpec(memory_space=pltpu.SMEM), whole, whole]
        + [any_spec] * (count + 3),
        out_specs=[any_spec] * 3,
        out_shape=[shape] * 3,
        scratch_shapes=[
            pltpu.VMEM((2, 3, chunk, width), BF16),
            pltpu.VMEM((2, 3, chunk, width), F32),
            pltpu.SemaphoreType.DMA((2,)),
            pltpu.SemaphoreType.DMA((2, 3)),
        ],
        input_output_aliases={3 + count + k: k for k in range(3)},
        compiler_params=pltpu.CompilerParams(vmem_limit_bytes=VMEM),
        cost_estimate=pl.CostEstimate(
            flops=2 * count * chunk * width * hidden_t.shape[1],
            bytes_accessed=count * 3 * chunk * width * 6,
            transcendentals=2 * count * chunk * width,
        ),
        name="patch",
    )(info, hidden_t, outs, *got, *news)


def halved(x, axis, dim):
    size = lax.axis_size(axis)
    me = lax.axis_index(axis)
    if size & (size - 1):
        return lax.psum_scatter(x, axis, scatter_dimension=dim, tiled=True)
    while size > 1:
        half = size // 2
        length = x.shape[dim] // 2
        bit = (me // half) % 2
        kept = lax.dynamic_slice_in_dim(x, bit * length, length, dim)
        sent = lax.dynamic_slice_in_dim(x, (1 - bit) * length, length, dim)
        route = [(i, i ^ half) for i in range(lax.axis_size(axis))]
        x = kept + lax.ppermute(sent, axis, route)
        size = half
    return x


def per_device(tokens, d_out, w_gate, w_up, w_down, failed, master, moment1, moment2):
    n = lax.axis_size("replica")
    me = lax.axis_index("replica")
    fsdp, tensor = lax.axis_size("fsdp"), lax.axis_size("tensor")
    _, rows, width = master.shape
    scale = 1.0 / (n - 1.0)

    failed_id = failed[0]
    source = (failed_id + 1) % n
    order = ring_order(n)
    place = jnp.array([order.index(i) for i in range(n)], jnp.int32)
    ahead = (place[failed_id] - place[source]) % n
    is_source = (me == source).astype(jnp.int32)[None]
    info = jnp.stack([(me == failed_id).astype(jnp.int32), ahead.astype(jnp.int32)])

    state = (master, moment1, moment2)
    chunks = largest(
        (c for c in range(2, MOST_CHUNKS + 1, 2) if rows % (TILE * c) == 0), 2
    )
    chunk = rows // chunks
    steps = (chunks + LAG * (n - 2)) // 2
    forward = [(order[p], order[(p + 1) % n]) for p in range(n)]
    backward = [(b, a) for a, b in forward]
    got = []
    for step in range(steps):
        seen = got[step - LAG] if step >= LAG else ()
        here = min(step, chunks - 1)
        sends = pack(is_source, state, seen, here, chunks - 1 - here, chunk)
        got.append(
            (
                lax.ppermute(sends[0], "replica", forward),
                lax.ppermute(sends[1], "replica", backward),
            )
        )

    both = jnp.concatenate([tokens[0], d_out[0]], axis=1)
    both = lax.all_gather(both, ("fsdp", "tensor"), axis=0, tiled=True)
    features = tokens.shape[2]
    x, dy = both[:, :features], both[:, features:]
    gate = jnp.dot(x, w_gate, preferred_element_type=F32)
    up = jnp.dot(x, w_up, preferred_element_type=F32)
    sig = 1.0 / (1.0 + jnp.exp(-gate))
    hidden = (gate * sig * up).astype(BF16)
    d_hidden = lax.dot_general(dy, w_down, (((1,), (1,)), ((), ())), preferred_element_type=F32)
    d_gate = (d_hidden * up * sig * (1.0 + gate * (1.0 - sig))).astype(BF16)
    d_up = (d_hidden * gate * sig).astype(BF16)
    d_rows = lax.dot_general(
        d_gate, w_gate, (((1,), (1,)), ((), ())), preferred_element_type=F32
    ) + lax.dot_general(d_up, w_up, (((1,), (1,)), ((), ())), preferred_element_type=F32)

    kept = jnp.where(me == failed_id, jnp.zeros_like(hidden), hidden)

    def parcel(to):
        slab = lax.dynamic_slice_in_dim(dy, to * width, width, 1)
        return jnp.concatenate([kept, slab], axis=1)

    parcels = [parcel(me)]
    for far in range(1, n):
        route = [(i, (i + far) % n) for i in range(n)]
        parcels.append(lax.ppermute(parcel((me + far) % n), "replica", route))
    parcels = jnp.concatenate(parcels, axis=0)
    hidden_t = parcels[:, :rows].T
    outs = parcels[:, rows:]

    d_rows = d_rows.reshape(fsdp, tensor, -1, features)
    d_rows = halved(halved(d_rows, "tensor", 1), "fsdp", 0)
    d_tokens = d_rows.reshape(1, -1, features).astype(BF16)

    news = update(hidden_t, outs, state, scale)
    for group in (range(steps - 1), range(steps - 1, steps)):
        arrivals = [(step, way) for step in group for way in (True, False)]
        blocks = [block for step in group for block in got[step]]
        news = patch(info, hidden_t, outs, blocks, arrivals, news, chunks, n, scale)
    return (d_tokens, *news)


def solution(mesh):
    placed = (
        P("replica", ("fsdp", "tensor"), None),
        P("replica", ("fsdp", "tensor"), None),
        P(None, ("fsdp", "tensor")),
        P(None, ("fsdp", "tensor")),
        P(("fsdp", "tensor"), None),
        P(("fsdp", "tensor")),
        P(None, ("fsdp", "tensor"), "replica"),
        P(None, ("fsdp", "tensor"), "replica"),
        P(None, ("fsdp", "tensor"), "replica"),
    )
    return jax.shard_map(
        per_device,
        mesh=mesh,
        in_specs=placed,
        out_specs=(
            P("replica", ("fsdp", "tensor"), None),
            P(("fsdp", "tensor"), "replica"),
            P(("fsdp", "tensor"), "replica"),
            P(("fsdp", "tensor"), "replica"),
        ),
        check_vma=False,
    )
```

time: 875 us -> 248 us (0.28)
  the two profiles are of different devices: /device:TPU:0 before, /device:TPU:16 now
where the time goes in v1:
time: 248 us; the launch traced here: 246 us
  Pallas kernels  75.7 us (31%)
  waiting for transfers between devices  60.1 us (24%)
  matrix products  45.6 us (18%)
  starting transfers between devices  35.1 us (14%)
  blocking collectives  12.5 us (5%)
  local copies, waits for them, and re-layouts  8.23 us (3%)
  other arithmetic  5.51 us (2%)
  between operations  3.25 us (1%)
    ppermute x12, waiting for transfers between devices, per_device(): lax.ppermute(sends[0], 'replica', forward)  35.3 us
    pallas_call x12, Pallas kernels, pack(): pl.pallas_call(pack_body, grid_spec=pltpu.PrefetchScalarGridSpec(num_scal...  28.4 us
    pallas_call x2, Pallas kernels, patch(): pl.pallas_call(functools.partial(patch_body, arrivals=arrivals, chunks=ch...  27 us
    pallas_call x1, Pallas kernels, update(): pl.pallas_call(functools.partial(update_body, scale=scale), grid=(rows //...  20.3 us
    ppermute x3, waiting for transfers between devices, per_device(): parcels.append(lax.ppermute(parcel((me + far) % n), 'replica', route))  18.1 us
    ppermute x12, starting transfers between devices, per_device(): lax.ppermute(sends[1], 'replica', backward)  15.7 us
    all_gather x1, blocking collectives, per_device(): both = lax.all_gather(both, ('fsdp', 'tensor'), axis=0, tiled=True)  12.5 us
    dot_general x1, matrix products, per_device(): lax.dot_general(d_up, w_up, (((1,), (1,)), ((), ())), preferred_element_t...  10.4 us
  transfers between devices with their start and end apart: 30, of which 11 were waited for; matrix products, arithmetic and copies ran while one was open for 16% of the time, Pallas kernels for 29%

profile of v1, /device:TPU:16, one launch (start us, length us, event | category | flops | bytes accessed | tf_op | source)
XLA Modules:
  0.0 245.9 jit_solution(13985619478690336375)
XLA Ops:
  1.4 12.5 %all-gather = bf16[8,2,8192]{2,1,0:T(2,128)(2,1)S(1)} all-gather(bf16[1,2,8192]{2,1,0:T(2,128)(2,1)S(1)} %maximum_bitcast_fusion), channel_id=1, replica_groups=mesh['replica'=4,'fsdp'=4,'tensor'=2] {'fsdp','tensor'}, dimensions={0}, use_global_device_ids=true | all-gather | bytes 294912 | tf_op jit(solution)/shard_map/all_gather | solution.py:265
  14.7 7.6 %fusion = f32[16,1920]{1,0:T(8,128)S(1)} fusion(bf16[4096,1920]{1,0:T(8,128)(2,1)} %param.12, bf16[16,8192]{1,0:T(8,128)(2,1)S(1)} %reshape.30), kind=kOutput, calls=%fused_computation.9 | convolution fusion | flops 251658240 | bytes 15982592 | tf_op jit(solution)/shard_map/dot_general | solution.py:268
  22.4 8.3 %broadcast_select_fusion = (bf16[16,1920]{1,0:T(8,128)(2,1)S(1)}, f32[16,1920]{1,0:T(8,128)}) fusion(pred[]{:T(512)S(6)} %eq.16, f32[16,1920]{1,0:T(8,128)S(1)} %fusion, bf16[4096,1920]{1,0:T(8,128)(2,1)} %param.13, bf16[16,8192]{1,0:T(8,128)(2,1)S(1)} %reshape.30), kind=kOutput, calls=%fused_computation.20 | convolution fusion | flops 251873280 | bytes 16166913 | tf_op jit(solution)/shard_map/dot_general | solution.py:269
  32.1 1.5 collective-permute-start.3
  33.6 2.5 %pack.18 = (bf16[3,96,1024]{2,1,0:T(8,128)(2,1)}, bf16[3,96,1024]{2,1,0:T(8,128)(2,1)S(1)}) custom-call(s32[1]{0:T(128)} %bitcast.9.flag, f32[2,1920,1024]{2,1,0:T(8,128)} %m_ref.1, f32[2,1920,1024]{2,1,0:T(8,128)} %a_ref.1, f32[2,1920,1024]{2,1,0:T(8,128)} %b_ref.1, f32[2,1920,1024]{2,1,0:T(8,128)} %m_ref.1, f32[2,1920,1024]{2,1,0:T(8,128)} %a_ref.1, ...), custom_call_target="tpu_custom_call" | custom-call | bytes 4718592 | tf_op jit(solution)/shard_map/pack/pallas_call | solution.py:63
  36.1 1.5 collective-permute-start.18
  38.1 2.5 %pack.12 = (bf16[3,96,1024]{2,1,0:T(8,128)(2,1)}, bf16[3,96,1024]{2,1,0:T(8,128)(2,1)S(1)}) custom-call(s32[1]{0:T(128)} %bitcast.9.flag, f32[2,1920,1024]{2,1,0:T(8,128)} %m_ref.1, f32[2,1920,1024]{2,1,0:T(8,128)} %a_ref.1, f32[2,1920,1024]{2,1,0:T(8,128)} %b_ref.1, f32[2,1920,1024]{2,1,0:T(8,128)} %m_ref.1, f32[2,1920,1024]{2,1,0:T(8,128)} %a_ref.1, ...), custom_call_target="tpu_custom_call" | custom-call | bytes 4718592 | tf_op jit(solution)/shard_map/pack/pallas_call | solution.py:63
  40.6 1.5 collective-permute-start.6
  42.7 9.6 %fusion.10 = f32[16,1920]{1,0:T(8,128)S(1)} fusion(bf16[1920,4096]{1,0:T(8,128)(2,1)} %param.14, bf16[16,8192]{1,0:T(8,128)(2,1)S(1)} %copy-done.16), kind=kOutput, calls=%fused_computation.34 | convolution fusion | flops 251658240 | bytes 15982592 | tf_op jit(solution)/shard_map/dot_general | solution.py:272
  52.3 9.6 %fusion.4 = f32[16,4096]{1,0:T(8,128)S(1)} fusion(bf16[4096,1920]{1,0:T(8,128)(2,1)} %param.12, f32[16,1920]{1,0:T(8,128)S(1)} %copy-done.18, f32[16,1920]{1,0:T(8,128)S(1)} %fusion.10, f32[16,1920]{1,0:T(8,128)S(1)} %copy-done.25), kind=kOutput, calls=%fused_computation.17 | convolution fusion | flops 251965440 | bytes 16359424 | tf_op jit(solution)/shard_map/dot_general | solution.py:275
  61.9 10.4 %convolution_add_fusion = f32[16,4096]{1,0:T(8,128)} fusion(f32[16,4096]{1,0:T(8,128)S(1)} %fusion.4, bf16[4096,1920]{1,0:T(8,128)(2,1)} %param.13, f32[16,1920]{1,0:T(8,128)S(1)} %fusion.10, f32[16,1920]{1,0:T(8,128)S(1)} %copy-done.18), kind=kOutput, calls=%fused_computation | convolution fusion | flops 251908096 | bytes 16498688 | tf_op jit(solution)/shard_map/dot_general | solution.py:277
  72.3 1.8 reshape.26
  74.1 1.5 collective-permute-start.4
  75.6 2.6 %pack.19 = (bf16[3,96,1024]{2,1,0:T(8,128)(2,1)}, bf16[3,96,1024]{2,1,0:T(8,128)(2,1)}) custom-call(s32[1]{0:T(128)} %bitcast.9.flag, f32[2,1920,1024]{2,1,0:T(8,128)} %m_ref.1, f32[2,1920,1024]{2,1,0:T(8,128)} %a_ref.1, f32[2,1920,1024]{2,1,0:T(8,128)} %b_ref.1, f32[2,1920,1024]{2,1,0:T(8,128)} %m_ref.1, f32[2,1920,1024]{2,1,0:T(8,128)} %a_ref.1, ...), custom_call_target="tpu_custom_call" | custom-call | bytes 4718592 | tf_op jit(solution)/shard_map/pack/pallas_call | solution.py:63
  78.8 1.5 collective-permute-start.21
  80.3 2.6 %pack.13 = (bf16[3,96,1024]{2,1,0:T(8,128)(2,1)}, bf16[3,96,1024]{2,1,0:T(8,128)(2,1)}) custom-call(s32[1]{0:T(128)} %bitcast.9.flag, f32[2,1920,1024]{2,1,0:T(8,128)} %m_ref.1, f32[2,1920,1024]{2,1,0:T(8,128)} %a_ref.1, f32[2,1920,1024]{2,1,0:T(8,128)} %b_ref.1, f32[2,1920,1024]{2,1,0:T(8,128)} %m_ref.1, f32[2,1920,1024]{2,1,0:T(8,128)} %a_ref.1, ...), custom_call_target="tpu_custom_call" | custom-call | bytes 4718592 | tf_op jit(solution)/shard_map/pack/pallas_call | solution.py:63
  83.5 1.5 collective-permute-start.9
  89.2 18.1 %collective-permute-done.5 = bf16[16,2944]{1,0:T(8,128)(2,1)S(1)} collective-permute-done((bf16[16,2944]{1,0:T(8,128)(2,1)}, bf16[16,2944]{1,0:T(8,128)(2,1)S(1)}, u32[]{:S(2)}, u32[]{:S(2)}) %collective-permute-start.5) | collective-permute-done | bytes 94240 | tf_op jit(solution)/shard_map/ppermute | solution.py:288
  108.3 2.0 pack.20
  110.4 1.6 collective-permute-start.22
  112.5 2.1 pack.14
  114.5 1.6 collective-permute-start.10
  116.7 9.9 %collective-permute-done.22.refs_6_.refs_8_ = bf16[3,96,1024]{2,1,0:T(8,128)(2,1)S(1)} collective-permute-done((bf16[3,96,1024]{2,1,0:T(8,128)(2,1)S(1)}, bf16[3,96,1024]{2,1,0:T(8,128)(2,1)S(1)}, u32[]{:S(2)}, u32[]{:S(2)}) %collective-permute-start.22) | collective-permute-done | bytes 589856 | tf_op jit(solution)/shard_map/ppermute | solution.py:259
  126.6 1.6 collective-permute-done.23.refs_7_.refs_9_
  128.2 2.0 pack.21
  130.5 1.8 collective-permute-start.25
  132.3 6.9 %collective-permute-done.10.refs_6_.refs_10_ = bf16[3,96,1024]{2,1,0:T(8,128)(2,1)S(1)} collective-permute-done((bf16[3,96,1024]{2,1,0:T(8,128)(2,1)S(1)}, bf16[3,96,1024]{2,1,0:T(8,128)(2,1)S(1)}, u32[]{:S(2)}, u32[]{:S(2)}) %collective-permute-start.10) | collective-permute-done | bytes 589856 | tf_op jit(solution)/shard_map/ppermute | solution.py:259
  139.2 1.6 collective-permute-done.11.refs_7_.refs_11_
  140.8 2.0 pack.15
  143.2 1.8 collective-permute-start.13
  144.9 2.3 collective-permute-start.1
  148.0 3.9 %collective-permute-done.24.refs_6_.refs_12_ = bf16[3,96,1024]{2,1,0:T(8,128)(2,1)S(1)} collective-permute-done((bf16[3,96,1024]{2,1,0:T(8,128)(2,1)S(1)}, bf16[3,96,1024]{2,1,0:T(8,128)(2,1)S(1)}, u32[]{:S(2)}, u32[]{:S(2)}) %collective-permute-start.24) | collective-permute-done | bytes 589856 | tf_op jit(solution)/shard_map/ppermute | solution.py:259
  151.9 1.6 collective-permute-done.25.refs_7_.refs_13_
  153.4 2.8 %pack.22 = (bf16[3,96,1024]{2,1,0:T(8,128)(2,1)}, bf16[3,96,1024]{2,1,0:T(8,128)(2,1)}) custom-call(s32[1]{0:T(128)} %bitcast.9.flag, f32[2,1920,1024]{2,1,0:T(8,128)} %m_ref.1, f32[2,1920,1024]{2,1,0:T(8,128)} %a_ref.1, f32[2,1920,1024]{2,1,0:T(8,128)} %b_ref.1, f32[2,1920,1024]{2,1,0:T(8,128)} %m_ref.1, f32[2,1920,1024]{2,1,0:T(8,128)} %a_ref.1, ...), custom_call_target="tpu_custom_call" | custom-call | bytes 4718592 | tf_op jit(solution)/shard_map/pack/pallas_call | solution.py:63
  156.6 1.8 collective-permute-start.27
  158.3 6.2 %collective-permute-done.12.refs_6_.refs_14_ = bf16[3,96,1024]{2,1,0:T(8,128)(2,1)S(1)} collective-permute-done((bf16[3,96,1024]{2,1,0:T(8,128)(2,1)S(1)}, bf16[3,96,1024]{2,1,0:T(8,128)(2,1)S(1)}, u32[]{:S(2)}, u32[]{:S(2)}) %collective-permute-start.12) | collective-permute-done | bytes 589856 | tf_op jit(solution)/shard_map/ppermute | solution.py:259
  164.5 1.6 collective-permute-done.13.refs_7_.refs_15_
  166.1 2.8 %pack.16 = (bf16[3,96,1024]{2,1,0:T(8,128)(2,1)}, bf16[3,96,1024]{2,1,0:T(8,128)(2,1)}) custom-call(s32[1]{0:T(128)} %bitcast.9.flag, f32[2,1920,1024]{2,1,0:T(8,128)} %m_ref.1, f32[2,1920,1024]{2,1,0:T(8,128)} %a_ref.1, f32[2,1920,1024]{2,1,0:T(8,128)} %b_ref.1, f32[2,1920,1024]{2,1,0:T(8,128)} %m_ref.1, f32[2,1920,1024]{2,1,0:T(8,128)} %a_ref.1, ...), custom_call_target="tpu_custom_call" | custom-call | bytes 4718592 | tf_op jit(solution)/shard_map/pack/pallas_call | solution.py:63
  169.2 1.8 collective-permute-start.15
  171.6 3.4 %collective-permute-start.2 = (f32[1,1,2,4096]{3,2,1,0:T(2,128)}, f32[1,1,2,4096]{3,2,1,0:T(2,128)}, u32[]{:S(2)}, u32[]{:S(2)}) collective-permute-start(f32[1,1,2,4096]{3,2,1,0:T(2,128)} %constant_dynamic-slice_fusion.4), channel_id=1, source_target_pairs={{0,2},{2,0},{4,6},{6,4},{1,3},{3,1},{5,7},{7,5},{8,10},{10,8},{12,... | collective-permute-start | bytes 98312 | tf_op jit(solution)/shard_map/ppermute | solution.py:224
  178.6 20.3 %update.1 = (f32[1920,1024]{1,0:T(8,128)}, f32[1920,1024]{1,0:T(8,128)}, f32[1920,1024]{1,0:T(8,128)}) custom-call(bf16[1920,64]{1,0:T(8,128)(2,1)S(1)} %copy.25.hid_ref, bf16[64,1024]{1,0:T(8,128)(2,1)S(1)} %copy-done.13, f32[2,1920,1024]{2,1,0:T(8,128)} %m_ref.1, f32[2,1920,1024]{2,1,0:T(8,128)} %a_ref.1, f32[2,1920,1024]{2,1,0:T(8,128)} %b_ref.1), custom_call_target="tpu_custom_call" | custom-call | flops 251658240 | bytes 47185920 | tf_op jit(solution)/shard_map/update/pallas_call | solution.py:92
  198.9 2.2 pack.23
  201.5 1.8 collective-permute-start.29
  203.3 2.2 pack.17
  205.9 1.7 collective-permute-start.17
  209.0 8.5 %collective-permute-done.28.refs_20_ = bf16[3,96,1024]{2,1,0:T(8,128)(2,1)S(1)} collective-permute-done((bf16[3,96,1024]{2,1,0:T(8,128)(2,1)S(1)}, bf16[3,96,1024]{2,1,0:T(8,128)(2,1)S(1)}, u32[]{:S(2)}, u32[]{:S(2)}) %collective-permute-start.28) | collective-permute-done | bytes 589856 | tf_op jit(solution)/shard_map/ppermute | solution.py:259
  218.7 23.7 %patch.2 = (f32[1920,1024]{1,0:T(8,128)}, f32[1920,1024]{1,0:T(8,128)}, f32[1920,1024]{1,0:T(8,128)}) custom-call(s32[2]{0:T(128)S(1)} %pad_add_fusion.info, bf16[1920,64]{1,0:T(8,128)(2,1)S(1)} %copy.25.hid_ref, bf16[64,1024]{1,0:T(8,128)(2,1)S(1)} %copy-done.14, ...), custom_call_target="tpu_custom_call", output_to_operand_aliasing={{0}: (25, {}), {1}: (26, {}), {2}: (27, {})} | custom-call | flops 276824064 | bytes 38928384 | tf_op jit(solution)/shard_map/patch/pallas_call | solution.py:189
  242.4 3.3 %patch.3 = (f32[1920,1024]{1,0:T(8,128)}, f32[1920,1024]{1,0:T(8,128)}, f32[1920,1024]{1,0:T(8,128)}) custom-call(s32[2]{0:T(128)S(1)} %pad_add_fusion.info, bf16[1920,64]{1,0:T(8,128)(2,1)S(1)} %copy.25.hid_ref, bf16[64,1024]{1,0:T(8,128)(2,1)S(1)} %copy-done.14, ...), custom_call_target="tpu_custom_call", output_to_operand_aliasing={{0}: (5, {}), {1}: (6, {}), {2}: (7, {})} | custom-call | flops 25165824 | bytes 3538944 | tf_op jit(solution)/shard_map/patch/pallas_call | solution.py:189
  (111 shorter events, 18.9 us)
Async XLA Ops:
  14.0 16.7 %copy-start.15 = (bf16[16,8192]{1,0:T(8,128)(2,1)}, bf16[16,8192]{1,0:T(8,128)(2,1)S(1)}, u32[]{:S(2)}) copy-start(bf16[16,8192]{1,0:T(8,128)(2,1)S(1)} %reshape.30) | copy-start | bytes 786436
  22.3 11.2 %copy-start.17 = (f32[16,1920]{1,0:T(8,128)}, f32[16,1920]{1,0:T(8,128)S(1)}, u32[]{:S(2)}) copy-start(f32[16,1920]{1,0:T(8,128)S(1)} %fusion) | copy-start | bytes 368644
  32.1 51.4 %collective-permute-start.3 = (bf16[16,2944]{1,0:T(8,128)(2,1)}, bf16[16,2944]{1,0:T(8,128)(2,1)}, u32[]{:S(2)}, u32[]{:S(2)}) collective-permute-start(bf16[16,2944]{1,0:T(8,128)(2,1)} %get-tuple-element.74), channel_id=1, source_target_pairs={{0,8},{8,16},{16,24},{24,0},{1,9},{9,17},{17,25},{25,1},{2,10},{10... | collective-permute-start | bytes 282632 | tf_op jit(solution)/shard_map/ppermute | solution.py:288
  36.1 38.0 %collective-permute-start.18 = (bf16[3,96,1024]{2,1,0:T(8,128)(2,1)}, bf16[3,96,1024]{2,1,0:T(8,128)(2,1)S(1)}, u32[]{:S(2)}, u32[]{:S(2)}) collective-permute-start(bf16[3,96,1024]{2,1,0:T(8,128)(2,1)} %get-tuple-element.49), channel_id=1, source_target_pairs={{0,8},{8,24},{24,16},{16,0},{1,9},{9,25},{25,17},{17,1},{2,10},{10... | collective-permute-start | bytes 1769480 | tf_op jit(solution)/shard_map/ppermute | solution.py:259
  37.6 5.1 %copy-start.16 = (bf16[16,8192]{1,0:T(8,128)(2,1)S(1)}, bf16[16,8192]{1,0:T(8,128)(2,1)}, u32[]{:S(2)}) copy-start(bf16[16,8192]{1,0:T(8,128)(2,1)} %copy-done.15) | copy-start | bytes 786436
  37.6 38.1 %collective-permute-start.19 = (bf16[3,96,1024]{2,1,0:T(8,128)(2,1)S(1)}, bf16[3,96,1024]{2,1,0:T(8,128)(2,1)S(1)}, u32[]{:S(2)}, u32[]{:S(2)}) collective-permute-start(bf16[3,96,1024]{2,1,0:T(8,128)(2,1)S(1)} %get-tuple-element.50), channel_id=1, source_target_pairs={{8,0},{24,8},{16,24},{0,16},{9,1},{25,9},{17,25},{1,17},{10,2},{26... | collective-permute-start | bytes 1769480 | tf_op jit(solution)/shard_map/ppermute | solution.py:260
  40.6 11.7 %copy-start.18 = (f32[16,1920]{1,0:T(8,128)S(1)}, f32[16,1920]{1,0:T(8,128)}, u32[]{:S(2)}) copy-start(f32[16,1920]{1,0:T(8,128)} %copy-done.17) | copy-start | bytes 368644
  40.6 11.7 %copy-start.25 = (f32[16,1920]{1,0:T(8,128)S(1)}, f32[16,1920]{1,0:T(8,128)}, u32[]{:S(2)}) copy-start(f32[16,1920]{1,0:T(8,128)} %get-tuple-element.80) | copy-start | bytes 368644
  40.6 38.2 %collective-permute-start.6 = (bf16[3,96,1024]{2,1,0:T(8,128)(2,1)}, bf16[3,96,1024]{2,1,0:T(8,128)(2,1)S(1)}, u32[]{:S(2)}, u32[]{:S(2)}) collective-permute-start(bf16[3,96,1024]{2,1,0:T(8,128)(2,1)} %get-tuple-element.37), channel_id=1, source_target_pairs={{0,8},{8,24},{24,16},{16,0},{1,9},{9,25},{25,17},{17,1},{2,10},{10... | collective-permute-start | bytes 1769480 | tf_op jit(solution)/shard_map/ppermute | solution.py:259
  42.1 38.2 %collective-permute-start.7 = (bf16[3,96,1024]{2,1,0:T(8,128)(2,1)S(1)}, bf16[3,96,1024]{2,1,0:T(8,128)(2,1)S(1)}, u32[]{:S(2)}, u32[]{:S(2)}) collective-permute-start(bf16[3,96,1024]{2,1,0:T(8,128)(2,1)S(1)} %get-tuple-element.38), channel_id=1, source_target_pairs={{8,0},{24,8},{16,24},{0,16},{9,1},{25,9},{17,25},{1,17},{10,2},{26... | collective-permute-start | bytes 1769480 | tf_op jit(solution)/shard_map/ppermute | solution.py:260
  74.1 4.1 %copy-start = (bf16[3,96,1024]{2,1,0:T(8,128)(2,1)}, bf16[3,96,1024]{2,1,0:T(8,128)(2,1)S(1)}, u32[]{:S(2)}) copy-start(bf16[3,96,1024]{2,1,0:T(8,128)(2,1)S(1)} %collective-permute-done.18.refs_6_.refs_0_) | copy-start | bytes 1769476
  74.1 13.5 %collective-permute-start.4 = (bf16[16,2944]{1,0:T(8,128)(2,1)}, bf16[16,2944]{1,0:T(8,128)(2,1)}, u32[]{:S(2)}, u32[]{:S(2)}) collective-permute-start(bf16[16,2944]{1,0:T(8,128)(2,1)} %get-tuple-element.75), channel_id=1, source_target_pairs={{0,16},{8,24},{16,0},{24,8},{1,17},{9,25},{17,1},{25,9},{2,18},{10... | collective-permute-start | bytes 282632 | tf_op jit(solution)/shard_map/ppermute | solution.py:288
  78.3 30.1 %collective-permute-start.20 = (bf16[3,96,1024]{2,1,0:T(8,128)(2,1)}, bf16[3,96,1024]{2,1,0:T(8,128)(2,1)S(1)}, u32[]{:S(2)}, u32[]{:S(2)}) collective-permute-start(bf16[3,96,1024]{2,1,0:T(8,128)(2,1)} %get-tuple-element.51), channel_id=1, source_target_pairs={{0,8},{8,24},{24,16},{16,0},{1,9},{9,25},{25,17},{17,1},{2,10},{10... | collective-permute-start | bytes 1769480 | tf_op jit(solution)/shard_map/ppermute | solution.py:259
  78.8 6.2 %copy-start.19 = (f32[4,2,2,4096]{3,2,1,0:T(2,128)S(1)}, f32[4,2,2,4096]{3,2,1,0:T(2,128)}, u32[]{:S(2)}) copy-start(f32[4,2,2,4096]{3,2,1,0:T(2,128)} %reshape.26) | copy-start | bytes 786436
  78.8 6.8 %copy-start.29 = (s32[4]{0:T(128)S(1)}, s32[4]{0:T(128)}, u32[]{:S(2)}) copy-start(s32[4]{0:T(128)} %constant.99.clone) | copy-start | bytes 52
  78.8 29.5 %collective-permute-start.21 = (bf16[3,96,1024]{2,1,0:T(8,128)(2,1)}, bf16[3,96,1024]{2,1,0:T(8,128)(2,1)S(1)}, u32[]{:S(2)}, u32[]{:S(2)}) collective-permute-start(bf16[3,96,1024]{2,1,0:T(8,128)(2,1)} %get-tuple-element.52), channel_id=1, source_target_pairs={{8,0},{24,8},{16,24},{0,16},{9,1},{25,9},{17,25},{1,17},{10,2},{26... | collective-permute-start | bytes 1769480 | tf_op jit(solution)/shard_map/ppermute | solution.py:260
  82.9 29.5 %collective-permute-start.8 = (bf16[3,96,1024]{2,1,0:T(8,128)(2,1)}, bf16[3,96,1024]{2,1,0:T(8,128)(2,1)S(1)}, u32[]{:S(2)}, u32[]{:S(2)}) collective-permute-start(bf16[3,96,1024]{2,1,0:T(8,128)(2,1)} %get-tuple-element.39), channel_id=1, source_target_pairs={{0,8},{8,24},{24,16},{16,0},{1,9},{9,25},{25,17},{17,1},{2,10},{10... | collective-permute-start | bytes 1769480 | tf_op jit(solution)/shard_map/ppermute | solution.py:259
  83.5 29.0 %collective-permute-start.9 = (bf16[3,96,1024]{2,1,0:T(8,128)(2,1)}, bf16[3,96,1024]{2,1,0:T(8,128)(2,1)}, u32[]{:S(2)}, u32[]{:S(2)}) collective-permute-start(bf16[3,96,1024]{2,1,0:T(8,128)(2,1)} %get-tuple-element.40), channel_id=1, source_target_pairs={{8,0},{24,8},{16,24},{0,16},{9,1},{25,9},{17,25},{1,17},{10,2},{26... | collective-permute-start | bytes 1769480 | tf_op jit(solution)/shard_map/ppermute | solution.py:260
  87.6 19.7 %collective-permute-start.5 = (bf16[16,2944]{1,0:T(8,128)(2,1)}, bf16[16,2944]{1,0:T(8,128)(2,1)S(1)}, u32[]{:S(2)}, u32[]{:S(2)}) collective-permute-start(bf16[16,2944]{1,0:T(8,128)(2,1)} %get-tuple-element.76), channel_id=1, source_target_pairs={{0,24},{8,0},{16,8},{24,16},{1,25},{9,1},{17,9},{25,17},{2,26},{10... | collective-permute-start | bytes 282632 | tf_op jit(solution)/shard_map/ppermute | solution.py:288
  107.3 9.3 %collective-permute-start = (f32[4,1,2,4096]{3,2,1,0:T(2,128)}, f32[4,1,2,4096]{3,2,1,0:T(2,128)S(1)}, u32[]{:S(2)}, u32[]{:S(2)}) collective-permute-start(f32[4,1,2,4096]{3,2,1,0:T(2,128)} %constant_dynamic-slice_fusion.6), channel_id=1, source_target_pairs={{0,1},{1,0},{2,3},{3,2},{4,5},{5,4},{6,7},{7,6},{8,9},{9,8},{10,11... | collective-permute-start | bytes 393224 | tf_op jit(solution)/shard_map/ppermute | solution.py:224
  110.4 16.2 %collective-permute-start.22 = (bf16[3,96,1024]{2,1,0:T(8,128)(2,1)S(1)}, bf16[3,96,1024]{2,1,0:T(8,128)(2,1)S(1)}, u32[]{:S(2)}, u32[]{:S(2)}) collective-permute-start(bf16[3,96,1024]{2,1,0:T(8,128)(2,1)S(1)} %get-tuple-element.53), channel_id=1, source_target_pairs={{0,8},{8,24},{24,16},{16,0},{1,9},{9,25},{25,17},{17,1},{2,10},{10... | collective-permute-start | bytes 1769480 | tf_op jit(solution)/shard_map/ppermute | solution.py:259
  112.0 4.7 %copy-start.20 = (f32[4,2,2,4096]{3,2,1,0:T(2,128)S(1)}, f32[4,2,2,4096]{3,2,1,0:T(2,128)}, u32[]{:S(2)}) copy-start(f32[4,2,2,4096]{3,2,1,0:T(2,128)} %reshape.26) | copy-start | bytes 786436
  112.0 16.2 %collective-permute-start.23 = (bf16[3,96,1024]{2,1,0:T(8,128)(2,1)S(1)}, bf16[3,96,1024]{2,1,0:T(8,128)(2,1)S(1)}, u32[]{:S(2)}, u32[]{:S(2)}) collective-permute-start(bf16[3,96,1024]{2,1,0:T(8,128)(2,1)S(1)} %get-tuple-element.54), channel_id=1, source_target_pairs={{8,0},{24,8},{16,24},{0,16},{9,1},{25,9},{17,25},{1,17},{10,2},{26... | collective-permute-start | bytes 1769480 | tf_op jit(solution)/shard_map/ppermute | solution.py:260
  114.5 24.7 %collective-permute-start.10 = (bf16[3,96,1024]{2,1,0:T(8,128)(2,1)S(1)}, bf16[3,96,1024]{2,1,0:T(8,128)(2,1)S(1)}, u32[]{:S(2)}, u32[]{:S(2)}) collective-permute-start(bf16[3,96,1024]{2,1,0:T(8,128)(2,1)S(1)} %get-tuple-element.41), channel_id=1, source_target_pairs={{0,8},{8,24},{24,16},{16,0},{1,9},{9,25},{25,17},{17,1},{2,10},{10... | collective-permute-start | bytes 1769480 | tf_op jit(solution)/shard_map/ppermute | solution.py:259
  116.2 24.6 %collective-permute-start.11 = (bf16[3,96,1024]{2,1,0:T(8,128)(2,1)S(1)}, bf16[3,96,1024]{2,1,0:T(8,128)(2,1)S(1)}, u32[]{:S(2)}, u32[]{:S(2)}) collective-permute-start(bf16[3,96,1024]{2,1,0:T(8,128)(2,1)S(1)} %get-tuple-element.42), channel_id=1, source_target_pairs={{8,0},{24,8},{16,24},{0,16},{9,1},{25,9},{17,25},{1,17},{10,2},{26... | collective-permute-start | bytes 1769480 | tf_op jit(solution)/shard_map/ppermute | solution.py:260
  130.2 21.6 %collective-permute-start.24 = (bf16[3,96,1024]{2,1,0:T(8,128)(2,1)S(1)}, bf16[3,96,1024]{2,1,0:T(8,128)(2,1)S(1)}, u32[]{:S(2)}, u32[]{:S(2)}) collective-permute-start(bf16[3,96,1024]{2,1,0:T(8,128)(2,1)S(1)} %get-tuple-element.55), channel_id=1, source_target_pairs={{0,8},{8,24},{24,16},{16,0},{1,9},{9,25},{25,17},{17,1},{2,10},{10... | collective-permute-start | bytes 1769480 | tf_op jit(solution)/shard_map/ppermute | solution.py:259
  130.5 22.9 %collective-permute-start.25 = (bf16[3,96,1024]{2,1,0:T(8,128)(2,1)S(1)}, bf16[3,96,1024]{2,1,0:T(8,128)(2,1)S(1)}, u32[]{:S(2)}, u32[]{:S(2)}) collective-permute-start(bf16[3,96,1024]{2,1,0:T(8,128)(2,1)S(1)} %get-tuple-element.56), channel_id=1, source_target_pairs={{8,0},{24,8},{16,24},{0,16},{9,1},{25,9},{17,25},{1,17},{10,2},{26... | collective-permute-start | bytes 1769480 | tf_op jit(solution)/shard_map/ppermute | solution.py:260
  142.8 21.6 %collective-permute-start.12 = (bf16[3,96,1024]{2,1,0:T(8,128)(2,1)S(1)}, bf16[3,96,1024]{2,1,0:T(8,128)(2,1)S(1)}, u32[]{:S(2)}, u32[]{:S(2)}) collective-permute-start(bf16[3,96,1024]{2,1,0:T(8,128)(2,1)S(1)} %get-tuple-element.43), channel_id=1, source_target_pairs={{0,8},{8,24},{24,16},{16,0},{1,9},{9,25},{25,17},{17,1},{2,10},{10... | collective-permute-start | bytes 1769480 | tf_op jit(solution)/shard_map/ppermute | solution.py:259
  143.2 22.9 %collective-permute-start.13 = (bf16[3,96,1024]{2,1,0:T(8,128)(2,1)S(1)}, bf16[3,96,1024]{2,1,0:T(8,128)(2,1)S(1)}, u32[]{:S(2)}, u32[]{:S(2)}) collective-permute-start(bf16[3,96,1024]{2,1,0:T(8,128)(2,1)S(1)} %get-tuple-element.44), channel_id=1, source_target_pairs={{8,0},{24,8},{16,24},{0,16},{9,1},{25,9},{17,25},{1,17},{10,2},{26... | collective-permute-start | bytes 1769480 | tf_op jit(solution)/shard_map/ppermute | solution.py:260
  144.9 26.0 %collective-permute-start.1 = (f32[2,1,2,4096]{3,2,1,0:T(2,128)S(1)}, f32[2,1,2,4096]{3,2,1,0:T(2,128)S(1)}, u32[]{:S(2)}, u32[]{:S(2)}) collective-permute-start(f32[2,1,2,4096]{3,2,1,0:T(2,128)S(1)} %constant_dynamic-slice_fusion.5), channel_id=1, source_target_pairs={{0,4},{2,6},{4,0},{6,2},{1,5},{3,7},{5,1},{7,3},{8,12},{10,14},{12... | collective-permute-start | bytes 196616 | tf_op jit(solution)/shard_map/ppermute | solution.py:224
  151.9 4.4 %copy-start.9 = (bf16[3,96,1024]{2,1,0:T(8,128)(2,1)}, bf16[3,96,1024]{2,1,0:T(8,128)(2,1)S(1)}, u32[]{:S(2)}) copy-start(bf16[3,96,1024]{2,1,0:T(8,128)(2,1)S(1)} %collective-permute-done.24.refs_6_.refs_12_) | copy-start | bytes 1769476
  156.2 42.6 %collective-permute-start.26 = (bf16[3,96,1024]{2,1,0:T(8,128)(2,1)}, bf16[3,96,1024]{2,1,0:T(8,128)(2,1)}, u32[]{:S(2)}, u32[]{:S(2)}) collective-permute-start(bf16[3,96,1024]{2,1,0:T(8,128)(2,1)} %get-tuple-element.57), channel_id=1, source_target_pairs={{0,8},{8,24},{24,16},{16,0},{1,9},{9,25},{25,17},{17,1},{2,10},{10... | collective-permute-start | bytes 1769480 | tf_op jit(solution)/shard_map/ppermute | solution.py:259
  156.5 18.4 %copy-start.22 = (bf16[16,1920]{1,0:T(8,128)(2,1)S(1)}, bf16[16,1920]{1,0:T(8,128)(2,1)}, u32[]{:S(2)}) copy-start(bf16[16,1920]{1,0:T(8,128)(2,1)} %copy-done.21) | copy-start | bytes 184324
  156.5 18.4 %copy-start.27 = (bf16[16,2944]{1,0:T(8,128)(2,1)S(1)}, bf16[16,2944]{1,0:T(8,128)(2,1)}, u32[]{:S(2)}) copy-start(bf16[16,2944]{1,0:T(8,128)(2,1)} %copy-done.26) | copy-start | bytes 282628
  156.6 18.4 %copy-start.28 = (bf16[16,1024]{1,0:T(8,128)(2,1)S(1)}, bf16[16,1024]{1,0:T(8,128)(2,1)}, u32[]{:S(2)}) copy-start(bf16[16,1024]{1,0:T(8,128)(2,1)} %get-tuple-element.70) | copy-start | bytes 98308
  156.6 42.3 %collective-permute-start.27 = (bf16[3,96,1024]{2,1,0:T(8,128)(2,1)}, bf16[3,96,1024]{2,1,0:T(8,128)(2,1)}, u32[]{:S(2)}, u32[]{:S(2)}) collective-permute-start(bf16[3,96,1024]{2,1,0:T(8,128)(2,1)} %get-tuple-element.58), channel_id=1, source_target_pairs={{8,0},{24,8},{16,24},{0,16},{9,1},{25,9},{17,25},{1,17},{10,2},{26... | collective-permute-start | bytes 1769480 | tf_op jit(solution)/shard_map/ppermute | solution.py:260
  164.5 4.4 %copy-start.11 = (bf16[3,96,1024]{2,1,0:T(8,128)(2,1)}, bf16[3,96,1024]{2,1,0:T(8,128)(2,1)S(1)}, u32[]{:S(2)}) copy-start(bf16[3,96,1024]{2,1,0:T(8,128)(2,1)S(1)} %collective-permute-done.12.refs_6_.refs_14_) | copy-start | bytes 1769476
  168.9 34.4 %collective-permute-start.14 = (bf16[3,96,1024]{2,1,0:T(8,128)(2,1)}, bf16[3,96,1024]{2,1,0:T(8,128)(2,1)}, u32[]{:S(2)}, u32[]{:S(2)}) collective-permute-start(bf16[3,96,1024]{2,1,0:T(8,128)(2,1)} %get-tuple-element.45), channel_id=1, source_target_pairs={{0,8},{8,24},{24,16},{16,0},{1,9},{9,25},{25,17},{17,1},{2,10},{10... | collective-permute-start | bytes 1769480 | tf_op jit(solution)/shard_map/ppermute | solution.py:259
  169.2 34.1 %collective-permute-start.15 = (bf16[3,96,1024]{2,1,0:T(8,128)(2,1)}, bf16[3,96,1024]{2,1,0:T(8,128)(2,1)}, u32[]{:S(2)}, u32[]{:S(2)}) collective-permute-start(bf16[3,96,1024]{2,1,0:T(8,128)(2,1)} %get-tuple-element.46), channel_id=1, source_target_pairs={{8,0},{24,8},{16,24},{0,16},{9,1},{25,9},{17,25},{1,17},{10,2},{26... | collective-permute-start | bytes 1769480 | tf_op jit(solution)/shard_map/ppermute | solution.py:260
  171.6 36.0 %collective-permute-start.2 = (f32[1,1,2,4096]{3,2,1,0:T(2,128)}, f32[1,1,2,4096]{3,2,1,0:T(2,128)}, u32[]{:S(2)}, u32[]{:S(2)}) collective-permute-start(f32[1,1,2,4096]{3,2,1,0:T(2,128)} %constant_dynamic-slice_fusion.4), channel_id=1, source_target_pairs={{0,2},{2,0},{4,6},{6,4},{1,3},{3,1},{5,7},{7,5},{8,10},{10,8},{12,... | collective-permute-start | bytes 98312 | tf_op jit(solution)/shard_map/ppermute | solution.py:224
  201.2 16.3 %collective-permute-start.28 = (bf16[3,96,1024]{2,1,0:T(8,128)(2,1)S(1)}, bf16[3,96,1024]{2,1,0:T(8,128)(2,1)S(1)}, u32[]{:S(2)}, u32[]{:S(2)}) collective-permute-start(bf16[3,96,1024]{2,1,0:T(8,128)(2,1)S(1)} %get-tuple-element.59), channel_id=1, source_target_pairs={{0,8},{8,24},{24,16},{16,0},{1,9},{9,25},{25,17},{17,1},{2,10},{10... | collective-permute-start | bytes 1769480 | tf_op jit(solution)/shard_map/ppermute | solution.py:259
  201.5 17.2 %copy-start.1 = (bf16[3,96,1024]{2,1,0:T(8,128)(2,1)S(1)}, bf16[3,96,1024]{2,1,0:T(8,128)(2,1)}, u32[]{:S(2)}) copy-start(bf16[3,96,1024]{2,1,0:T(8,128)(2,1)} %copy-done) | copy-start | bytes 1769476
  201.5 17.2 %copy-start.3 = (bf16[3,96,1024]{2,1,0:T(8,128)(2,1)S(1)}, bf16[3,96,1024]{2,1,0:T(8,128)(2,1)}, u32[]{:S(2)}) copy-start(bf16[3,96,1024]{2,1,0:T(8,128)(2,1)} %copy-done.2) | copy-start | bytes 1769476
  201.5 17.2 %copy-start.5 = (bf16[3,96,1024]{2,1,0:T(8,128)(2,1)S(1)}, bf16[3,96,1024]{2,1,0:T(8,128)(2,1)}, u32[]{:S(2)}) copy-start(bf16[3,96,1024]{2,1,0:T(8,128)(2,1)} %copy-done.4) | copy-start | bytes 1769476
  201.5 17.2 %copy-start.14 = (bf16[64,1024]{1,0:T(8,128)(2,1)S(1)}, bf16[64,1024]{1,0:T(8,128)(2,1)}, u32[]{:S(2)}) copy-start(bf16[64,1024]{1,0:T(8,128)(2,1)} %pad_maximum_fusion.1.out_ref) | copy-start | bytes 393220
  201.5 16.3 %collective-permute-start.29 = (bf16[3,96,1024]{2,1,0:T(8,128)(2,1)S(1)}, bf16[3,96,1024]{2,1,0:T(8,128)(2,1)S(1)}, u32[]{:S(2)}, u32[]{:S(2)}) collective-permute-start(bf16[3,96,1024]{2,1,0:T(8,128)(2,1)S(1)} %get-tuple-element.60), channel_id=1, source_target_pairs={{8,0},{24,8},{16,24},{0,16},{9,1},{25,9},{17,25},{1,17},{10,2},{26... | collective-permute-start | bytes 1769480 | tf_op jit(solution)/shard_map/ppermute | solution.py:260
  205.5 36.9 %collective-permute-start.16 = (bf16[3,96,1024]{2,1,0:T(8,128)(2,1)S(1)}, bf16[3,96,1024]{2,1,0:T(8,128)(2,1)S(1)}, u32[]{:S(2)}, u32[]{:S(2)}) collective-permute-start(bf16[3,96,1024]{2,1,0:T(8,128)(2,1)S(1)} %get-tuple-element.47), channel_id=1, source_target_pairs={{0,8},{8,24},{24,16},{16,0},{1,9},{9,25},{25,17},{17,1},{2,10},{10... | collective-permute-start | bytes 1769480 | tf_op jit(solution)/shard_map/ppermute | solution.py:259
  205.9 36.5 %collective-permute-start.17 = (bf16[3,96,1024]{2,1,0:T(8,128)(2,1)S(1)}, bf16[3,96,1024]{2,1,0:T(8,128)(2,1)S(1)}, u32[]{:S(2)}, u32[]{:S(2)}) collective-permute-start(bf16[3,96,1024]{2,1,0:T(8,128)(2,1)S(1)} %get-tuple-element.48), channel_id=1, source_target_pairs={{8,0},{24,8},{16,24},{0,16},{9,1},{25,9},{17,25},{1,17},{10,2},{26... | collective-permute-start | bytes 1769480 | tf_op jit(solution)/shard_map/ppermute | solution.py:260
  (12 other events, 27.5 us)

commit v2 on v1

v2 whole, which is shorter than its diff:
```python
import functools

import jax
import jax.numpy as jnp
from jax import lax
from jax.experimental import pallas as pl
from jax.experimental.pallas import tpu as pltpu
from jax.sharding import PartitionSpec as P

BF16, F32 = jnp.bfloat16, jnp.float32
LAG = 2
MOST_CHUNKS = 20
TILE = 16
VMEM = 48 << 20

ANY = pl.BlockSpec(memory_space=pl.ANY)
SMEM = pl.BlockSpec(memory_space=pltpu.SMEM)
WHOLE = pl.BlockSpec(memory_space=pltpu.VMEM)
PARAMS = pltpu.CompilerParams(vmem_limit_bytes=VMEM)


def ring_order(n):
    return [0, 1, 3, 2] if n == 4 else list(range(n))


def largest(options, default):
    options = list(options)
    return max(options) if options else default


def cost(flops, bytes_accessed, transcendentals=0):
    return pl.CostEstimate(
        flops=flops, bytes_accessed=bytes_accessed, transcendentals=transcendentals
    )


def updated(master_old, first_old, second_old, total, healthy):
    first_new = 0.9 * first_old + (0.1 / healthy) * total
    second_new = 0.95 * second_old + (0.05 / healthy**2) * (total * total)
    root = second_new * lax.rsqrt(second_new)
    step = first_new * pl.reciprocal(root + 1e-08)
    return master_old - 0.01 * step, first_new, second_new


def pack_body(flag, *refs, places, chunk, count_seen, count_after):
    state = refs[0:3]
    seen = refs[3 : 3 + count_seen]
    rest = refs[3 + count_seen + count_after :]
    sends = rest[:2]
    held, made, in_sem, out_sem = rest[2:]

    def fetch(j):
        way, k = divmod(j, 3)
        rows = pl.ds(places[way] * chunk, chunk)
        return pltpu.make_async_copy(state[k].at[1, rows], held.at[j], in_sem.at[j])

    def store(j):
        way, k = divmod(j, 3)
        return pltpu.make_async_copy(made.at[j], sends[way].at[k], out_sem.at[j])

    def convert():
        for j in range(6):
            fetch(j).start()
        for j in range(6):
            fetch(j).wait()
            made[j] = held[j].astype(BF16)
            store(j).start()
        for j in range(6):
            store(j).wait()

    def relay(way):
        return pltpu.make_async_copy(seen[way], sends[way], out_sem.at[way])

    if not seen:
        convert()
        return
    pl.when(flag[0] == 1)(convert)

    @pl.when(flag[0] == 0)
    def _():
        for way in range(2):
            relay(way).start()
        for way in range(2):
            relay(way).wait()


def pack(is_source, state, seen, after, places, chunk):
    width = state[0].shape[2]
    shape = jax.ShapeDtypeStruct((3, chunk, width), BF16)
    return pl.pallas_call(
        functools.partial(
            pack_body,
            places=places,
            chunk=chunk,
            count_seen=len(seen),
            count_after=len(after),
        ),
        in_specs=[SMEM] + [ANY] * (3 + len(seen) + len(after)),
        out_specs=[ANY, ANY],
        out_shape=[shape, shape],
        scratch_shapes=[
            pltpu.VMEM((6, chunk, width), F32),
            pltpu.VMEM((6, chunk, width), BF16),
            pltpu.SemaphoreType.DMA((6,)),
            pltpu.SemaphoreType.DMA((6,)),
        ],
        compiler_params=PARAMS,
        cost_estimate=cost(0, 2 * 3 * chunk * width * 6),
        name="pack",
    )(is_source, *state, *seen, *after)


def beside_body(*refs):
    tokens, d_out, out = refs[0], refs[1], refs[-1]
    width = tokens.shape[1]
    out[:, :width] = tokens[...]
    out[:, width:] = d_out[...]


def beside(tokens, d_out, after):
    rows, width = tokens.shape
    return pl.pallas_call(
        beside_body,
        in_specs=[WHOLE, WHOLE] + [ANY] * len(after),
        out_specs=WHOLE,
        out_shape=jax.ShapeDtypeStruct((rows, 2 * width), tokens.dtype),
        compiler_params=PARAMS,
        cost_estimate=cost(0, 4 * rows * width * 2),
        name="beside",
    )(tokens, d_out, *after)


def by_rows(a, b):
    return lax.dot_general(a, b, (((1,), (1,)), ((), ())), preferred_element_type=F32)


def layer_body(both, gate_ref, up_ref, down_ref, *refs, resumed):
    hidden_ref, sum_ref = refs[-2:]
    features = gate_ref.shape[0]
    tile = gate_ref.shape[1]
    x, dy = both[:, :features], both[:, features:]
    w_gate, w_up = gate_ref[...], up_ref[...]
    joined = tile % 128 == 0
    if joined:
        w_both = jnp.concatenate([w_gate, w_up], axis=1)
        gate_up = jnp.dot(x, w_both, preferred_element_type=F32)
        gate, up = gate_up[:, :tile], gate_up[:, tile:]
    else:
        gate = jnp.dot(x, w_gate, preferred_element_type=F32)
        up = jnp.dot(x, w_up, preferred_element_type=F32)
    d_hidden = by_rows(dy, down_ref[...])
    sig = 1.0 / (1.0 + jnp.exp(-gate))
    hidden_ref[...] = (gate * sig * up).astype(BF16)
    d_gate = (d_hidden * up * sig * (1.0 + gate * (1.0 - sig))).astype(BF16)
    d_up = (d_hidden * gate * sig).astype(BF16)
    if joined:
        term = by_rows(jnp.concatenate([d_gate, d_up], axis=1), w_both)
    else:
        term = by_rows(d_gate, w_gate) + by_rows(d_up, w_up)

    @pl.when(pl.program_id(0) == 0)
    def _():
        sum_ref[...] = (refs[0][...] + term) if resumed else term

    @pl.when(pl.program_id(0) > 0)
    def _():
        sum_ref[...] += term


def layer(both, w_gate, w_up, w_down, partial_sum, after, tile, first, count):
    rows = both.shape[0]
    features = w_gate.shape[0]
    across = pl.BlockSpec((features, tile), lambda i: (0, first + i))
    resumed = partial_sum is not None
    fixed = pl.BlockSpec((rows, features), lambda i: (0, 0))
    return pl.pallas_call(
        functools.partial(layer_body, resumed=resumed),
        grid=(count,),
        in_specs=[
            pl.BlockSpec(both.shape, lambda i: (0, 0)),
            across,
            across,
            pl.BlockSpec((tile, features), lambda i: (first + i, 0)),
        ]
        + [fixed] * resumed
        + [ANY] * len(after),
        out_specs=[pl.BlockSpec((rows, tile), lambda i: (0, i)), fixed],
        out_shape=[
            jax.ShapeDtypeStruct((rows, count * tile), BF16),
            jax.ShapeDtypeStruct((rows, features), F32),
        ],
        compiler_params=PARAMS,
        cost_estimate=cost(
            10 * rows * features * count * tile,
            3 * features * count * tile * 2,
            rows * count * tile,
        ),
        name="layer",
    )(both, w_gate, w_up, w_down, *([partial_sum] if resumed else []), *after)


def halve_body(bit, *refs, arrived, final):
    value = refs[0][...]
    if arrived:
        value = value + refs[1][...]
    if final:
        refs[-1][...] = value.astype(BF16)
        return
    kept, sent = refs[-2:]
    half = value.shape[0] // 2
    low, high = value[:half], value[half:]
    upper = bit[0] == 1
    kept[...] = jnp.where(upper, high, low)
    sent[...] = jnp.where(upper, low, high)


def halve(bit, value, arrived, after, final):
    rows, features = value.shape
    if final:
        out_shape = jax.ShapeDtypeStruct((rows, features), BF16)
    else:
        out_shape = [jax.ShapeDtypeStruct((rows // 2, features), F32)] * 2
    return pl.pallas_call(
        functools.partial(halve_body, arrived=bool(arrived), final=final),
        in_specs=[SMEM] + [WHOLE] * (1 + len(arrived)) + [ANY] * len(after),
        out_specs=WHOLE if final else [WHOLE, WHOLE],
        out_shape=out_shape,
        compiler_params=PARAMS,
        cost_estimate=cost(0, 3 * rows * features * 4),
        name="halve",
    )(bit, value, *arrived, *after)


def sum_scattered(value, axes, afters):
    sizes = [lax.axis_size(axis) for axis in axes]
    if any(size & (size - 1) for size in sizes):
        return lax.psum_scatter(value, axes, scatter_dimension=0, tiled=True).astype(BF16)
    arrived = ()
    level = 0
    for axis, size in zip(axes, sizes):
        me = lax.axis_index(axis)
        apart = size // 2
        while apart:
            bit = ((me // apart) % 2).astype(jnp.int32)[None]
            after = afters[min(level, len(afters) - 1)]
            value, sent = halve(bit, value, arrived, after, False)
            route = [(i, i ^ apart) for i in range(size)]
            arrived = (lax.ppermute(sent, axis, route),)
            apart //= 2
            level += 1
    after = afters[min(level, len(afters) - 1)]
    return halve(jnp.zeros((1,), jnp.int32), value, arrived, after, True)


def collect_body(*refs, count, units):
    hidden_t, outs = refs[-2:]
    rows = refs[0].shape[0]
    for j in range(count):
        outs[pl.ds(j * rows, rows)] = refs[j][:, units:]
    hidden = jnp.concatenate([refs[j][:, :units] for j in range(count)], axis=0)
    hidden_t[...] = hidden.astype(F32).T.astype(BF16)


def collect(parcels, units, after):
    rows, length = parcels[0].shape
    depth = rows * len(parcels)
    return pl.pallas_call(
        functools.partial(collect_body, count=len(parcels), units=units),
        in_specs=[WHOLE] * len(parcels) + [ANY] * len(after),
        out_specs=[WHOLE, WHOLE],
        out_shape=[
            jax.ShapeDtypeStruct((units, depth), BF16),
            jax.ShapeDtypeStruct((depth, length - units), BF16),
        ],
        compiler_params=PARAMS,
        cost_estimate=cost(0, 4 * depth * length),
        name="collect",
    )(*parcels, *after)


def update_body(info, hid_ref, out_ref, m_ref, a_ref, b_ref, *refs, healthy):
    m_new, a_new, b_new = refs[-3:]

    @pl.when(info[0] == 0)
    def _():
        total = jnp.dot(hid_ref[...], out_ref[...], preferred_element_type=F32)
        m_new[...], a_new[...], b_new[...] = updated(
            m_ref[0], a_ref[0], b_ref[0], total, healthy
        )


def update(info, hidden_t, outs, state, news, after, healthy, block, first, count):
    _, rows, width = state[0].shape
    depth = hidden_t.shape[1]

    def at(i, info):
        return jnp.where(info[0] == 1, first, first + i)

    spec = pl.BlockSpec((1, block, width), lambda i, info: (0, at(i, info), 0))
    out = pl.BlockSpec((block, width), lambda i, info: (at(i, info), 0))
    shape = jax.ShapeDtypeStruct((rows, width), F32)
    return pl.pallas_call(
        functools.partial(update_body, healthy=healthy),
        grid_spec=pltpu.PrefetchScalarGridSpec(
            num_scalar_prefetch=1,
            grid=(count,),
            in_specs=[
                pl.BlockSpec((block, depth), lambda i, info: (at(i, info), 0)),
                pl.BlockSpec((depth, width), lambda i, info: (0, 0)),
                spec,
                spec,
                spec,
            ]
            + [ANY] * (len(news) + len(after)),
            out_specs=[out] * 3,
        ),
        out_shape=[shape] * 3,
        input_output_aliases={6 + k: k for k in range(len(news))},
        compiler_params=PARAMS,
        cost_estimate=cost(
            2 * count * block * width * depth,
            6 * count * block * width * 4,
            2 * count * block * width,
        ),
        name="update",
    )(info, hidden_t, outs, *state, *news, *after)


def patch_body(info, hid_ref, out_ref, *refs, arrivals, chunks, n, count_after):
    count = len(arrivals)
    got = refs[:count]
    rest = refs[count + 3 + count_after :]
    news = rest[:3]
    held, made, in_sem, out_sem = rest[3:]
    chunk = held.shape[2]
    part = largest((p for p in (16, 32, 48) if chunk % p == 0), chunk)
    ahead = info[1]
    lag_of = {True: LAG * (ahead - 1), False: LAG * (n - ahead - 1)}

    def fetch(j):
        return pltpu.make_async_copy(got[j], held.at[j % 2], in_sem.at[j % 2])

    def first_row(j):
        step, forward = arrivals[j]
        place = step - lag_of[forward]
        if not forward:
            place = chunks - 1 - place
        return pl.multiple_of(jnp.clip(place, 0, chunks - 1) * chunk, TILE)

    def store(j, k):
        return pltpu.make_async_copy(
            made.at[j % 2, k], news[k].at[pl.ds(first_row(j), chunk)], out_sem.at[j % 2, k]
        )

    def valid(j):
        step, forward = arrivals[j]
        return step >= lag_of[forward]

    def finish(j):
        @pl.when(valid(j))
        def _():
            for k in range(3):
                store(j, k).wait()

    @pl.when(info[0] == 1)
    def _():
        fetch(0).start()
        for j in range(count):
            slot = j % 2
            if j + 1 < count:
                fetch(j + 1).start()
            fetch(j).wait()
            if j >= 2:
                finish(j - 2)

            @pl.when(valid(j))
            def _(j=j, slot=slot):
                first = first_row(j)

                @pl.loop(0, chunk // part)
                def _(i):
                    base = pl.multiple_of(i * part, part)
                    here = pl.ds(base, part)
                    units = hid_ref[pl.ds(pl.multiple_of(first + base, TILE), part)]
                    total = jnp.dot(units, out_ref[...], preferred_element_type=F32)
                    old = [held[slot, k, here].astype(F32) for k in range(3)]
                    new = updated(*old, total, n - 1.0)
                    for k in range(3):
                        made[slot, k, here] = new[k]

                for k in range(3):
                    store(j, k).start()

        for j in range(max(count - 2, 0), count):
            finish(j)


def patch(info, hidden_t, outs, got, arrivals, news, after, chunks, n):
    rows, width = news[0].shape
    chunk = rows // chunks
    count = len(got)
    shape = jax.ShapeDtypeStruct((rows, width), F32)
    return pl.pallas_call(
        functools.partial(
            patch_body, arrivals=arrivals, chunks=chunks, n=n, count_after=len(after)
        ),
        in_specs=[SMEM, WHOLE, WHOLE] + [ANY] * (count + 3 + len(after)),
        out_specs=[ANY] * 3,
        out_shape=[shape] * 3,
        scratch_shapes=[
            pltpu.VMEM((2, 3, chunk, width), BF16),
            pltpu.VMEM((2, 3, chunk, width), F32),
            pltpu.SemaphoreType.DMA((2,)),
            pltpu.SemaphoreType.DMA((2, 3)),
        ],
        input_output_aliases={3 + count + k: k for k in range(3)},
        compiler_params=PARAMS,
        cost_estimate=cost(
            2 * count * chunk * width * hidden_t.shape[1],
            count * 3 * chunk * width * 6,
            2 * count * chunk * width,
        ),
        name="patch",
    )(info, hidden_t, outs, *got, *news, *after)


def per_device(tokens, d_out, w_gate, w_up, w_down, failed, master, moment1, moment2):
    n = lax.axis_size("replica")
    me = lax.axis_index("replica")
    _, rows, width = master.shape
    features, units = w_gate.shape

    failed_id = failed[0]
    source = (failed_id + 1) % n
    order = ring_order(n)
    place = jnp.array([order.index(i) for i in range(n)], jnp.int32)
    ahead = (place[failed_id] - place[source]) % n
    is_source = (me == source).astype(jnp.int32)[None]
    info = jnp.stack([(me == failed_id).astype(jnp.int32), ahead.astype(jnp.int32)])

    state = (master, moment1, moment2)
    chunks = largest(
        (c for c in range(2, MOST_CHUNKS + 1, 2) if rows % (TILE * c) == 0), 2
    )
    steps = (chunks + LAG * (n - 2)) // 2
    forward = [(order[p], order[(p + 1) % n]) for p in range(n)]
    backward = [(b, a) for a, b in forward]
    sends, got = [], []

    def send(*after):
        step = len(got)
        seen = got[step - LAG] if step >= LAG else ()
        here = min(step, chunks - 1)
        places = (here, chunks - 1 - here)
        sends.append(pack(is_source, state, seen, after, places, rows // chunks))
        got.append(
            (
                lax.ppermute(sends[-1][0], "replica", forward),
                lax.ppermute(sends[-1][1], "replica", backward),
            )
        )
        return (sends[-1][0],)

    sent = send()
    sent = send(*sent)
    both = beside(tokens[0], d_out[0], sent)
    both = lax.all_gather(both, ("fsdp", "tensor"), axis=0, tiled=True)
    sent = send(both)

    tile = 128 if units % 128 == 0 else units
    tiles = units // tile
    pieces = largest((p for p in (1, 3) if tiles % p == 0), 1)
    hidden, d_rows = [], None
    for piece in range(pieces):
        count = tiles // pieces
        part, d_rows = layer(
            both, w_gate, w_up, w_down, d_rows, sent, tile, piece * count, count
        )
        hidden.append(part)
        sent = send(d_rows)
    hidden = jnp.concatenate(hidden, axis=1)

    kept = jnp.where(me == failed_id, jnp.zeros_like(hidden), hidden)

    def parcel(to):
        slab = lax.dynamic_slice_in_dim(both, features + to * width, width, 1)
        return jnp.concatenate([kept, slab], axis=1)

    parcels = [parcel(me)]
    for far in range(1, n):
        route = [(i, (i + far) % n) for i in range(n)]
        parcels.append(lax.ppermute(parcel((me + far) % n), "replica", route))

    afters = [sent]
    for _ in range(3):
        afters.append(send(*afters[-1]))
    d_tokens = sum_scattered(d_rows, ("fsdp", "tensor"), afters)

    hidden_t, outs = collect(parcels, units, afters[-1])
    block = largest((b for b in range(TILE, 193, TILE) if rows % b == 0), rows)
    blocks = rows // block
    sent = (hidden_t,)
    news = ()
    turns = 2 if blocks % 2 == 0 else 1
    for turn in range(turns):
        count = blocks // turns
        news = update(
            info, hidden_t, outs, state, news, sent, n - 1.0, block, turn * count, count
        )
        sent = send(news[0])

    patched = 0

    def patch_to(step, news, after):
        nonlocal patched
        arrivals = [(s, way) for s in range(patched, step) for way in (True, False)]
        blocks = [b for s in range(patched, step) for b in got[s]]
        patched = step
        return patch(info, hidden_t, outs, blocks, arrivals, news, after, chunks, n)

    news = patch_to(len(got) - 2, news, sent)
    while len(got) < steps:
        sent = send(news[0])
    news = patch_to(steps - 1, news, sent)
    news = patch_to(steps, news, ())
    return (d_tokens[None], *news)


def solution(mesh):
    placed = (
        P("replica", ("fsdp", "tensor"), None),
        P("replica", ("fsdp", "tensor"), None),
        P(None, ("fsdp", "tensor")),
        P(None, ("fsdp", "tensor")),
        P(("fsdp", "tensor"), None),
        P(("fsdp", "tensor")),
        P(None, ("fsdp", "tensor"), "replica"),
        P(None, ("fsdp", "tensor"), "replica"),
        P(None, ("fsdp", "tensor"), "replica"),
    )
    return jax.shard_map(
        per_device,
        mesh=mesh,
        in_specs=placed,
        out_specs=(
            P("replica", ("fsdp", "tensor"), None),
            P(("fsdp", "tensor"), "replica"),
            P(("fsdp", "tensor"), "replica"),
            P(("fsdp", "tensor"), "replica"),
        ),
        check_vma=False,
    )
```

time: 248 us -> 207 us (0.83)
  the two profiles are of different devices: /device:TPU:16 before, /device:TPU:0 now
where the time goes in v2:
time: 207 us
  Pallas kernels  95.8 us (46%)
  starting transfers between devices  57.2 us (28%)
  waiting for transfers between devices  28.7 us (14%)
  blocking collectives  14.9 us (7%)
  local copies, waits for them, and re-layouts  6.47 us (3%)
  between operations  3.26 us (2%)
    pallas_call x12, Pallas kernels, pack(): pl.pallas_call(functools.partial(pack_body, places=places, chunk=chunk, c...  33.5 us
    ppermute x12, starting transfers between devices, send(): lax.ppermute(sends[-1][1], 'replica', backward)  30.3 us
    pallas_call x3, Pallas kernels, layer(): pl.pallas_call(functools.partial(layer_body, resumed=resumed), grid=(coun...  28.9 us
    pallas_call x3, Pallas kernels, patch(): pl.pallas_call(functools.partial(patch_body, arrivals=arrivals, chunks=ch...  25.4 us
    ppermute x12, starting transfers between devices, send(): lax.ppermute(sends[-1][0], 'replica', forward)  22.6 us
    all_gather x1, blocking collectives, per_device(): both = lax.all_gather(both, ('fsdp', 'tensor'), axis=0, tiled=True)  14.9 us
    ppermute x3, waiting for transfers between devices, sum_scattered(): arrived = (lax.ppermute(sent, axis, route),)  12.5 us
    ppermute x12, waiting for transfers between devices, send(): lax.ppermute(sends[-1][1], 'replica', backward)  9.28 us
  transfers between devices with their start and end apart: 30, of which 7 were waited for; matrix products, arithmetic and copies ran while one was open for 1% of the time, Pallas kernels for 43%

profile of v2, /device:TPU:0, one launch (start us, length us, event | category | flops | bytes accessed | tf_op | source)
XLA Modules:
  0.0 207.1 jit_solution(9971328849412280554)
XLA Ops:
  1.3 2.4 %pack.12 = (bf16[3,96,1024]{2,1,0:T(8,128)(2,1)}, bf16[3,96,1024]{2,1,0:T(8,128)(2,1)}) custom-call(s32[1]{0:T(128)} %bitcast.6.flag, f32[2,1920,1024]{2,1,0:T(8,128)} %refs_0_.23, f32[2,1920,1024]{2,1,0:T(8,128)} %refs_1_.23, f32[2,1920,1024]{2,1,0:T(8,128)} %refs_2_.23), custom_call_target="tpu_custom_call" | custom-call | bytes 3538944 | tf_op jit(solution)/shard_map/pack/pallas_call | solution.py:90
  3.7 3.0 %collective-permute-start.1 = (bf16[3,96,1024]{2,1,0:T(8,128)(2,1)}, bf16[3,96,1024]{2,1,0:T(8,128)(2,1)S(1)}, u32[]{:S(2)}, u32[]{:S(2)}) collective-permute-start(bf16[3,96,1024]{2,1,0:T(8,128)(2,1)} %get-tuple-element.59), channel_id=1, source_target_pairs={{8,0},{24,8},{16,24},{0,16},{9,1},{25,9},{17,25},{1,17},{10,2},{26... | collective-permute-start | bytes 1769480 | tf_op jit(solution)/shard_map/ppermute | solution.py:459
  6.8 2.7 %pack.13 = (bf16[3,96,1024]{2,1,0:T(8,128)(2,1)S(1)}, bf16[3,96,1024]{2,1,0:T(8,128)(2,1)}) custom-call(s32[1]{0:T(128)} %bitcast.6.flag, f32[2,1920,1024]{2,1,0:T(8,128)} %refs_0_.23, f32[2,1920,1024]{2,1,0:T(8,128)} %refs_1_.23, f32[2,1920,1024]{2,1,0:T(8,128)} %refs_2_.23, bf16[3,96,1024]{2,1,0:T(8,128)(2,1)} %get-tuple-element.57.refs_3_), custom_call_target="tpu_custom_call" | custom-call | bytes 3538944 | tf_op jit(solution)/shard_map/pack/pallas_call | solution.py:90
  9.5 2.0 collective-permute-start.3
  11.6 14.9 %all-gather = bf16[8,2,8192]{2,1,0:T(2,128)(2,1)S(1)} all-gather(bf16[1,2,8192]{2,1,0:T(2,128)(2,1)S(1)} %bitcast.17), channel_id=1, replica_groups=mesh['replica'=4,'fsdp'=4,'tensor'=2] {'fsdp','tensor'}, dimensions={0}, use_global_device_ids=true | all-gather | bytes 294912 | tf_op jit(solution)/shard_map/all_gather | solution.py:467
  27.6 1.5 collective-permute-start.5
  29.2 2.2 %collective-permute-start.4 = (bf16[3,96,1024]{2,1,0:T(8,128)(2,1)S(1)}, bf16[3,96,1024]{2,1,0:T(8,128)(2,1)S(1)}, u32[]{:S(2)}, u32[]{:S(2)}) collective-permute-start(bf16[3,96,1024]{2,1,0:T(8,128)(2,1)S(1)} %get-tuple-element.60.refs_0_), channel_id=1, source_target_pairs={{0,8},{8,24},{24,16},{16,0},{1,9},{9,25},{25,17},{17,1},{2,10},{10... | collective-permute-start | bytes 1769480 | tf_op jit(solution)/shard_map/ppermute | solution.py:458
  31.3 9.6 %layer.3 = (bf16[16,640]{1,0:T(8,128)(2,1)S(1)}, f32[16,4096]{1,0:T(8,128)S(1)}) custom-call(bf16[16,8192]{1,0:T(8,128)(2,1)S(1)} %reshape.12.refs_5_.both, bf16[4096,1920]{1,0:T(8,128)(2,1)} %gate_ref.5, bf16[4096,1920]{1,0:T(8,128)(2,1)} %up_ref.5, bf16[1920,4096]{1,0:T(8,128)(2,1)} %down_ref.5, bf16[3,96,1024]{2,1,0:T(8,128)(2,1)S(1)} %get-tuple-element.60.refs_0_), custom_call_target="tpu_custom_call" | custom-call | flops 419430400 | bytes 15728640 | tf_op jit(solution)/shard_map/layer/pallas_call | solution.py:176
  42.1 4.1 %collective-permute-start.6 = (bf16[3,96,1024]{2,1,0:T(8,128)(2,1)S(1)}, bf16[3,96,1024]{2,1,0:T(8,128)(2,1)S(1)}, u32[]{:S(2)}, u32[]{:S(2)}) collective-permute-start(bf16[3,96,1024]{2,1,0:T(8,128)(2,1)S(1)} %get-tuple-element.63.refs_1_), channel_id=1, source_target_pairs={{0,8},{8,24},{24,16},{16,0},{1,9},{9,25},{25,17},{17,1},{2,10},{10... | collective-permute-start | bytes 1769480 | tf_op jit(solution)/shard_map/ppermute | solution.py:458
  46.1 9.6 %layer.4 = (bf16[16,640]{1,0:T(8,128)(2,1)S(1)}, f32[16,4096]{1,0:T(8,128)S(1)}) custom-call(bf16[16,8192]{1,0:T(8,128)(2,1)S(1)} %reshape.12.refs_5_.both, bf16[4096,1920]{1,0:T(8,128)(2,1)} %gate_ref.5, bf16[4096,1920]{1,0:T(8,128)(2,1)} %up_ref.5, bf16[1920,4096]{1,0:T(8,128)(2,1)} %down_ref.5, f32[16,4096]{1,0:T(8,128)S(1)} %get-tuple-element.61.refs_5_.refs_0_, ...), custom_call_target="tpu_custom_call" | custom-call | flops 419430400 | bytes 15728640 | tf_op jit(solution)/shard_map/layer/pallas_call | solution.py:176
  55.8 1.3 pack.16
  57.3 3.5 %collective-permute-start.9 = (bf16[3,96,1024]{2,1,0:T(8,128)(2,1)}, bf16[3,96,1024]{2,1,0:T(8,128)(2,1)S(1)}, u32[]{:S(2)}, u32[]{:S(2)}) collective-permute-start(bf16[3,96,1024]{2,1,0:T(8,128)(2,1)} %get-tuple-element.66.refs_1_), channel_id=1, source_target_pairs={{0,8},{8,24},{24,16},{16,0},{1,9},{9,25},{25,17},{17,1},{2,10},{10... | collective-permute-start | bytes 1769480 | tf_op jit(solution)/shard_map/ppermute | solution.py:458
  60.7 9.6 %layer.5 = (bf16[16,640]{1,0:T(8,128)(2,1)S(1)}, f32[16,4096]{1,0:T(8,128)S(1)}) custom-call(bf16[16,8192]{1,0:T(8,128)(2,1)S(1)} %reshape.12.refs_5_.both, bf16[4096,1920]{1,0:T(8,128)(2,1)} %gate_ref.5, bf16[4096,1920]{1,0:T(8,128)(2,1)} %up_ref.5, bf16[1920,4096]{1,0:T(8,128)(2,1)} %down_ref.5, f32[16,4096]{1,0:T(8,128)S(1)} %get-tuple-element.64.refs_5_.refs_0_, ...), custom_call_target="tpu_custom_call" | custom-call | flops 419430400 | bytes 15728640 | tf_op jit(solution)/shard_map/layer/pallas_call | solution.py:176
  70.4 1.2 pack.17
  71.7 3.8 %collective-permute-start.12 = (bf16[3,96,1024]{2,1,0:T(8,128)(2,1)S(1)}, bf16[3,96,1024]{2,1,0:T(8,128)(2,1)}, u32[]{:S(2)}, u32[]{:S(2)}) collective-permute-start(bf16[3,96,1024]{2,1,0:T(8,128)(2,1)S(1)} %get-tuple-element.69.refs_1_.refs_5_), channel_id=1, source_target_pairs={{0,8},{8,24},{24,16},{16,0},{1,9},{9,25},{25,17},{17,1},{2,10},{10... | collective-permute-start | bytes 1769480 | tf_op jit(solution)/shard_map/ppermute | solution.py:458
  75.6 1.2 pack.18
  76.9 3.9 %collective-permute-start.15 = (bf16[3,96,1024]{2,1,0:T(8,128)(2,1)S(1)}, bf16[3,96,1024]{2,1,0:T(8,128)(2,1)}, u32[]{:S(2)}, u32[]{:S(2)}) collective-permute-start(bf16[3,96,1024]{2,1,0:T(8,128)(2,1)S(1)} %get-tuple-element.73.refs_2_.refs_5_), channel_id=1, source_target_pairs={{0,8},{8,24},{24,16},{16,0},{1,9},{9,25},{25,17},{17,1},{2,10},{10... | collective-permute-start | bytes 1769480 | tf_op jit(solution)/shard_map/ppermute | solution.py:458
  80.8 9.3 %collective-permute-done.13.refs_4_.refs_11_ = bf16[3,96,1024]{2,1,0:T(8,128)(2,1)} collective-permute-done((bf16[3,96,1024]{2,1,0:T(8,128)(2,1)}, bf16[3,96,1024]{2,1,0:T(8,128)(2,1)}, u32[]{:S(2)}, u32[]{:S(2)}) %collective-permute-start.13) | collective-permute-done | bytes 589856 | tf_op jit(solution)/shard_map/ppermute | solution.py:459
  90.1 19.1 %pack.19 = (bf16[3,96,1024]{2,1,0:T(8,128)(2,1)S(1)}, bf16[3,96,1024]{2,1,0:T(8,128)(2,1)}) custom-call(s32[1]{0:T(128)} %bitcast.6.flag, f32[2,1920,1024]{2,1,0:T(8,128)} %refs_0_.23, f32[2,1920,1024]{2,1,0:T(8,128)} %refs_1_.23, f32[2,1920,1024]{2,1,0:T(8,128)} %refs_2_.23, bf16[3,96,1024]{2,1,0:T(8,128)(2,1)} %collective-permute-done.12.refs_3_.refs_10_, ...), custom_call_target="tpu_custom_call" | custom-call | bytes 3538944 | tf_op jit(solution)/shard_map/pack/pallas_call | solution.py:90
  109.2 1.9 collective-permute-start.21
  111.3 0.7 pad_maximum_fusion
  111.9 3.3 %collective-permute-start.19 = (bf16[16,2944]{1,0:T(8,128)(2,1)}, bf16[16,2944]{1,0:T(8,128)(2,1)S(1)}, u32[]{:S(2)}, u32[]{:S(2)}) collective-permute-start(bf16[16,2944]{1,0:T(8,128)(2,1)} %get-tuple-element.114), channel_id=1, source_target_pairs={{0,24},{8,0},{16,8},{24,16},{1,25},{9,1},{17,9},{25,17},{2,26},{10... | collective-permute-start | bytes 282632 | tf_op jit(solution)/shard_map/ppermute | solution.py:492
  115.2 0.8 copy-done.23
  116.0 0.6 fusion
  118.0 0.6 collective-permute-start.18
  118.6 1.1 copy-done.24
  119.7 1.2 pack.20
  120.8 5.4 %collective-permute-done.19.refs_3_ = bf16[16,2944]{1,0:T(8,128)(2,1)S(1)} collective-permute-done((bf16[16,2944]{1,0:T(8,128)(2,1)}, bf16[16,2944]{1,0:T(8,128)(2,1)S(1)}, u32[]{:S(2)}, u32[]{:S(2)}) %collective-permute-start.19) | collective-permute-done | bytes 94240 | tf_op jit(solution)/shard_map/ppermute | solution.py:492
  126.2 1.8 collective-permute-start.25
  128.0 1.5 collective-permute-done.17.refs_1_
  129.9 3.6 %update.2 = (f32[1920,1024]{1,0:T(8,128)}, f32[1920,1024]{1,0:T(8,128)}, f32[1920,1024]{1,0:T(8,128)}) custom-call(s32[2]{0:T(128)S(1)} %pad_add_fusion.info, bf16[1920,64]{1,0:T(8,128)(2,1)S(1)} %get-tuple-element.85.hid_ref.refs_0_, bf16[64,1024]{1,0:T(8,128)(2,1)S(1)} %get-tuple-element.86.out_ref, f32[2,1920,1024]{2,1,0:T(8,128)} %refs_0_.23, ...), custom_call_target="tpu_custom_call" | custom-call | flops 125829120 | bytes 23592960 | tf_op jit(solution)/shard_map/update/pallas_call | solution.py:302
  133.5 1.4 pack.21
  134.9 10.2 %collective-permute-start.23 = (bf16[3,96,1024]{2,1,0:T(8,128)(2,1)S(1)}, bf16[3,96,1024]{2,1,0:T(8,128)(2,1)S(1)}, u32[]{:S(2)}, u32[]{:S(2)}) collective-permute-start(bf16[3,96,1024]{2,1,0:T(8,128)(2,1)S(1)} %get-tuple-element.90), channel_id=1, source_target_pairs={{8,0},{24,8},{16,24},{0,16},{9,1},{25,9},{17,25},{1,17},{10,2},{26... | collective-permute-start | bytes 1769480 | tf_op jit(solution)/shard_map/ppermute | solution.py:459
  145.7 3.6 %update.3 = (f32[1920,1024]{1,0:T(8,128)}, f32[1920,1024]{1,0:T(8,128)}, f32[1920,1024]{1,0:T(8,128)}) custom-call(s32[2]{0:T(128)S(1)} %pad_add_fusion.info, bf16[1920,64]{1,0:T(8,128)(2,1)S(1)} %get-tuple-element.85.hid_ref.refs_0_, bf16[64,1024]{1,0:T(8,128)(2,1)S(1)} %get-tuple-element.86.out_ref, ...), custom_call_target="tpu_custom_call", output_to_operand_aliasing={{0}: (6, {}), {1}: (7, {}), {2}: (8, {})} | custom-call | flops 125829120 | bytes 23592960 | tf_op jit(solution)/shard_map/update/pallas_call | solution.py:302
  149.4 1.1 pack.22
  150.7 9.7 %collective-permute-start.29 = (bf16[3,96,1024]{2,1,0:T(8,128)(2,1)}, bf16[3,96,1024]{2,1,0:T(8,128)(2,1)}, u32[]{:S(2)}, u32[]{:S(2)}) collective-permute-start(bf16[3,96,1024]{2,1,0:T(8,128)(2,1)} %get-tuple-element.101), channel_id=1, source_target_pairs={{8,0},{24,8},{16,24},{0,16},{9,1},{25,9},{17,25},{1,17},{10,2},{26... | collective-permute-start | bytes 1769480 | tf_op jit(solution)/shard_map/ppermute | solution.py:459
  160.4 2.2 %collective-permute-start.28 = (bf16[3,96,1024]{2,1,0:T(8,128)(2,1)}, bf16[3,96,1024]{2,1,0:T(8,128)(2,1)}, u32[]{:S(2)}, u32[]{:S(2)}) collective-permute-start(bf16[3,96,1024]{2,1,0:T(8,128)(2,1)} %get-tuple-element.97.refs_21_), channel_id=1, source_target_pairs={{0,8},{8,24},{24,16},{16,0},{1,9},{9,25},{25,17},{17,1},{2,10},{10... | collective-permute-start | bytes 1769480 | tf_op jit(solution)/shard_map/ppermute | solution.py:458
  162.6 16.9 %patch.3 = (f32[1920,1024]{1,0:T(8,128)}, f32[1920,1024]{1,0:T(8,128)}, f32[1920,1024]{1,0:T(8,128)}) custom-call(s32[2]{0:T(128)S(1)} %pad_add_fusion.info, bf16[1920,64]{1,0:T(8,128)(2,1)S(1)} %get-tuple-element.85.hid_ref.refs_0_, bf16[64,1024]{1,0:T(8,128)(2,1)S(1)} %get-tuple-element.86.out_ref, ...), custom_call_target="tpu_custom_call", output_to_operand_aliasing={{0}: (21, {}), {1}: (22, {}), {2}: (23, {})} | custom-call | flops 226492416 | bytes 31850496 | tf_op jit(solution)/shard_map/patch/pallas_call | solution.py:403
  179.5 1.2 pack.23
  180.8 2.0 collective-permute-start.26
  182.9 7.2 %collective-permute-done.8.refs_1_ = f32[8,4096]{1,0:T(8,128)S(1)} collective-permute-done((f32[8,4096]{1,0:T(8,128)S(1)}, f32[8,4096]{1,0:T(8,128)S(1)}, u32[]{:S(2)}, u32[]{:S(2)}) %collective-permute-start.8) | collective-permute-done | bytes 131104 | tf_op jit(solution)/shard_map/ppermute | solution.py:248
  190.1 1.1 copy-done.3
  191.6 4.0 %collective-permute-done.11.refs_1_ = f32[4,4096]{1,0:T(4,128)S(1)} collective-permute-done((f32[4,4096]{1,0:T(4,128)S(1)}, f32[4,4096]{1,0:T(4,128)S(1)}, u32[]{:S(2)}, u32[]{:S(2)}) %collective-permute-start.11) | collective-permute-done | bytes 65568 | tf_op jit(solution)/shard_map/ppermute | solution.py:248
  195.6 1.1 copy-done.1
  196.7 1.2 collective-permute-done.14.refs_1_
  197.9 0.6 halve.7
  198.6 4.9 %patch.4 = (f32[1920,1024]{1,0:T(8,128)}, f32[1920,1024]{1,0:T(8,128)}, f32[1920,1024]{1,0:T(8,128)}) custom-call(s32[2]{0:T(128)S(1)} %pad_add_fusion.info, bf16[1920,64]{1,0:T(8,128)(2,1)S(1)} %get-tuple-element.85.hid_ref.refs_0_, bf16[64,1024]{1,0:T(8,128)(2,1)S(1)} %get-tuple-element.86.out_ref, ...), custom_call_target="tpu_custom_call", output_to_operand_aliasing={{0}: (7, {}), {1}: (8, {}), {2}: (9, {})} | custom-call | flops 50331648 | bytes 7077888 | tf_op jit(solution)/shard_map/patch/pallas_call | solution.py:403
  203.5 3.6 %patch.5 = (f32[1920,1024]{1,0:T(8,128)}, f32[1920,1024]{1,0:T(8,128)}, f32[1920,1024]{1,0:T(8,128)}) custom-call(s32[2]{0:T(128)S(1)} %pad_add_fusion.info, bf16[1920,64]{1,0:T(8,128)(2,1)S(1)} %get-tuple-element.85.hid_ref.refs_0_, bf16[64,1024]{1,0:T(8,128)(2,1)S(1)} %get-tuple-element.86.out_ref, ...), custom_call_target="tpu_custom_call", output_to_operand_aliasing={{0}: (5, {}), {1}: (6, {}), {2}: (7, {})} | custom-call | flops 25165824 | bytes 3538944 | tf_op jit(solution)/shard_map/patch/pallas_call | solution.py:403
  (105 shorter events, 4.7 us)
Async XLA Ops:
  3.7 22.9 %collective-permute-start.1 = (bf16[3,96,1024]{2,1,0:T(8,128)(2,1)}, bf16[3,96,1024]{2,1,0:T(8,128)(2,1)S(1)}, u32[]{:S(2)}, u32[]{:S(2)}) collective-permute-start(bf16[3,96,1024]{2,1,0:T(8,128)(2,1)} %get-tuple-element.59), channel_id=1, source_target_pairs={{8,0},{24,8},{16,24},{0,16},{9,1},{25,9},{17,25},{1,17},{10,2},{26... | collective-permute-start | bytes 1769480 | tf_op jit(solution)/shard_map/ppermute | solution.py:459
  6.7 4.9 %copy-start.27 = (bf16[1,2,4096]{2,1,0:T(2,128)(2,1)S(1)}, bf16[1,2,4096]{2,1,0:T(2,128)(2,1)}, u32[]{:S(2)}) copy-start(bf16[1,2,4096]{2,1,0:T(2,128)(2,1)} %param.10) | copy-start | bytes 49156
  6.7 4.9 %copy-start.28 = (bf16[1,2,4096]{2,1,0:T(2,128)(2,1)S(1)}, bf16[1,2,4096]{2,1,0:T(2,128)(2,1)}, u32[]{:S(2)}) copy-start(bf16[1,2,4096]{2,1,0:T(2,128)(2,1)} %param.11) | copy-start | bytes 49156
  6.7 19.9 %collective-permute-start = (bf16[3,96,1024]{2,1,0:T(8,128)(2,1)}, bf16[3,96,1024]{2,1,0:T(8,128)(2,1)S(1)}, u32[]{:S(2)}, u32[]{:S(2)}) collective-permute-start(bf16[3,96,1024]{2,1,0:T(8,128)(2,1)} %get-tuple-element.57.refs_3_), channel_id=1, source_target_pairs={{0,8},{8,24},{24,16},{16,0},{1,9},{9,25},{25,17},{17,1},{2,10},{10... | collective-permute-start | bytes 1769480 | tf_op jit(solution)/shard_map/ppermute | solution.py:458
  9.5 31.4 %collective-permute-start.3 = (bf16[3,96,1024]{2,1,0:T(8,128)(2,1)}, bf16[3,96,1024]{2,1,0:T(8,128)(2,1)S(1)}, u32[]{:S(2)}, u32[]{:S(2)}) collective-permute-start(bf16[3,96,1024]{2,1,0:T(8,128)(2,1)} %get-tuple-element.62), channel_id=1, source_target_pairs={{8,0},{24,8},{16,24},{0,16},{9,1},{25,9},{17,25},{1,17},{10,2},{26... | collective-permute-start | bytes 1769480 | tf_op jit(solution)/shard_map/ppermute | solution.py:459
  11.6 29.4 %collective-permute-start.2 = (bf16[3,96,1024]{2,1,0:T(8,128)(2,1)S(1)}, bf16[3,96,1024]{2,1,0:T(8,128)(2,1)S(1)}, u32[]{:S(2)}, u32[]{:S(2)}) collective-permute-start(bf16[3,96,1024]{2,1,0:T(8,128)(2,1)S(1)} %get-tuple-element.58.refs_2_), channel_id=1, source_target_pairs={{0,8},{8,24},{24,16},{16,0},{1,9},{9,25},{25,17},{17,1},{2,10},{10... | collective-permute-start | bytes 1769480 | tf_op jit(solution)/shard_map/ppermute | solution.py:458
  27.6 28.1 %collective-permute-start.5 = (bf16[3,96,1024]{2,1,0:T(8,128)(2,1)S(1)}, bf16[3,96,1024]{2,1,0:T(8,128)(2,1)S(1)}, u32[]{:S(2)}, u32[]{:S(2)}) collective-permute-start(bf16[3,96,1024]{2,1,0:T(8,128)(2,1)S(1)} %get-tuple-element.65), channel_id=1, source_target_pairs={{8,0},{24,8},{16,24},{0,16},{9,1},{25,9},{17,25},{1,17},{10,2},{26... | collective-permute-start | bytes 1769480 | tf_op jit(solution)/shard_map/ppermute | solution.py:459
  29.2 26.6 %collective-permute-start.4 = (bf16[3,96,1024]{2,1,0:T(8,128)(2,1)S(1)}, bf16[3,96,1024]{2,1,0:T(8,128)(2,1)S(1)}, u32[]{:S(2)}, u32[]{:S(2)}) collective-permute-start(bf16[3,96,1024]{2,1,0:T(8,128)(2,1)S(1)} %get-tuple-element.60.refs_0_), channel_id=1, source_target_pairs={{0,8},{8,24},{24,16},{16,0},{1,9},{9,25},{25,17},{17,1},{2,10},{10... | collective-permute-start | bytes 1769480 | tf_op jit(solution)/shard_map/ppermute | solution.py:458
  42.1 28.3 %collective-permute-start.7 = (bf16[3,96,1024]{2,1,0:T(8,128)(2,1)S(1)}, bf16[3,96,1024]{2,1,0:T(8,128)(2,1)S(1)}, u32[]{:S(2)}, u32[]{:S(2)}) collective-permute-start(bf16[3,96,1024]{2,1,0:T(8,128)(2,1)S(1)} %get-tuple-element.68), channel_id=1, source_target_pairs={{8,0},{24,8},{16,24},{0,16},{9,1},{25,9},{17,25},{1,17},{10,2},{26... | collective-permute-start | bytes 1769480 | tf_op jit(solution)/shard_map/ppermute | solution.py:459
  42.1 28.3 %collective-permute-start.6 = (bf16[3,96,1024]{2,1,0:T(8,128)(2,1)S(1)}, bf16[3,96,1024]{2,1,0:T(8,128)(2,1)S(1)}, u32[]{:S(2)}, u32[]{:S(2)}) collective-permute-start(bf16[3,96,1024]{2,1,0:T(8,128)(2,1)S(1)} %get-tuple-element.63.refs_1_), channel_id=1, source_target_pairs={{0,8},{8,24},{24,16},{16,0},{1,9},{9,25},{25,17},{17,1},{2,10},{10... | collective-permute-start | bytes 1769480 | tf_op jit(solution)/shard_map/ppermute | solution.py:458
  55.8 1.3 copy-start.12
  55.8 1.4 copy-start.14
  57.3 18.3 %collective-permute-start.10 = (bf16[3,96,1024]{2,1,0:T(8,128)(2,1)}, bf16[3,96,1024]{2,1,0:T(8,128)(2,1)S(1)}, u32[]{:S(2)}, u32[]{:S(2)}) collective-permute-start(bf16[3,96,1024]{2,1,0:T(8,128)(2,1)} %get-tuple-element.72), channel_id=1, source_target_pairs={{8,0},{24,8},{16,24},{0,16},{9,1},{25,9},{17,25},{1,17},{10,2},{26... | collective-permute-start | bytes 1769480 | tf_op jit(solution)/shard_map/ppermute | solution.py:459
  57.3 18.3 %collective-permute-start.9 = (bf16[3,96,1024]{2,1,0:T(8,128)(2,1)}, bf16[3,96,1024]{2,1,0:T(8,128)(2,1)S(1)}, u32[]{:S(2)}, u32[]{:S(2)}) collective-permute-start(bf16[3,96,1024]{2,1,0:T(8,128)(2,1)} %get-tuple-element.66.refs_1_), channel_id=1, source_target_pairs={{0,8},{8,24},{24,16},{16,0},{1,9},{9,25},{25,17},{17,1},{2,10},{10... | collective-permute-start | bytes 1769480 | tf_op jit(solution)/shard_map/ppermute | solution.py:458
  71.7 18.4 %collective-permute-start.13 = (bf16[3,96,1024]{2,1,0:T(8,128)(2,1)}, bf16[3,96,1024]{2,1,0:T(8,128)(2,1)}, u32[]{:S(2)}, u32[]{:S(2)}) collective-permute-start(bf16[3,96,1024]{2,1,0:T(8,128)(2,1)} %get-tuple-element.76), channel_id=1, source_target_pairs={{8,0},{24,8},{16,24},{0,16},{9,1},{25,9},{17,25},{1,17},{10,2},{26... | collective-permute-start | bytes 1769480 | tf_op jit(solution)/shard_map/ppermute | solution.py:459
  71.7 18.3 %collective-permute-start.12 = (bf16[3,96,1024]{2,1,0:T(8,128)(2,1)S(1)}, bf16[3,96,1024]{2,1,0:T(8,128)(2,1)}, u32[]{:S(2)}, u32[]{:S(2)}) collective-permute-start(bf16[3,96,1024]{2,1,0:T(8,128)(2,1)S(1)} %get-tuple-element.69.refs_1_.refs_5_), channel_id=1, source_target_pairs={{0,8},{8,24},{24,16},{16,0},{1,9},{9,25},{25,17},{17,1},{2,10},{10... | collective-permute-start | bytes 1769480 | tf_op jit(solution)/shard_map/ppermute | solution.py:458
  75.6 1.3 copy-start.21
  76.8 32.3 %copy-start.2 = (bf16[3,96,1024]{2,1,0:T(8,128)(2,1)}, bf16[3,96,1024]{2,1,0:T(8,128)(2,1)S(1)}, u32[]{:S(2)}) copy-start(bf16[3,96,1024]{2,1,0:T(8,128)(2,1)S(1)} %get-tuple-element.73.refs_2_.refs_5_) | copy-start | bytes 1769476
  76.8 38.4 %collective-permute-start.16 = (bf16[3,96,1024]{2,1,0:T(8,128)(2,1)}, bf16[3,96,1024]{2,1,0:T(8,128)(2,1)S(1)}, u32[]{:S(2)}, u32[]{:S(2)}) collective-permute-start(bf16[3,96,1024]{2,1,0:T(8,128)(2,1)} %get-tuple-element.80), channel_id=1, source_target_pairs={{8,0},{24,8},{16,24},{0,16},{9,1},{25,9},{17,25},{1,17},{10,2},{26... | collective-permute-start | bytes 1769480 | tf_op jit(solution)/shard_map/ppermute | solution.py:459
  76.9 39.1 %copy-start.29 = (s32[4]{0:T(128)S(1)}, s32[4]{0:T(128)}, u32[]{:S(2)}) copy-start(s32[4]{0:T(128)} %constant.103.clone) | copy-start | bytes 52
  76.9 41.0 %collective-permute-start.15 = (bf16[3,96,1024]{2,1,0:T(8,128)(2,1)S(1)}, bf16[3,96,1024]{2,1,0:T(8,128)(2,1)}, u32[]{:S(2)}, u32[]{:S(2)}) collective-permute-start(bf16[3,96,1024]{2,1,0:T(8,128)(2,1)S(1)} %get-tuple-element.73.refs_2_.refs_5_), channel_id=1, source_target_pairs={{0,8},{8,24},{24,16},{16,0},{1,9},{9,25},{25,17},{17,1},{2,10},{10... | collective-permute-start | bytes 1769480 | tf_op jit(solution)/shard_map/ppermute | solution.py:458
  109.2 11.7 %copy-start = (bf16[3,96,1024]{2,1,0:T(8,128)(2,1)}, bf16[3,96,1024]{2,1,0:T(8,128)(2,1)S(1)}, u32[]{:S(2)}) copy-start(bf16[3,96,1024]{2,1,0:T(8,128)(2,1)S(1)} %get-tuple-element.77.refs_2_.refs_5_) | copy-start | bytes 1769476
  109.2 24.3 %collective-permute-start.21 = (bf16[3,96,1024]{2,1,0:T(8,128)(2,1)}, bf16[3,96,1024]{2,1,0:T(8,128)(2,1)}, u32[]{:S(2)}, u32[]{:S(2)}) collective-permute-start(bf16[3,96,1024]{2,1,0:T(8,128)(2,1)} %get-tuple-element.87), channel_id=1, source_target_pairs={{8,0},{24,8},{16,24},{0,16},{9,1},{25,9},{17,25},{1,17},{10,2},{26... | collective-permute-start | bytes 1769480 | tf_op jit(solution)/shard_map/ppermute | solution.py:459
  111.0 22.5 %collective-permute-start.20 = (bf16[3,96,1024]{2,1,0:T(8,128)(2,1)S(1)}, bf16[3,96,1024]{2,1,0:T(8,128)(2,1)}, u32[]{:S(2)}, u32[]{:S(2)}) collective-permute-start(bf16[3,96,1024]{2,1,0:T(8,128)(2,1)S(1)} %get-tuple-element.77.refs_2_.refs_5_), channel_id=1, source_target_pairs={{0,8},{8,24},{24,16},{16,0},{1,9},{9,25},{25,17},{17,1},{2,10},{10... | collective-permute-start | bytes 1769480 | tf_op jit(solution)/shard_map/ppermute | solution.py:458
  111.9 14.3 %collective-permute-start.19 = (bf16[16,2944]{1,0:T(8,128)(2,1)}, bf16[16,2944]{1,0:T(8,128)(2,1)S(1)}, u32[]{:S(2)}, u32[]{:S(2)}) collective-permute-start(bf16[16,2944]{1,0:T(8,128)(2,1)} %get-tuple-element.114), channel_id=1, source_target_pairs={{0,24},{8,0},{16,8},{24,16},{1,25},{9,1},{17,9},{25,17},{2,26},{10... | collective-permute-start | bytes 282632 | tf_op jit(solution)/shard_map/ppermute | solution.py:492
  116.0 13.4 %collective-permute-start.17 = (bf16[16,2944]{1,0:T(8,128)(2,1)S(1)}, bf16[16,2944]{1,0:T(8,128)(2,1)S(1)}, u32[]{:S(2)}, u32[]{:S(2)}) collective-permute-start(bf16[16,2944]{1,0:T(8,128)(2,1)S(1)} %get-tuple-element.115), channel_id=1, source_target_pairs={{0,8},{8,16},{16,24},{24,0},{1,9},{9,17},{17,25},{25,1},{2,10},{10... | collective-permute-start | bytes 282632 | tf_op jit(solution)/shard_map/ppermute | solution.py:492
  118.0 11.7 %collective-permute-start.18 = (bf16[16,2944]{1,0:T(8,128)(2,1)S(1)}, bf16[16,2944]{1,0:T(8,128)(2,1)S(1)}, u32[]{:S(2)}, u32[]{:S(2)}) collective-permute-start(bf16[16,2944]{1,0:T(8,128)(2,1)S(1)} %get-tuple-element.116), channel_id=1, source_target_pairs={{0,16},{8,24},{16,0},{24,8},{1,17},{9,25},{17,1},{25,9},{2,18},{10... | collective-permute-start | bytes 282632 | tf_op jit(solution)/shard_map/ppermute | solution.py:492
  126.2 23.0 %collective-permute-start.25 = (bf16[3,96,1024]{2,1,0:T(8,128)(2,1)S(1)}, bf16[3,96,1024]{2,1,0:T(8,128)(2,1)S(1)}, u32[]{:S(2)}, u32[]{:S(2)}) collective-permute-start(bf16[3,96,1024]{2,1,0:T(8,128)(2,1)S(1)} %get-tuple-element.91), channel_id=1, source_target_pairs={{8,0},{24,8},{16,24},{0,16},{9,1},{25,9},{17,25},{1,17},{10,2},{26... | collective-permute-start | bytes 1769480 | tf_op jit(solution)/shard_map/ppermute | solution.py:459
  129.5 19.8 %collective-permute-start.24 = (bf16[3,96,1024]{2,1,0:T(8,128)(2,1)S(1)}, bf16[3,96,1024]{2,1,0:T(8,128)(2,1)S(1)}, u32[]{:S(2)}, u32[]{:S(2)}) collective-permute-start(bf16[3,96,1024]{2,1,0:T(8,128)(2,1)S(1)} %get-tuple-element.81.refs_2_.refs_4_), channel_id=1, source_target_pairs={{0,8},{8,24},{24,16},{16,0},{1,9},{9,25},{25,17},{17,1},{2,10},{10... | collective-permute-start | bytes 1769480 | tf_op jit(solution)/shard_map/ppermute | solution.py:458
  134.9 44.6 %collective-permute-start.23 = (bf16[3,96,1024]{2,1,0:T(8,128)(2,1)S(1)}, bf16[3,96,1024]{2,1,0:T(8,128)(2,1)S(1)}, u32[]{:S(2)}, u32[]{:S(2)}) collective-permute-start(bf16[3,96,1024]{2,1,0:T(8,128)(2,1)S(1)} %get-tuple-element.90), channel_id=1, source_target_pairs={{8,0},{24,8},{16,24},{0,16},{9,1},{25,9},{17,25},{1,17},{10,2},{26... | collective-permute-start | bytes 1769480 | tf_op jit(solution)/shard_map/ppermute | solution.py:459
  145.1 34.4 %collective-permute-start.22 = (bf16[3,96,1024]{2,1,0:T(8,128)(2,1)S(1)}, bf16[3,96,1024]{2,1,0:T(8,128)(2,1)S(1)}, u32[]{:S(2)}, u32[]{:S(2)}) collective-permute-start(bf16[3,96,1024]{2,1,0:T(8,128)(2,1)S(1)} %get-tuple-element.89.refs_3_), channel_id=1, source_target_pairs={{0,8},{8,24},{24,16},{16,0},{1,9},{9,25},{25,17},{17,1},{2,10},{10... | collective-permute-start | bytes 1769480 | tf_op jit(solution)/shard_map/ppermute | solution.py:458
  149.3 1.4 copy-start.26
  149.3 13.3 %copy-start.5 = (bf16[3,96,1024]{2,1,0:T(8,128)(2,1)S(1)}, bf16[3,96,1024]{2,1,0:T(8,128)(2,1)}, u32[]{:S(2)}) copy-start(bf16[3,96,1024]{2,1,0:T(8,128)(2,1)} %copy-done.4) | copy-start | bytes 1769476
  149.3 13.3 %copy-start.7 = (bf16[3,96,1024]{2,1,0:T(8,128)(2,1)S(1)}, bf16[3,96,1024]{2,1,0:T(8,128)(2,1)}, u32[]{:S(2)}) copy-start(bf16[3,96,1024]{2,1,0:T(8,128)(2,1)} %copy-done.6) | copy-start | bytes 1769476
  149.3 13.3 %copy-start.9 = (bf16[3,96,1024]{2,1,0:T(8,128)(2,1)S(1)}, bf16[3,96,1024]{2,1,0:T(8,128)(2,1)}, u32[]{:S(2)}) copy-start(bf16[3,96,1024]{2,1,0:T(8,128)(2,1)} %copy-done.8) | copy-start | bytes 1769476
  149.3 13.3 %copy-start.11 = (bf16[3,96,1024]{2,1,0:T(8,128)(2,1)S(1)}, bf16[3,96,1024]{2,1,0:T(8,128)(2,1)}, u32[]{:S(2)}) copy-start(bf16[3,96,1024]{2,1,0:T(8,128)(2,1)} %copy-done.10) | copy-start | bytes 1769476
  149.3 13.3 %copy-start.13 = (bf16[3,96,1024]{2,1,0:T(8,128)(2,1)S(1)}, bf16[3,96,1024]{2,1,0:T(8,128)(2,1)}, u32[]{:S(2)}) copy-start(bf16[3,96,1024]{2,1,0:T(8,128)(2,1)} %copy-done.12) | copy-start | bytes 1769476
  149.3 13.3 %copy-start.15 = (bf16[3,96,1024]{2,1,0:T(8,128)(2,1)S(1)}, bf16[3,96,1024]{2,1,0:T(8,128)(2,1)}, u32[]{:S(2)}) copy-start(bf16[3,96,1024]{2,1,0:T(8,128)(2,1)} %copy-done.14) | copy-start | bytes 1769476
  149.3 13.3 %copy-start.17 = (bf16[3,96,1024]{2,1,0:T(8,128)(2,1)S(1)}, bf16[3,96,1024]{2,1,0:T(8,128)(2,1)}, u32[]{:S(2)}) copy-start(bf16[3,96,1024]{2,1,0:T(8,128)(2,1)} %copy-done.16) | copy-start | bytes 1769476
  149.3 13.3 %copy-start.19 = (bf16[3,96,1024]{2,1,0:T(8,128)(2,1)S(1)}, bf16[3,96,1024]{2,1,0:T(8,128)(2,1)}, u32[]{:S(2)}) copy-start(bf16[3,96,1024]{2,1,0:T(8,128)(2,1)} %copy-done.18) | copy-start | bytes 1769476
  149.4 13.3 %copy-start.22 = (bf16[3,96,1024]{2,1,0:T(8,128)(2,1)S(1)}, bf16[3,96,1024]{2,1,0:T(8,128)(2,1)}, u32[]{:S(2)}) copy-start(bf16[3,96,1024]{2,1,0:T(8,128)(2,1)} %copy-done.21) | copy-start | bytes 1769476
  150.7 47.9 %collective-permute-start.29 = (bf16[3,96,1024]{2,1,0:T(8,128)(2,1)}, bf16[3,96,1024]{2,1,0:T(8,128)(2,1)}, u32[]{:S(2)}, u32[]{:S(2)}) collective-permute-start(bf16[3,96,1024]{2,1,0:T(8,128)(2,1)} %get-tuple-element.101), channel_id=1, source_target_pairs={{8,0},{24,8},{16,24},{0,16},{9,1},{25,9},{17,25},{1,17},{10,2},{26... | collective-permute-start | bytes 1769480 | tf_op jit(solution)/shard_map/ppermute | solution.py:459
  160.4 38.2 %collective-permute-start.28 = (bf16[3,96,1024]{2,1,0:T(8,128)(2,1)}, bf16[3,96,1024]{2,1,0:T(8,128)(2,1)}, u32[]{:S(2)}, u32[]{:S(2)}) collective-permute-start(bf16[3,96,1024]{2,1,0:T(8,128)(2,1)} %get-tuple-element.97.refs_21_), channel_id=1, source_target_pairs={{0,8},{8,24},{24,16},{16,0},{1,9},{9,25},{25,17},{17,1},{2,10},{10... | collective-permute-start | bytes 1769480 | tf_op jit(solution)/shard_map/ppermute | solution.py:458
  180.7 22.8 %collective-permute-start.27 = (bf16[3,96,1024]{2,1,0:T(8,128)(2,1)}, bf16[3,96,1024]{2,1,0:T(8,128)(2,1)}, u32[]{:S(2)}, u32[]{:S(2)}) collective-permute-start(bf16[3,96,1024]{2,1,0:T(8,128)(2,1)} %get-tuple-element.100), channel_id=1, source_target_pairs={{8,0},{24,8},{16,24},{0,16},{9,1},{25,9},{17,25},{1,17},{10,2},{26... | collective-permute-start | bytes 1769480 | tf_op jit(solution)/shard_map/ppermute | solution.py:459
  180.8 22.7 %collective-permute-start.26 = (bf16[3,96,1024]{2,1,0:T(8,128)(2,1)}, bf16[3,96,1024]{2,1,0:T(8,128)(2,1)}, u32[]{:S(2)}, u32[]{:S(2)}) collective-permute-start(bf16[3,96,1024]{2,1,0:T(8,128)(2,1)} %get-tuple-element.99.refs_7_), channel_id=1, source_target_pairs={{0,8},{8,24},{24,16},{16,0},{1,9},{9,25},{25,17},{17,1},{2,10},{10... | collective-permute-start | bytes 1769480 | tf_op jit(solution)/shard_map/ppermute | solution.py:458
  182.8 7.3 %collective-permute-start.8 = (f32[8,4096]{1,0:T(8,128)S(1)}, f32[8,4096]{1,0:T(8,128)S(1)}, u32[]{:S(2)}, u32[]{:S(2)}) collective-permute-start(f32[8,4096]{1,0:T(8,128)S(1)} %get-tuple-element.71), channel_id=1, source_target_pairs={{0,4},{2,6},{4,0},{6,2},{1,5},{3,7},{5,1},{7,3},{8,12},{10,14},{12... | collective-permute-start | bytes 393224 | tf_op jit(solution)/shard_map/ppermute | solution.py:248
  191.2 4.3 %collective-permute-start.11 = (f32[4,4096]{1,0:T(4,128)S(1)}, f32[4,4096]{1,0:T(4,128)S(1)}, u32[]{:S(2)}, u32[]{:S(2)}) collective-permute-start(f32[4,4096]{1,0:T(4,128)S(1)} %get-tuple-element.75), channel_id=1, source_target_pairs={{0,2},{2,0},{4,6},{6,4},{1,3},{3,1},{5,7},{7,5},{8,10},{10,8},{12,... | collective-permute-start | bytes 196616 | tf_op jit(solution)/shard_map/ppermute | solution.py:248
  196.7 1.3 collective-permute-start.14
  (12 other events, 12.7 us)

commit v3 on v2

--- a/solution.py
+++ b/solution.py
@@ -11,6 +11,7 @@
 LAG = 2
 MOST_CHUNKS = 20
 TILE = 16
+GROUP = 8
 VMEM = 48 << 20
 
 ANY = pl.BlockSpec(memory_space=pl.ANY)
@@ -26,6 +27,12 @@
 def largest(options, default):
     options = list(options)
     return max(options) if options else default
+
+
+def shares(total, parts):
+    parts = min(parts, total)
+    edges = [total * i // parts for i in range(parts + 1)]
+    return [(a, b - a) for a, b in zip(edges, edges[1:])]
 
 
 def cost(flops, bytes_accessed, transcendentals=0):
@@ -47,29 +54,23 @@
     seen = refs[3 : 3 + count_seen]
     rest = refs[3 + count_seen + count_after :]
     sends = rest[:2]
-    held, made, in_sem, out_sem = rest[2:]
+    held, sem = rest[2:]
 
     def fetch(j):
         way, k = divmod(j, 3)
         rows = pl.ds(places[way] * chunk, chunk)
-        return pltpu.make_async_copy(state[k].at[1, rows], held.at[j], in_sem.at[j])
-
-    def store(j):
-        way, k = divmod(j, 3)
-        return pltpu.make_async_copy(made.at[j], sends[way].at[k], out_sem.at[j])
+        return pltpu.make_async_copy(state[k].at[1, rows], held.at[j], sem.at[j])
 
     def convert():
         for j in range(6):
             fetch(j).start()
         for j in range(6):
+            way, k = divmod(j, 3)
             fetch(j).wait()
-            made[j] = held[j].astype(BF16)
-            store(j).start()
-        for j in range(6):
-            store(j).wait()
+            sends[way][k] = held[j].astype(BF16)
 
     def relay(way):
-        return pltpu.make_async_copy(seen[way], sends[way], out_sem.at[way])
+        return pltpu.make_async_copy(seen[way], sends[way], sem.at[way])
 
     if not seen:
         convert()
@@ -96,12 +97,10 @@
             count_after=len(after),
         ),
         in_specs=[SMEM] + [ANY] * (3 + len(seen) + len(after)),
-        out_specs=[ANY, ANY],
+        out_specs=[WHOLE, WHOLE],
         out_shape=[shape, shape],
         scratch_shapes=[
             pltpu.VMEM((6, chunk, width), F32),
-            pltpu.VMEM((6, chunk, width), BF16),
-            pltpu.SemaphoreType.DMA((6,)),
             pltpu.SemaphoreType.DMA((6,)),
         ],
         compiler_params=PARAMS,
@@ -231,25 +230,68 @@
     )(bit, value, *arrived, *after)
 
 
-def sum_scattered(value, axes, afters):
-    sizes = [lax.axis_size(axis) for axis in axes]
-    if any(size & (size - 1) for size in sizes):
-        return lax.psum_scatter(value, axes, scatter_dimension=0, tiled=True).astype(BF16)
-    arrived = ()
-    level = 0
-    for axis, size in zip(axes, sizes):
-        me = lax.axis_index(axis)
-        apart = size // 2
-        while apart:
-            bit = ((me // apart) % 2).astype(jnp.int32)[None]
-            after = afters[min(level, len(afters) - 1)]
-            value, sent = halve(bit, value, arrived, after, False)
+class ScatteredSum:
+    def __init__(self, value, axes):
+        sizes = [lax.axis_size(axis) for axis in axes]
+        self.value, self.arrived, self.levels = value, (), []
+        self.done = any(size & (size - 1) for size in sizes)
+        if self.done:
+            summed = lax.psum_scatter(value, axes, scatter_dimension=0, tiled=True)
+            self.value = summed.astype(BF16)
+            return
+        for axis, size in zip(axes, sizes):
+            apart = size // 2
+            while apart:
+                self.levels.append((axis, size, apart))
+                apart //= 2
+
+    def advance(self, after):
+        if self.done:
+            return ()
+        if self.levels:
+            axis, size, apart = self.levels.pop(0)
+            bit = ((lax.axis_index(axis) // apart) % 2).astype(jnp.int32)[None]
+            self.value, sent = halve(bit, self.value, self.arrived, after, False)
             route = [(i, i ^ apart) for i in range(size)]
-            arrived = (lax.ppermute(sent, axis, route),)
-            apart //= 2
-            level += 1
-    after = afters[min(level, len(afters) - 1)]
-    return halve(jnp.zeros((1,), jnp.int32), value, arrived, after, True)
+            self.arrived = (lax.ppermute(sent, axis, route),)
+        else:
+            bit = jnp.zeros((1,), jnp.int32)
+            self.value = halve(bit, self.value, self.arrived, after, True)
+            self.done = True
+        return (self.value,)
+
+
+def parcels_body(where, *refs, count, n, features):
+    both, hidden = refs[0], refs[1 : 1 + count]
+    parcels = refs[-n:]
+    units = sum(part.shape[1] for part in hidden)
+    width = parcels[0].shape[1] - units
+    keep = where[1] == 0
+    for far in range(n):
+        to = lax.rem(where[0] + far, n)
+        first = 0
+        for part in hidden:
+            here = pl.ds(first, part.shape[1])
+            parcels[far][:, here] = jnp.where(keep, part[...], jnp.zeros_like(part))
+            first += part.shape[1]
+        slab = pl.ds(pl.multiple_of(features + to * width, 128), width)
+        parcels[far][:, pl.ds(units, width)] = both[:, slab]
+
+
+def make_parcels(where, both, hidden, after, n, width):
+    rows = both.shape[0]
+    features = both.shape[1] // 2
+    length = sum(part.shape[1] for part in hidden) + width
+    shape = jax.ShapeDtypeStruct((rows, length), BF16)
+    return pl.pallas_call(
+        functools.partial(parcels_body, count=len(hidden), n=n, features=features),
+        in_specs=[SMEM] + [WHOLE] * (1 + len(hidden)) + [ANY] * len(after),
+        out_specs=[WHOLE] * n,
+        out_shape=[shape] * n,
+        compiler_params=PARAMS,
+        cost_estimate=cost(0, 4 * n * rows * length),
+        name="parcels",
+    )(where, both, *hidden, *after)
 
 
 def collect_body(*refs, count, units):
@@ -278,43 +320,57 @@
     )(*parcels, *after)
 
 
-def update_body(info, hid_ref, out_ref, m_ref, a_ref, b_ref, *refs, healthy):
-    m_new, a_new, b_new = refs[-3:]
+def update_body(info, hid_ref, out_ref, *refs, healthy, block, first, count, unread):
+    state, news = refs[:3], refs[3 + unread : 6 + unread]
+    total = refs[6 + unread]
+    width = out_ref.shape[1]
+
+    def step(hid, m_ref, a_ref, b_ref, m_new, a_new, b_new):
+        total[...] = jnp.dot(hid[...], out_ref[...], preferred_element_type=F32)
+
+        @pl.loop(0, block // GROUP)
+        def _(i):
+            here = pl.ds(pl.multiple_of(i * GROUP, GROUP), GROUP)
+            m_new[here], a_new[here], b_new[here] = updated(
+                m_ref[0, here], a_ref[0, here], b_ref[0, here], total[here], healthy
+            )
+
+    old = pl.BlockSpec((1, block, width), lambda i: (0, first + i, 0))
+    new = pl.BlockSpec((block, width), lambda i: (first + i, 0))
 
     @pl.when(info[0] == 0)
     def _():
-        total = jnp.dot(hid_ref[...], out_ref[...], preferred_element_type=F32)
-        m_new[...], a_new[...], b_new[...] = updated(
-            m_ref[0], a_ref[0], b_ref[0], total, healthy
-        )
+        pltpu.emit_pipeline(
+            step,
+            grid=(count,),
+            in_specs=[
+                pl.BlockSpec((block, hid_ref.shape[1]), lambda i: (first + i, 0)),
+                old,
+                old,
+                old,
+            ],
+            out_specs=[new] * 3,
+        )(hid_ref, *state, *news)
 
 
 def update(info, hidden_t, outs, state, news, after, healthy, block, first, count):
     _, rows, width = state[0].shape
     depth = hidden_t.shape[1]
-
-    def at(i, info):
-        return jnp.where(info[0] == 1, first, first + i)
-
-    spec = pl.BlockSpec((1, block, width), lambda i, info: (0, at(i, info), 0))
-    out = pl.BlockSpec((block, width), lambda i, info: (at(i, info), 0))
     shape = jax.ShapeDtypeStruct((rows, width), F32)
-    return pl.pallas_call(
-        functools.partial(update_body, healthy=healthy),
-        grid_spec=pltpu.PrefetchScalarGridSpec(
-            num_scalar_prefetch=1,
-            grid=(count,),
-            in_specs=[
-                pl.BlockSpec((block, depth), lambda i, info: (at(i, info), 0)),
-                pl.BlockSpec((depth, width), lambda i, info: (0, 0)),
-                spec,
-                spec,
-                spec,
-            ]
-            + [ANY] * (len(news) + len(after)),
-            out_specs=[out] * 3,
+    unread = len(news) + len(after)
+    return pl.pallas_call(
+        functools.partial(
+            update_body,
+            healthy=healthy,
+            block=block,
+            first=first,
+            count=count,
+            unread=unread,
         ),
+        in_specs=[SMEM, ANY, WHOLE] + [ANY] * (3 + unread),
+        out_specs=[ANY] * 3,
         out_shape=[shape] * 3,
+        scratch_shapes=[pltpu.VMEM((block, width), F32)],
         input_output_aliases={6 + k: k for k in range(len(news))},
         compiler_params=PARAMS,
         cost_estimate=cost(
@@ -331,9 +387,8 @@
     got = refs[:count]
     rest = refs[count + 3 + count_after :]
     news = rest[:3]
-    held, made, in_sem, out_sem = rest[3:]
+    held, made, total, in_sem, out_sem = rest[3:]
     chunk = held.shape[2]
-    part = largest((p for p in (16, 32, 48) if chunk % p == 0), chunk)
     ahead = info[1]
     lag_of = {True: LAG * (ahead - 1), False: LAG * (n - ahead - 1)}
 
@@ -377,14 +432,14 @@
             def _(j=j, slot=slot):
                 first = first_row(j)
 
-                @pl.loop(0, chunk // part)
+                units = hid_ref[pl.ds(first, chunk)]
+                total[...] = jnp.dot(units, out_ref[...], preferred_element_type=F32)
+
+                @pl.loop(0, chunk // TILE)
                 def _(i):
-                    base = pl.multiple_of(i * part, part)
-                    here = pl.ds(base, part)
-                    units = hid_ref[pl.ds(pl.multiple_of(first + base, TILE), part)]
-                    total = jnp.dot(units, out_ref[...], preferred_element_type=F32)
+                    here = pl.ds(pl.multiple_of(i * TILE, TILE), TILE)
                     old = [held[slot, k, here].astype(F32) for k in range(3)]
-                    new = updated(*old, total, n - 1.0)
+                    new = updated(*old, total[here], n - 1.0)
                     for k in range(3):
                         made[slot, k, here] = new[k]
 
@@ -410,6 +465,7 @@
         scratch_shapes=[
             pltpu.VMEM((2, 3, chunk, width), BF16),
             pltpu.VMEM((2, 3, chunk, width), F32),
+            pltpu.VMEM((chunk, width), F32),
             pltpu.SemaphoreType.DMA((2,)),
             pltpu.SemaphoreType.DMA((2, 3)),
         ],
@@ -468,62 +524,56 @@
     sent = send(both)
 
     tile = 128 if units % 128 == 0 else units
-    tiles = units // tile
-    pieces = largest((p for p in (1, 3) if tiles % p == 0), 1)
     hidden, d_rows = [], None
-    for piece in range(pieces):
-        count = tiles // pieces
-        part, d_rows = layer(
-            both, w_gate, w_up, w_down, d_rows, sent, tile, piece * count, count
-        )
+    for first, count in shares(units // tile, 4):
+        part, d_rows = layer(both, w_gate, w_up, w_down, d_rows, sent, tile, first, count)
         hidden.append(part)
         sent = send(d_rows)
-    hidden = jnp.concatenate(hidden, axis=1)
-
-    kept = jnp.where(me == failed_id, jnp.zeros_like(hidden), hidden)
-
-    def parcel(to):
-        slab = lax.dynamic_slice_in_dim(both, features + to * width, width, 1)
-        return jnp.concatenate([kept, slab], axis=1)
-
-    parcels = [parcel(me)]
+
+    where = jnp.stack([me, info[0]])
+    parcels = make_parcels(where, both, hidden, sent, n, width)
+    arrived = [parcels[0]]
     for far in range(1, n):
         route = [(i, (i + far) % n) for i in range(n)]
-        parcels.append(lax.ppermute(parcel((me + far) % n), "replica", route))
-
-    afters = [sent]
-    for _ in range(3):
-        afters.append(send(*afters[-1]))
-    d_tokens = sum_scattered(d_rows, ("fsdp", "tensor"), afters)
-
-    hidden_t, outs = collect(parcels, units, afters[-1])
+        arrived.append(lax.ppermute(parcels[far], "replica", route))
+    cotangents = ScatteredSum(d_rows, ("fsdp", "tensor"))
+    sent = send(parcels[0], *cotangents.advance((parcels[0],)))
+    sent = send(*cotangents.advance(sent))
+
+    hidden_t, outs = collect(arrived, units, sent)
+    sent = (hidden_t,)
     block = largest((b for b in range(TILE, 193, TILE) if rows % b == 0), rows)
-    blocks = rows // block
-    sent = (hidden_t,)
+    turns = shares(rows // block, 3)
     news = ()
-    turns = 2 if blocks % 2 == 0 else 1
-    for turn in range(turns):
-        count = blocks // turns
-        news = update(
-            info, hidden_t, outs, state, news, sent, n - 1.0, block, turn * count, count
+    patched = 0
+
+    def update_next(after):
+        first, count = turns.pop(0)
+        return update(
+            info, hidden_t, outs, state, news, after, n - 1.0, block, first, count
         )
-        sent = send(news[0])
-
-    patched = 0
-
-    def patch_to(step, news, after):
+
+    def patch_to(step, after):
         nonlocal patched
         arrivals = [(s, way) for s in range(patched, step) for way in (True, False)]
+        if not arrivals:
+            return news
         blocks = [b for s in range(patched, step) for b in got[s]]
         patched = step
         return patch(info, hidden_t, outs, blocks, arrivals, news, after, chunks, n)
 
-    news = patch_to(len(got) - 2, news, sent)
     while len(got) < steps:
-        sent = send(news[0])
-    news = patch_to(steps - 1, news, sent)
-    news = patch_to(steps, news, ())
-    return (d_tokens[None], *news)
+        if len(turns) > 1:
+            news = update_next(sent)
+            news = patch_to(len(got) // 2 if patched == 0 else len(got) - 2, ())
+        sent = send(*news[:1], *cotangents.advance(sent))
+    while turns:
+        news = update_next(sent)
+    news = patch_to(steps - 1, sent)
+    news = patch_to(steps, ())
+    while not cotangents.done:
+        cotangents.advance(sent)
+    return (cotangents.value[None], *news)
 
 
 def solution(mesh):

time: 207 us -> 177 us (0.86); the launches traced: 207 us -> 175 us
  starting transfers between devices: 57.2 us -> 31 us
  Pallas kernels: 95.8 us -> 88.5 us
  waiting for transfers between devices: 28.7 us -> 35.2 us
  local copies, waits for them, and re-layouts: 6.47 us -> 2.07 us
    pallas_call x3 -> x4, Pallas kernels: 25.4 us -> 2.49 us  [patch(): pl.pallas_call(functools.partial(patch_body, arrivals=arrivals, chunks=ch...]
    pallas_call x2 -> x4, Pallas kernels: 7.16 us -> 29.3 us  [the longest x3 28.1 us: update(): pl.pallas_call(functools.partial(update_body, healthy=healthy, block=bloc...]
    ppermute x12, starting transfers between devices: 30.3 us -> 10.7 us  [send(): lax.ppermute(sends[-1][1], 'replica', backward)]
    pallas_call x12, Pallas kernels: 33.5 us -> 25.9 us  [pack(): pl.pallas_call(functools.partial(pack_body, places=places, chunk=chunk, c...]
    ppermute x12, starting transfers between devices: 22.6 us -> 15.1 us  [send(): lax.ppermute(sends[-1][0], 'replica', forward)]
    ppermute x12, waiting for transfers between devices: 9.28 us -> 14.9 us  [send(): lax.ppermute(sends[-1][1], 'replica', backward)]
    unnamed x61 -> x41, local copies, waits for them, and re-layouts: 5.86 us -> 1.49 us
    ppermute x12, waiting for transfers between devices: 0.03 us -> 2.96 us  [send(): lax.ppermute(sends[-1][0], 'replica', forward)]
  transfers between devices with their start and end apart: 30 -> 30, of which waited for: 7 -> 8; matrix products, arithmetic and copies ran while one was open for 1% -> 0% of each run, Pallas kernels for 43% -> 49%
where the time goes in v3:
time: 177 us; the launch traced here: 175 us
  Pallas kernels  88.5 us (50%)
  waiting for transfers between devices  35.2 us (20%)
  starting transfers between devices  31 us (18%)
  blocking collectives  14.9 us (8%)
  between operations  3.11 us (2%)
  local copies, waits for them, and re-layouts  2.07 us (1%)
    pallas_call x4, Pallas kernels, layer(): pl.pallas_call(functools.partial(layer_body, resumed=resumed), grid=(coun...  30 us
    pallas_call x3, Pallas kernels, update(): pl.pallas_call(functools.partial(update_body, healthy=healthy, block=bloc...  28.1 us
    pallas_call x12, Pallas kernels, pack(): pl.pallas_call(functools.partial(pack_body, places=places, chunk=chunk, c...  25.9 us
    ppermute x12, starting transfers between devices, send(): lax.ppermute(sends[-1][0], 'replica', forward)  15.1 us
    ppermute x12, waiting for transfers between devices, send(): lax.ppermute(sends[-1][1], 'replica', backward)  14.9 us
    all_gather x1, blocking collectives, per_device(): both = lax.all_gather(both, ('fsdp', 'tensor'), axis=0, tiled=True)  14.9 us
    ppermute x3, waiting for transfers between devices, per_device(): arrived.append(lax.ppermute(parcels[far], 'replica', route))  12.7 us
    ppermute x12, starting transfers between devices, send(): lax.ppermute(sends[-1][1], 'replica', backward)  10.7 us
  transfers between devices with their start and end apart: 30, of which 8 were waited for; matrix products, arithmetic and copies ran while one was open for 0% of the time, Pallas kernels for 49%

profile of v3, /device:TPU:0, one launch (start us, length us, event | category | flops | bytes accessed | tf_op | source)
XLA Modules:
  0.0 175.1 jit_solution(204468037504452413)
XLA Ops:
  1.3 2.5 %pack.12 = (bf16[3,96,1024]{2,1,0:T(8,128)(2,1)S(1)}, bf16[3,96,1024]{2,1,0:T(8,128)(2,1)}) custom-call(s32[1]{0:T(128)} %bitcast.6.flag, f32[2,1920,1024]{2,1,0:T(8,128)} %refs_0_.29, f32[2,1920,1024]{2,1,0:T(8,128)} %refs_1_.29, f32[2,1920,1024]{2,1,0:T(8,128)} %refs_2_.29), custom_call_target="tpu_custom_call" | custom-call | bytes 3538944 | tf_op jit(solution)/shard_map/pack/pallas_call | solution.py:91
  3.8 3.0 %collective-permute-start.1 = (bf16[3,96,1024]{2,1,0:T(8,128)(2,1)}, bf16[3,96,1024]{2,1,0:T(8,128)(2,1)S(1)}, u32[]{:S(2)}, u32[]{:S(2)}) collective-permute-start(bf16[3,96,1024]{2,1,0:T(8,128)(2,1)} %get-tuple-element.71), channel_id=1, source_target_pairs={{8,0},{24,8},{16,24},{0,16},{9,1},{25,9},{17,25},{1,17},{10,2},{26... | collective-permute-start | bytes 1769480 | tf_op jit(solution)/shard_map/ppermute | solution.py:515
  6.9 2.6 %pack.13 = (bf16[3,96,1024]{2,1,0:T(8,128)(2,1)}, bf16[3,96,1024]{2,1,0:T(8,128)(2,1)}) custom-call(s32[1]{0:T(128)} %bitcast.6.flag, f32[2,1920,1024]{2,1,0:T(8,128)} %refs_0_.29, f32[2,1920,1024]{2,1,0:T(8,128)} %refs_1_.29, f32[2,1920,1024]{2,1,0:T(8,128)} %refs_2_.29, bf16[3,96,1024]{2,1,0:T(8,128)(2,1)S(1)} %get-tuple-element.69.refs_3_), custom_call_target="tpu_custom_call" | custom-call | bytes 3538944 | tf_op jit(solution)/shard_map/pack/pallas_call | solution.py:91
  9.5 2.0 %collective-permute-start.3 = (bf16[3,96,1024]{2,1,0:T(8,128)(2,1)}, bf16[3,96,1024]{2,1,0:T(8,128)(2,1)S(1)}, u32[]{:S(2)}, u32[]{:S(2)}) collective-permute-start(bf16[3,96,1024]{2,1,0:T(8,128)(2,1)} %get-tuple-element.74), channel_id=1, source_target_pairs={{8,0},{24,8},{16,24},{0,16},{9,1},{25,9},{17,25},{1,17},{10,2},{26... | collective-permute-start | bytes 1769480 | tf_op jit(solution)/shard_map/ppermute | solution.py:515
  11.6 14.9 %all-gather = bf16[8,2,8192]{2,1,0:T(2,128)(2,1)S(1)} all-gather(bf16[1,2,8192]{2,1,0:T(2,128)(2,1)S(1)} %bitcast.18), channel_id=1, replica_groups=mesh['replica'=4,'fsdp'=4,'tensor'=2] {'fsdp','tensor'}, dimensions={0}, use_global_device_ids=true | all-gather | bytes 294912 | tf_op jit(solution)/shard_map/all_gather | solution.py:523
  26.6 1.7 pack.14
  28.5 1.9 %collective-permute-start.4 = (bf16[3,96,1024]{2,1,0:T(8,128)(2,1)S(1)}, bf16[3,96,1024]{2,1,0:T(8,128)(2,1)S(1)}, u32[]{:S(2)}, u32[]{:S(2)}) collective-permute-start(bf16[3,96,1024]{2,1,0:T(8,128)(2,1)S(1)} %get-tuple-element.72.refs_0_), channel_id=1, source_target_pairs={{0,8},{8,24},{24,16},{16,0},{1,9},{9,25},{25,17},{17,1},{2,10},{10... | collective-permute-start | bytes 1769480 | tf_op jit(solution)/shard_map/ppermute | solution.py:514
  30.4 6.4 %layer.4 = (bf16[16,384]{1,0:T(8,128)(2,1)S(1)}, f32[16,4096]{1,0:T(8,128)S(1)}) custom-call(bf16[16,8192]{1,0:T(8,128)(2,1)S(1)} %reshape.12.refs_5_.both.refs_0_, bf16[4096,1920]{1,0:T(8,128)(2,1)} %gate_ref.7, bf16[4096,1920]{1,0:T(8,128)(2,1)} %up_ref.7, bf16[1920,4096]{1,0:T(8,128)(2,1)} %down_ref.7, bf16[3,96,1024]{2,1,0:T(8,128)(2,1)S(1)} %get-tuple-element.72.refs_0_), custom_call_target="tpu_custom_call" | custom-call | flops 251658240 | bytes 9437184 | tf_op jit(solution)/shard_map/layer/pallas_call | solution.py:175
  36.8 1.7 pack.15
  38.5 2.0 %collective-permute-start.6 = (bf16[3,96,1024]{2,1,0:T(8,128)(2,1)S(1)}, bf16[3,96,1024]{2,1,0:T(8,128)(2,1)S(1)}, u32[]{:S(2)}, u32[]{:S(2)}) collective-permute-start(bf16[3,96,1024]{2,1,0:T(8,128)(2,1)S(1)} %get-tuple-element.75.refs_1_), channel_id=1, source_target_pairs={{0,8},{8,24},{24,16},{16,0},{1,9},{9,25},{25,17},{17,1},{2,10},{10... | collective-permute-start | bytes 1769480 | tf_op jit(solution)/shard_map/ppermute | solution.py:514
  40.5 7.9 %layer.5 = (bf16[16,512]{1,0:T(8,128)(2,1)S(1)}, f32[16,4096]{1,0:T(8,128)S(1)}) custom-call(bf16[16,8192]{1,0:T(8,128)(2,1)S(1)} %reshape.12.refs_5_.both.refs_0_, bf16[4096,1920]{1,0:T(8,128)(2,1)} %gate_ref.7, bf16[4096,1920]{1,0:T(8,128)(2,1)} %up_ref.7, bf16[1920,4096]{1,0:T(8,128)(2,1)} %down_ref.7, f32[16,4096]{1,0:T(8,128)S(1)} %get-tuple-element.73.refs_5_.refs_0_, ...), custom_call_target="tpu_custom_call" | custom-call | flops 335544320 | bytes 12582912 | tf_op jit(solution)/shard_map/layer/pallas_call | solution.py:175
  48.4 1.9 %pack.16 = (bf16[3,96,1024]{2,1,0:T(8,128)(2,1)S(1)}, bf16[3,96,1024]{2,1,0:T(8,128)(2,1)S(1)}) custom-call(s32[1]{0:T(128)} %bitcast.6.flag, f32[2,1920,1024]{2,1,0:T(8,128)} %refs_0_.29, f32[2,1920,1024]{2,1,0:T(8,128)} %refs_1_.29, f32[2,1920,1024]{2,1,0:T(8,128)} %refs_2_.29, bf16[3,96,1024]{2,1,0:T(8,128)(2,1)S(1)} %collective-permute-done.4.refs_3_.refs_4_, ...), custom_call_target="tpu_custom_call" | custom-call | bytes 3538944 | tf_op jit(solution)/shard_map/pack/pallas_call | solution.py:91
  50.7 1.8 %collective-permute-start.8 = (bf16[3,96,1024]{2,1,0:T(8,128)(2,1)S(1)}, bf16[3,96,1024]{2,1,0:T(8,128)(2,1)S(1)}, u32[]{:S(2)}, u32[]{:S(2)}) collective-permute-start(bf16[3,96,1024]{2,1,0:T(8,128)(2,1)S(1)} %get-tuple-element.78.refs_1_), channel_id=1, source_target_pairs={{0,8},{8,24},{24,16},{16,0},{1,9},{9,25},{25,17},{17,1},{2,10},{10... | collective-permute-start | bytes 1769480 | tf_op jit(solution)/shard_map/ppermute | solution.py:514
  52.4 7.9 %layer.6 = (bf16[16,512]{1,0:T(8,128)(2,1)S(1)}, f32[16,4096]{1,0:T(8,128)S(1)}) custom-call(bf16[16,8192]{1,0:T(8,128)(2,1)S(1)} %reshape.12.refs_5_.both.refs_0_, bf16[4096,1920]{1,0:T(8,128)(2,1)} %gate_ref.7, bf16[4096,1920]{1,0:T(8,128)(2,1)} %up_ref.7, bf16[1920,4096]{1,0:T(8,128)(2,1)} %down_ref.7, f32[16,4096]{1,0:T(8,128)S(1)} %get-tuple-element.76.refs_5_.refs_0_, ...), custom_call_target="tpu_custom_call" | custom-call | flops 335544320 | bytes 12582912 | tf_op jit(solution)/shard_map/layer/pallas_call | solution.py:175
  60.3 0.7 collective-permute-done.6.refs_3_.refs_6_
  61.0 2.9 %pack.17 = (bf16[3,96,1024]{2,1,0:T(8,128)(2,1)}, bf16[3,96,1024]{2,1,0:T(8,128)(2,1)}) custom-call(s32[1]{0:T(128)} %bitcast.6.flag, f32[2,1920,1024]{2,1,0:T(8,128)} %refs_0_.29, f32[2,1920,1024]{2,1,0:T(8,128)} %refs_1_.29, f32[2,1920,1024]{2,1,0:T(8,128)} %refs_2_.29, bf16[3,96,1024]{2,1,0:T(8,128)(2,1)S(1)} %collective-permute-done.6.refs_3_.refs_6_, ...), custom_call_target="tpu_custom_call" | custom-call | bytes 3538944 | tf_op jit(solution)/shard_map/pack/pallas_call | solution.py:91
  64.0 2.0 %collective-permute-start.11 = (bf16[3,96,1024]{2,1,0:T(8,128)(2,1)}, bf16[3,96,1024]{2,1,0:T(8,128)(2,1)}, u32[]{:S(2)}, u32[]{:S(2)}) collective-permute-start(bf16[3,96,1024]{2,1,0:T(8,128)(2,1)} %get-tuple-element.81.refs_1_), channel_id=1, source_target_pairs={{0,8},{8,24},{24,16},{16,0},{1,9},{9,25},{25,17},{17,1},{2,10},{10... | collective-permute-start | bytes 1769480 | tf_op jit(solution)/shard_map/ppermute | solution.py:514
  66.0 7.9 %layer.7 = (bf16[16,512]{1,0:T(8,128)(2,1)S(1)}, f32[16,4096]{1,0:T(8,128)S(1)}) custom-call(bf16[16,8192]{1,0:T(8,128)(2,1)S(1)} %reshape.12.refs_5_.both.refs_0_, bf16[4096,1920]{1,0:T(8,128)(2,1)} %gate_ref.7, bf16[4096,1920]{1,0:T(8,128)(2,1)} %up_ref.7, bf16[1920,4096]{1,0:T(8,128)(2,1)} %down_ref.7, f32[16,4096]{1,0:T(8,128)S(1)} %get-tuple-element.79.refs_5_.refs_0_, ...), custom_call_target="tpu_custom_call" | custom-call | flops 335544320 | bytes 12582912 | tf_op jit(solution)/shard_map/layer/pallas_call | solution.py:175
  73.9 3.1 %pack.18 = (bf16[3,96,1024]{2,1,0:T(8,128)(2,1)}, bf16[3,96,1024]{2,1,0:T(8,128)(2,1)}) custom-call(s32[1]{0:T(128)} %bitcast.6.flag, f32[2,1920,1024]{2,1,0:T(8,128)} %refs_0_.29, f32[2,1920,1024]{2,1,0:T(8,128)} %refs_1_.29, f32[2,1920,1024]{2,1,0:T(8,128)} %refs_2_.29, bf16[3,96,1024]{2,1,0:T(8,128)(2,1)S(1)} %collective-permute-done.8.refs_3_.refs_0_, ...), custom_call_target="tpu_custom_call" | custom-call | bytes 3538944 | tf_op jit(solution)/shard_map/pack/pallas_call | solution.py:91
  77.1 2.0 %collective-permute-start.17 = (bf16[3,96,1024]{2,1,0:T(8,128)(2,1)}, bf16[3,96,1024]{2,1,0:T(8,128)(2,1)}, u32[]{:S(2)}, u32[]{:S(2)}) collective-permute-start(bf16[3,96,1024]{2,1,0:T(8,128)(2,1)} %get-tuple-element.88.refs_5_), channel_id=1, source_target_pairs={{0,8},{8,24},{24,16},{16,0},{1,9},{9,25},{25,17},{17,1},{2,10},{10... | collective-permute-start | bytes 1769480 | tf_op jit(solution)/shard_map/ppermute | solution.py:514
  79.2 1.2 parcels.1
  81.0 3.4 %collective-permute-done.12.refs_4_.refs_3_ = bf16[3,96,1024]{2,1,0:T(8,128)(2,1)} collective-permute-done((bf16[3,96,1024]{2,1,0:T(8,128)(2,1)}, bf16[3,96,1024]{2,1,0:T(8,128)(2,1)}, u32[]{:S(2)}, u32[]{:S(2)}) %collective-permute-start.12) | collective-permute-done | bytes 589856 | tf_op jit(solution)/shard_map/ppermute | solution.py:515
  84.4 1.9 %collective-permute-done.11.refs_3_.refs_2_ = bf16[3,96,1024]{2,1,0:T(8,128)(2,1)} collective-permute-done((bf16[3,96,1024]{2,1,0:T(8,128)(2,1)}, bf16[3,96,1024]{2,1,0:T(8,128)(2,1)}, u32[]{:S(2)}, u32[]{:S(2)}) %collective-permute-start.11) | collective-permute-done | bytes 589856 | tf_op jit(solution)/shard_map/ppermute | solution.py:514
  86.4 2.8 %pack.19 = (bf16[3,96,1024]{2,1,0:T(8,128)(2,1)}, bf16[3,96,1024]{2,1,0:T(8,128)(2,1)}) custom-call(s32[1]{0:T(128)} %bitcast.6.flag, f32[2,1920,1024]{2,1,0:T(8,128)} %refs_0_.29, f32[2,1920,1024]{2,1,0:T(8,128)} %refs_1_.29, f32[2,1920,1024]{2,1,0:T(8,128)} %refs_2_.29, bf16[3,96,1024]{2,1,0:T(8,128)(2,1)} %collective-permute-done.11.refs_3_.refs_2_, ...), custom_call_target="tpu_custom_call" | custom-call | bytes 3538944 | tf_op jit(solution)/shard_map/pack/pallas_call | solution.py:91
  89.2 1.2 collective-permute-start.21
  90.4 0.9 collective-permute-start.20
  91.3 2.6 %collective-permute-start.10 = (f32[8,4096]{1,0:T(8,128)S(1)}, f32[8,4096]{1,0:T(8,128)S(1)}, u32[]{:S(2)}, u32[]{:S(2)}) collective-permute-start(f32[8,4096]{1,0:T(8,128)S(1)} %get-tuple-element.91), channel_id=1, source_target_pairs={{0,4},{2,6},{4,0},{6,2},{1,5},{3,7},{5,1},{7,3},{8,12},{10,14},{12... | collective-permute-start | bytes 393224 | tf_op jit(solution)/shard_map/ppermute | solution.py:256
  93.9 4.7 %collective-permute-done.10.refs_1_ = f32[8,4096]{1,0:T(8,128)S(1)} collective-permute-done((f32[8,4096]{1,0:T(8,128)S(1)}, f32[8,4096]{1,0:T(8,128)S(1)}, u32[]{:S(2)}, u32[]{:S(2)}) %collective-permute-start.10) | collective-permute-done | bytes 131104 | tf_op jit(solution)/shard_map/ppermute | solution.py:256
  100.5 12.5 %collective-permute-done.14.refs_1_ = bf16[16,2944]{1,0:T(8,128)(2,1)S(1)} collective-permute-done((bf16[16,2944]{1,0:T(8,128)(2,1)}, bf16[16,2944]{1,0:T(8,128)(2,1)S(1)}, u32[]{:S(2)}, u32[]{:S(2)}) %collective-permute-start.14) | collective-permute-done | bytes 94240 | tf_op jit(solution)/shard_map/ppermute | solution.py:538
  113.0 0.9 collective-permute-start.16
  113.9 1.7 collective-permute-start.13
  115.7 1.7 pack.20
  117.6 1.0 collective-permute-start.27
  118.6 1.0 collective-permute-start.26
  119.9 9.0 %update.3 = (f32[1920,1024]{1,0:T(8,128)}, f32[1920,1024]{1,0:T(8,128)}, f32[1920,1024]{1,0:T(8,128)}) custom-call(s32[2]{0:T(128)S(1)} %pad_add_fusion.1.info, bf16[1920,64]{1,0:T(8,128)(2,1)S(1)} %get-tuple-element.101.refs_2_.hid_ref.refs_3_, bf16[64,1024]{1,0:T(8,128)(2,1)S(1)} %get-tuple-element.105.out_ref, f32[2,1920,1024]{2,1,0:T(8,128)} %refs_0_.29, ...), custom_call_target="tpu_custom_call" | custom-call | flops 75497472 | bytes 14155776 | tf_op jit(solution)/shard_map/update/pallas_call | solution.py:361
  128.9 0.6 patch.4
  129.6 1.7 pack.21
  131.3 0.7 collective-permute-start.23
  132.0 1.4 collective-permute-start.22
  133.4 9.0 %update.4 = (f32[1920,1024]{1,0:T(8,128)}, f32[1920,1024]{1,0:T(8,128)}, f32[1920,1024]{1,0:T(8,128)}) custom-call(s32[2]{0:T(128)S(1)} %pad_add_fusion.1.info, bf16[1920,64]{1,0:T(8,128)(2,1)S(1)} %get-tuple-element.101.refs_2_.hid_ref.refs_3_, ...), custom_call_target="tpu_custom_call", output_to_operand_aliasing={{0}: (6, {}), {1}: (7, {}), {2}: (8, {})} | custom-call | flops 75497472 | bytes 14155776 | tf_op jit(solution)/shard_map/update/pallas_call | solution.py:361
  143.0 0.6 halve.7.refs_6_
  143.7 0.7 copy-done.12
  144.4 1.7 pack.23
  146.1 2.0 %collective-permute-start.29 = (bf16[3,96,1024]{2,1,0:T(8,128)(2,1)S(1)}, bf16[3,96,1024]{2,1,0:T(8,128)(2,1)S(1)}, u32[]{:S(2)}, u32[]{:S(2)}) collective-permute-start(bf16[3,96,1024]{2,1,0:T(8,128)(2,1)S(1)} %get-tuple-element.122), channel_id=1, source_target_pairs={{8,0},{24,8},{16,24},{0,16},{9,1},{25,9},{17,25},{1,17},{10,2},{26... | collective-permute-start | bytes 1769480 | tf_op jit(solution)/shard_map/ppermute | solution.py:515
  148.1 1.7 pack.22
  149.9 2.0 %collective-permute-start.24 = (bf16[3,96,1024]{2,1,0:T(8,128)(2,1)S(1)}, bf16[3,96,1024]{2,1,0:T(8,128)(2,1)S(1)}, u32[]{:S(2)}, u32[]{:S(2)}) collective-permute-start(bf16[3,96,1024]{2,1,0:T(8,128)(2,1)S(1)} %get-tuple-element.118.refs_6_.refs_9_), channel_id=1, source_target_pairs={{0,8},{8,24},{24,16},{16,0},{1,9},{9,25},{25,17},{17,1},{2,10},{10... | collective-permute-start | bytes 1769480 | tf_op jit(solution)/shard_map/ppermute | solution.py:514
  151.9 10.1 %update.5 = (f32[1920,1024]{1,0:T(8,128)}, f32[1920,1024]{1,0:T(8,128)}, f32[1920,1024]{1,0:T(8,128)}) custom-call(s32[2]{0:T(128)S(1)} %pad_add_fusion.1.info, bf16[1920,64]{1,0:T(8,128)(2,1)S(1)} %get-tuple-element.101.refs_2_.hid_ref.refs_3_, ...), custom_call_target="tpu_custom_call", output_to_operand_aliasing={{0}: (6, {}), {1}: (7, {}), {2}: (8, {})} | custom-call | flops 100663296 | bytes 18874368 | tf_op jit(solution)/shard_map/update/pallas_call | solution.py:361
  163.0 11.5 %collective-permute-done.25.refs_1_ = bf16[3,96,1024]{2,1,0:T(8,128)(2,1)S(1)} collective-permute-done((bf16[3,96,1024]{2,1,0:T(8,128)(2,1)S(1)}, bf16[3,96,1024]{2,1,0:T(8,128)(2,1)S(1)}, u32[]{:S(2)}, u32[]{:S(2)}) %collective-permute-start.25) | collective-permute-done | bytes 589856 | tf_op jit(solution)/shard_map/ppermute | solution.py:515
  (87 shorter events, 5.2 us)
Async XLA Ops:
  3.8 22.8 %collective-permute-start.1 = (bf16[3,96,1024]{2,1,0:T(8,128)(2,1)}, bf16[3,96,1024]{2,1,0:T(8,128)(2,1)S(1)}, u32[]{:S(2)}, u32[]{:S(2)}) collective-permute-start(bf16[3,96,1024]{2,1,0:T(8,128)(2,1)} %get-tuple-element.71), channel_id=1, source_target_pairs={{8,0},{24,8},{16,24},{0,16},{9,1},{25,9},{17,25},{1,17},{10,2},{26... | collective-permute-start | bytes 1769480 | tf_op jit(solution)/shard_map/ppermute | solution.py:515
  6.8 4.8 %copy-start.13 = (bf16[1,2,4096]{2,1,0:T(2,128)(2,1)S(1)}, bf16[1,2,4096]{2,1,0:T(2,128)(2,1)}, u32[]{:S(2)}) copy-start(bf16[1,2,4096]{2,1,0:T(2,128)(2,1)} %param.10) | copy-start | bytes 49156
  6.8 4.8 %copy-start.14 = (bf16[1,2,4096]{2,1,0:T(2,128)(2,1)S(1)}, bf16[1,2,4096]{2,1,0:T(2,128)(2,1)}, u32[]{:S(2)}) copy-start(bf16[1,2,4096]{2,1,0:T(2,128)(2,1)} %param.11) | copy-start | bytes 49156
  6.8 19.8 %collective-permute-start = (bf16[3,96,1024]{2,1,0:T(8,128)(2,1)S(1)}, bf16[3,96,1024]{2,1,0:T(8,128)(2,1)S(1)}, u32[]{:S(2)}, u32[]{:S(2)}) collective-permute-start(bf16[3,96,1024]{2,1,0:T(8,128)(2,1)S(1)} %get-tuple-element.69.refs_3_), channel_id=1, source_target_pairs={{0,8},{8,24},{24,16},{16,0},{1,9},{9,25},{25,17},{17,1},{2,10},{10... | collective-permute-start | bytes 1769480 | tf_op jit(solution)/shard_map/ppermute | solution.py:514
  9.5 27.2 %collective-permute-start.3 = (bf16[3,96,1024]{2,1,0:T(8,128)(2,1)}, bf16[3,96,1024]{2,1,0:T(8,128)(2,1)S(1)}, u32[]{:S(2)}, u32[]{:S(2)}) collective-permute-start(bf16[3,96,1024]{2,1,0:T(8,128)(2,1)} %get-tuple-element.74), channel_id=1, source_target_pairs={{8,0},{24,8},{16,24},{0,16},{9,1},{25,9},{17,25},{1,17},{10,2},{26... | collective-permute-start | bytes 1769480 | tf_op jit(solution)/shard_map/ppermute | solution.py:515
  11.5 25.2 %collective-permute-start.2 = (bf16[3,96,1024]{2,1,0:T(8,128)(2,1)}, bf16[3,96,1024]{2,1,0:T(8,128)(2,1)S(1)}, u32[]{:S(2)}, u32[]{:S(2)}) collective-permute-start(bf16[3,96,1024]{2,1,0:T(8,128)(2,1)} %get-tuple-element.70.refs_2_), channel_id=1, source_target_pairs={{0,8},{8,24},{24,16},{16,0},{1,9},{9,25},{25,17},{17,1},{2,10},{10... | collective-permute-start | bytes 1769480 | tf_op jit(solution)/shard_map/ppermute | solution.py:514
  28.3 20.1 %collective-permute-start.5 = (bf16[3,96,1024]{2,1,0:T(8,128)(2,1)S(1)}, bf16[3,96,1024]{2,1,0:T(8,128)(2,1)S(1)}, u32[]{:S(2)}, u32[]{:S(2)}) collective-permute-start(bf16[3,96,1024]{2,1,0:T(8,128)(2,1)S(1)} %get-tuple-element.77), channel_id=1, source_target_pairs={{8,0},{24,8},{16,24},{0,16},{9,1},{25,9},{17,25},{1,17},{10,2},{26... | collective-permute-start | bytes 1769480 | tf_op jit(solution)/shard_map/ppermute | solution.py:515
  28.5 19.9 %collective-permute-start.4 = (bf16[3,96,1024]{2,1,0:T(8,128)(2,1)S(1)}, bf16[3,96,1024]{2,1,0:T(8,128)(2,1)S(1)}, u32[]{:S(2)}, u32[]{:S(2)}) collective-permute-start(bf16[3,96,1024]{2,1,0:T(8,128)(2,1)S(1)} %get-tuple-element.72.refs_0_), channel_id=1, source_target_pairs={{0,8},{8,24},{24,16},{16,0},{1,9},{9,25},{25,17},{17,1},{2,10},{10... | collective-permute-start | bytes 1769480 | tf_op jit(solution)/shard_map/ppermute | solution.py:514
  38.5 21.8 %collective-permute-start.7 = (bf16[3,96,1024]{2,1,0:T(8,128)(2,1)S(1)}, bf16[3,96,1024]{2,1,0:T(8,128)(2,1)S(1)}, u32[]{:S(2)}, u32[]{:S(2)}) collective-permute-start(bf16[3,96,1024]{2,1,0:T(8,128)(2,1)S(1)} %get-tuple-element.80), channel_id=1, source_target_pairs={{8,0},{24,8},{16,24},{0,16},{9,1},{25,9},{17,25},{1,17},{10,2},{26... | collective-permute-start | bytes 1769480 | tf_op jit(solution)/shard_map/ppermute | solution.py:515
  38.5 22.5 %collective-permute-start.6 = (bf16[3,96,1024]{2,1,0:T(8,128)(2,1)S(1)}, bf16[3,96,1024]{2,1,0:T(8,128)(2,1)S(1)}, u32[]{:S(2)}, u32[]{:S(2)}) collective-permute-start(bf16[3,96,1024]{2,1,0:T(8,128)(2,1)S(1)} %get-tuple-element.75.refs_1_), channel_id=1, source_target_pairs={{0,8},{8,24},{24,16},{16,0},{1,9},{9,25},{25,17},{17,1},{2,10},{10... | collective-permute-start | bytes 1769480 | tf_op jit(solution)/shard_map/ppermute | solution.py:514
  48.4 1.9 %copy-start.2 = (bf16[3,96,1024]{2,1,0:T(8,128)(2,1)}, bf16[3,96,1024]{2,1,0:T(8,128)(2,1)S(1)}, u32[]{:S(2)}) copy-start(bf16[3,96,1024]{2,1,0:T(8,128)(2,1)S(1)} %collective-permute-done.4.refs_3_.refs_4_) | copy-start | bytes 1769476
  50.3 23.5 %collective-permute-start.9 = (bf16[3,96,1024]{2,1,0:T(8,128)(2,1)S(1)}, bf16[3,96,1024]{2,1,0:T(8,128)(2,1)S(1)}, u32[]{:S(2)}, u32[]{:S(2)}) collective-permute-start(bf16[3,96,1024]{2,1,0:T(8,128)(2,1)S(1)} %get-tuple-element.87), channel_id=1, source_target_pairs={{8,0},{24,8},{16,24},{0,16},{9,1},{25,9},{17,25},{1,17},{10,2},{26... | collective-permute-start | bytes 1769480 | tf_op jit(solution)/shard_map/ppermute | solution.py:515
  50.7 23.2 %collective-permute-start.8 = (bf16[3,96,1024]{2,1,0:T(8,128)(2,1)S(1)}, bf16[3,96,1024]{2,1,0:T(8,128)(2,1)S(1)}, u32[]{:S(2)}, u32[]{:S(2)}) collective-permute-start(bf16[3,96,1024]{2,1,0:T(8,128)(2,1)S(1)} %get-tuple-element.78.refs_1_), channel_id=1, source_target_pairs={{0,8},{8,24},{24,16},{16,0},{1,9},{9,25},{25,17},{17,1},{2,10},{10... | collective-permute-start | bytes 1769480 | tf_op jit(solution)/shard_map/ppermute | solution.py:514
  60.3 3.6 %copy-start.6 = (bf16[3,96,1024]{2,1,0:T(8,128)(2,1)}, bf16[3,96,1024]{2,1,0:T(8,128)(2,1)S(1)}, u32[]{:S(2)}) copy-start(bf16[3,96,1024]{2,1,0:T(8,128)(2,1)S(1)} %collective-permute-done.7.refs_4_.refs_7_) | copy-start | bytes 1769476
  61.0 2.9 %copy-start.8 = (bf16[3,96,1024]{2,1,0:T(8,128)(2,1)}, bf16[3,96,1024]{2,1,0:T(8,128)(2,1)S(1)}, u32[]{:S(2)}) copy-start(bf16[3,96,1024]{2,1,0:T(8,128)(2,1)S(1)} %collective-permute-done.6.refs_3_.refs_6_) | copy-start | bytes 1769476
  63.9 20.6 %collective-permute-start.12 = (bf16[3,96,1024]{2,1,0:T(8,128)(2,1)}, bf16[3,96,1024]{2,1,0:T(8,128)(2,1)}, u32[]{:S(2)}, u32[]{:S(2)}) collective-permute-start(bf16[3,96,1024]{2,1,0:T(8,128)(2,1)} %get-tuple-element.92), channel_id=1, source_target_pairs={{8,0},{24,8},{16,24},{0,16},{9,1},{25,9},{17,25},{1,17},{10,2},{26... | collective-permute-start | bytes 1769480 | tf_op jit(solution)/shard_map/ppermute | solution.py:515
  64.0 22.4 %collective-permute-start.11 = (bf16[3,96,1024]{2,1,0:T(8,128)(2,1)}, bf16[3,96,1024]{2,1,0:T(8,128)(2,1)}, u32[]{:S(2)}, u32[]{:S(2)}) collective-permute-start(bf16[3,96,1024]{2,1,0:T(8,128)(2,1)} %get-tuple-element.81.refs_1_), channel_id=1, source_target_pairs={{0,8},{8,24},{24,16},{16,0},{1,9},{9,25},{25,17},{17,1},{2,10},{10... | collective-permute-start | bytes 1769480 | tf_op jit(solution)/shard_map/ppermute | solution.py:514
  73.9 3.1 %copy-start = (bf16[3,96,1024]{2,1,0:T(8,128)(2,1)}, bf16[3,96,1024]{2,1,0:T(8,128)(2,1)S(1)}, u32[]{:S(2)}) copy-start(bf16[3,96,1024]{2,1,0:T(8,128)(2,1)S(1)} %collective-permute-done.9.refs_4_.refs_1_) | copy-start | bytes 1769476
  73.9 3.1 %copy-start.4 = (bf16[3,96,1024]{2,1,0:T(8,128)(2,1)}, bf16[3,96,1024]{2,1,0:T(8,128)(2,1)S(1)}, u32[]{:S(2)}) copy-start(bf16[3,96,1024]{2,1,0:T(8,128)(2,1)S(1)} %collective-permute-done.8.refs_3_.refs_0_) | copy-start | bytes 1769476
  77.0 36.0 %collective-permute-start.18 = (bf16[3,96,1024]{2,1,0:T(8,128)(2,1)}, bf16[3,96,1024]{2,1,0:T(8,128)(2,1)}, u32[]{:S(2)}, u32[]{:S(2)}) collective-permute-start(bf16[3,96,1024]{2,1,0:T(8,128)(2,1)} %get-tuple-element.99), channel_id=1, source_target_pairs={{8,0},{24,8},{16,24},{0,16},{9,1},{25,9},{17,25},{1,17},{10,2},{26... | collective-permute-start | bytes 1769480 | tf_op jit(solution)/shard_map/ppermute | solution.py:515
  77.1 36.8 %collective-permute-start.17 = (bf16[3,96,1024]{2,1,0:T(8,128)(2,1)}, bf16[3,96,1024]{2,1,0:T(8,128)(2,1)}, u32[]{:S(2)}, u32[]{:S(2)}) collective-permute-start(bf16[3,96,1024]{2,1,0:T(8,128)(2,1)} %get-tuple-element.88.refs_5_), channel_id=1, source_target_pairs={{0,8},{8,24},{24,16},{16,0},{1,9},{9,25},{25,17},{17,1},{2,10},{10... | collective-permute-start | bytes 1769480 | tf_op jit(solution)/shard_map/ppermute | solution.py:514
  80.4 6.0 %copy-start.17 = (bf16[16,2944]{1,0:T(8,128)(2,1)}, bf16[16,2944]{1,0:T(8,128)(2,1)S(1)}, u32[]{:S(2)}) copy-start(bf16[16,2944]{1,0:T(8,128)(2,1)S(1)} %get-tuple-element.97) | copy-start | bytes 282628
  80.4 8.8 %copy-start.10 = (bf16[16,2944]{1,0:T(8,128)(2,1)}, bf16[16,2944]{1,0:T(8,128)(2,1)S(1)}, u32[]{:S(2)}) copy-start(bf16[16,2944]{1,0:T(8,128)(2,1)S(1)} %get-tuple-element.89.refs_1_.refs_5_.refs_0_) | copy-start | bytes 282628
  86.4 12.2 %copy-start.19 = (s32[4]{0:T(128)S(1)}, s32[4]{0:T(128)}, u32[]{:S(2)}) copy-start(s32[4]{0:T(128)} %constant.78.clone) | copy-start | bytes 52
  86.4 26.7 %copy-start.18 = (bf16[16,2944]{1,0:T(8,128)(2,1)S(1)}, bf16[16,2944]{1,0:T(8,128)(2,1)}, u32[]{:S(2)}) copy-start(bf16[16,2944]{1,0:T(8,128)(2,1)} %copy-done.17) | copy-start | bytes 282628
  86.4 26.7 %copy-start.16 = (bf16[16,2944]{1,0:T(8,128)(2,1)S(1)}, bf16[16,2944]{1,0:T(8,128)(2,1)}, u32[]{:S(2)}) copy-start(bf16[16,2944]{1,0:T(8,128)(2,1)} %copy-done.15) | copy-start | bytes 282628
  89.2 40.4 %collective-permute-start.21 = (bf16[3,96,1024]{2,1,0:T(8,128)(2,1)}, bf16[3,96,1024]{2,1,0:T(8,128)(2,1)}, u32[]{:S(2)}, u32[]{:S(2)}) collective-permute-start(bf16[3,96,1024]{2,1,0:T(8,128)(2,1)} %get-tuple-element.104), channel_id=1, source_target_pairs={{8,0},{24,8},{16,24},{0,16},{9,1},{25,9},{17,25},{1,17},{10,2},{26... | collective-permute-start | bytes 1769480 | tf_op jit(solution)/shard_map/ppermute | solution.py:515
  90.4 39.2 %collective-permute-start.20 = (bf16[3,96,1024]{2,1,0:T(8,128)(2,1)}, bf16[3,96,1024]{2,1,0:T(8,128)(2,1)}, u32[]{:S(2)}, u32[]{:S(2)}) collective-permute-start(bf16[3,96,1024]{2,1,0:T(8,128)(2,1)} %get-tuple-element.93.refs_2_), channel_id=1, source_target_pairs={{0,8},{8,24},{24,16},{16,0},{1,9},{9,25},{25,17},{17,1},{2,10},{10... | collective-permute-start | bytes 1769480 | tf_op jit(solution)/shard_map/ppermute | solution.py:514
  91.3 7.3 %collective-permute-start.10 = (f32[8,4096]{1,0:T(8,128)S(1)}, f32[8,4096]{1,0:T(8,128)S(1)}, u32[]{:S(2)}, u32[]{:S(2)}) collective-permute-start(f32[8,4096]{1,0:T(8,128)S(1)} %get-tuple-element.91), channel_id=1, source_target_pairs={{0,4},{2,6},{4,0},{6,2},{1,5},{3,7},{5,1},{7,3},{8,12},{10,14},{12... | collective-permute-start | bytes 393224 | tf_op jit(solution)/shard_map/ppermute | solution.py:256
  98.6 14.4 %collective-permute-start.14 = (bf16[16,2944]{1,0:T(8,128)(2,1)}, bf16[16,2944]{1,0:T(8,128)(2,1)S(1)}, u32[]{:S(2)}, u32[]{:S(2)}) collective-permute-start(bf16[16,2944]{1,0:T(8,128)(2,1)} %get-tuple-element.96), channel_id=1, source_target_pairs={{0,8},{8,16},{16,24},{24,0},{1,9},{9,17},{17,25},{25,1},{2,10},{10... | collective-permute-start | bytes 282632 | tf_op jit(solution)/shard_map/ppermute | solution.py:538
  113.0 4.6 %collective-permute-start.15 = (bf16[16,2944]{1,0:T(8,128)(2,1)S(1)}, bf16[16,2944]{1,0:T(8,128)(2,1)S(1)}, u32[]{:S(2)}, u32[]{:S(2)}) collective-permute-start(bf16[16,2944]{1,0:T(8,128)(2,1)S(1)} %copy-done.18), channel_id=1, source_target_pairs={{0,16},{8,24},{16,0},{24,8},{1,17},{9,25},{17,1},{25,9},{2,18},{10... | collective-permute-start | bytes 282632 | tf_op jit(solution)/shard_map/ppermute | solution.py:538
  113.0 5.6 %collective-permute-start.16 = (bf16[16,2944]{1,0:T(8,128)(2,1)S(1)}, bf16[16,2944]{1,0:T(8,128)(2,1)S(1)}, u32[]{:S(2)}, u32[]{:S(2)}) collective-permute-start(bf16[16,2944]{1,0:T(8,128)(2,1)S(1)} %copy-done.16), channel_id=1, source_target_pairs={{0,24},{8,0},{16,8},{24,16},{1,25},{9,1},{17,9},{25,17},{2,26},{10... | collective-permute-start | bytes 282632 | tf_op jit(solution)/shard_map/ppermute | solution.py:538
  113.9 5.9 %collective-permute-start.13 = (f32[4,4096]{1,0:T(4,128)S(1)}, f32[4,4096]{1,0:T(4,128)S(1)}, u32[]{:S(2)}, u32[]{:S(2)}) collective-permute-start(f32[4,4096]{1,0:T(4,128)S(1)} %get-tuple-element.95), channel_id=1, source_target_pairs={{0,2},{2,0},{4,6},{6,4},{1,3},{3,1},{5,7},{7,5},{8,10},{10,8},{12,... | collective-permute-start | bytes 196616 | tf_op jit(solution)/shard_map/ppermute | solution.py:256
  115.7 3.9 %copy-start.11 = (bf16[16,2944]{1,0:T(8,128)(2,1)S(1)}, bf16[16,2944]{1,0:T(8,128)(2,1)}, u32[]{:S(2)}) copy-start(bf16[16,2944]{1,0:T(8,128)(2,1)} %copy-done.10) | copy-start | bytes 282628
  117.6 26.1 %collective-permute-start.27 = (bf16[3,96,1024]{2,1,0:T(8,128)(2,1)S(1)}, bf16[3,96,1024]{2,1,0:T(8,128)(2,1)S(1)}, u32[]{:S(2)}, u32[]{:S(2)}) collective-permute-start(bf16[3,96,1024]{2,1,0:T(8,128)(2,1)S(1)} %get-tuple-element.120), channel_id=1, source_target_pairs={{8,0},{24,8},{16,24},{0,16},{9,1},{25,9},{17,25},{1,17},{10,2},{26... | collective-permute-start | bytes 1769480 | tf_op jit(solution)/shard_map/ppermute | solution.py:515
  118.6 25.1 %collective-permute-start.26 = (bf16[3,96,1024]{2,1,0:T(8,128)(2,1)S(1)}, bf16[3,96,1024]{2,1,0:T(8,128)(2,1)S(1)}, u32[]{:S(2)}, u32[]{:S(2)}) collective-permute-start(bf16[3,96,1024]{2,1,0:T(8,128)(2,1)S(1)} %get-tuple-element.100.refs_4_), channel_id=1, source_target_pairs={{0,8},{8,24},{24,16},{16,0},{1,9},{9,25},{25,17},{17,1},{2,10},{10... | collective-permute-start | bytes 1769480 | tf_op jit(solution)/shard_map/ppermute | solution.py:514
  119.9 9.0 %copy-start.3 = (bf16[3,96,1024]{2,1,0:T(8,128)(2,1)S(1)}, bf16[3,96,1024]{2,1,0:T(8,128)(2,1)}, u32[]{:S(2)}) copy-start(bf16[3,96,1024]{2,1,0:T(8,128)(2,1)} %copy-done.2) | copy-start | bytes 1769476
  119.9 9.0 %copy-start.7 = (bf16[3,96,1024]{2,1,0:T(8,128)(2,1)S(1)}, bf16[3,96,1024]{2,1,0:T(8,128)(2,1)}, u32[]{:S(2)}) copy-start(bf16[3,96,1024]{2,1,0:T(8,128)(2,1)} %copy-done.6) | copy-start | bytes 1769476
  119.9 9.0 %copy-start.9 = (bf16[3,96,1024]{2,1,0:T(8,128)(2,1)S(1)}, bf16[3,96,1024]{2,1,0:T(8,128)(2,1)}, u32[]{:S(2)}) copy-start(bf16[3,96,1024]{2,1,0:T(8,128)(2,1)} %copy-done.8) | copy-start | bytes 1769476
  131.3 16.9 %collective-permute-start.23 = (bf16[3,96,1024]{2,1,0:T(8,128)(2,1)S(1)}, bf16[3,96,1024]{2,1,0:T(8,128)(2,1)S(1)}, u32[]{:S(2)}, u32[]{:S(2)}) collective-permute-start(bf16[3,96,1024]{2,1,0:T(8,128)(2,1)S(1)} %get-tuple-element.111), channel_id=1, source_target_pairs={{8,0},{24,8},{16,24},{0,16},{9,1},{25,9},{17,25},{1,17},{10,2},{26... | collective-permute-start | bytes 1769480 | tf_op jit(solution)/shard_map/ppermute | solution.py:515
  132.0 16.1 %collective-permute-start.22 = (bf16[3,96,1024]{2,1,0:T(8,128)(2,1)S(1)}, bf16[3,96,1024]{2,1,0:T(8,128)(2,1)S(1)}, u32[]{:S(2)}, u32[]{:S(2)}) collective-permute-start(bf16[3,96,1024]{2,1,0:T(8,128)(2,1)S(1)} %get-tuple-element.110.refs_2_.refs_6_), channel_id=1, source_target_pairs={{0,8},{8,24},{24,16},{16,0},{1,9},{9,25},{25,17},{17,1},{2,10},{10... | collective-permute-start | bytes 1769480 | tf_op jit(solution)/shard_map/ppermute | solution.py:514
  133.4 9.7 %collective-permute-start.19 = (f32[2,4096]{1,0:T(2,128)S(1)}, f32[2,4096]{1,0:T(2,128)S(1)}, u32[]{:S(2)}, u32[]{:S(2)}) collective-permute-start(f32[2,4096]{1,0:T(2,128)S(1)} %get-tuple-element.103), channel_id=1, source_target_pairs={{0,1},{1,0},{2,3},{3,2},{4,5},{5,4},{6,7},{7,6},{8,9},{9,8},{10,11... | collective-permute-start | bytes 98312 | tf_op jit(solution)/shard_map/ppermute | solution.py:256
  133.4 9.0 %copy-start.1 = (bf16[3,96,1024]{2,1,0:T(8,128)(2,1)S(1)}, bf16[3,96,1024]{2,1,0:T(8,128)(2,1)}, u32[]{:S(2)}) copy-start(bf16[3,96,1024]{2,1,0:T(8,128)(2,1)} %copy-done) | copy-start | bytes 1769476
  133.4 9.0 %copy-start.5 = (bf16[3,96,1024]{2,1,0:T(8,128)(2,1)S(1)}, bf16[3,96,1024]{2,1,0:T(8,128)(2,1)}, u32[]{:S(2)}) copy-start(bf16[3,96,1024]{2,1,0:T(8,128)(2,1)} %copy-done.4) | copy-start | bytes 1769476
  146.0 16.3 %collective-permute-start.28 = (bf16[3,96,1024]{2,1,0:T(8,128)(2,1)S(1)}, bf16[3,96,1024]{2,1,0:T(8,128)(2,1)S(1)}, u32[]{:S(2)}, u32[]{:S(2)}) collective-permute-start(bf16[3,96,1024]{2,1,0:T(8,128)(2,1)S(1)} %get-tuple-element.121), channel_id=1, source_target_pairs={{0,8},{8,24},{24,16},{16,0},{1,9},{9,25},{25,17},{17,1},{2,10},{10... | collective-permute-start | bytes 1769480 | tf_op jit(solution)/shard_map/ppermute | solution.py:514
  146.1 16.2 %collective-permute-start.29 = (bf16[3,96,1024]{2,1,0:T(8,128)(2,1)S(1)}, bf16[3,96,1024]{2,1,0:T(8,128)(2,1)S(1)}, u32[]{:S(2)}, u32[]{:S(2)}) collective-permute-start(bf16[3,96,1024]{2,1,0:T(8,128)(2,1)S(1)} %get-tuple-element.122), channel_id=1, source_target_pairs={{8,0},{24,8},{16,24},{0,16},{9,1},{25,9},{17,25},{1,17},{10,2},{26... | collective-permute-start | bytes 1769480 | tf_op jit(solution)/shard_map/ppermute | solution.py:515
  149.8 24.6 %collective-permute-start.25 = (bf16[3,96,1024]{2,1,0:T(8,128)(2,1)S(1)}, bf16[3,96,1024]{2,1,0:T(8,128)(2,1)S(1)}, u32[]{:S(2)}, u32[]{:S(2)}) collective-permute-start(bf16[3,96,1024]{2,1,0:T(8,128)(2,1)S(1)} %get-tuple-element.119), channel_id=1, source_target_pairs={{8,0},{24,8},{16,24},{0,16},{9,1},{25,9},{17,25},{1,17},{10,2},{26... | collective-permute-start | bytes 1769480 | tf_op jit(solution)/shard_map/ppermute | solution.py:515
  149.9 24.6 %collective-permute-start.24 = (bf16[3,96,1024]{2,1,0:T(8,128)(2,1)S(1)}, bf16[3,96,1024]{2,1,0:T(8,128)(2,1)S(1)}, u32[]{:S(2)}, u32[]{:S(2)}) collective-permute-start(bf16[3,96,1024]{2,1,0:T(8,128)(2,1)S(1)} %get-tuple-element.118.refs_6_.refs_9_), channel_id=1, source_target_pairs={{0,8},{8,24},{24,16},{16,0},{1,9},{9,25},{25,17},{17,1},{2,10},{10... | collective-permute-start | bytes 1769480 | tf_op jit(solution)/shard_map/ppermute | solution.py:514
  (2 other events, 1.3 us)

commit v4 on v3

--- a/solution.py
+++ b/solution.py
@@ -11,7 +11,6 @@
 LAG = 2
 MOST_CHUNKS = 20
 TILE = 16
-GROUP = 8
 VMEM = 48 << 20
 
 ANY = pl.BlockSpec(memory_space=pl.ANY)
@@ -33,6 +32,10 @@
     parts = min(parts, total)
     edges = [total * i // parts for i in range(parts + 1)]
     return [(a, b - a) for a, b in zip(edges, edges[1:])]
+
+
+def row_group(rows):
+    return largest((g for g in (16, 32) if rows % g == 0), rows)
 
 
 def cost(flops, bytes_accessed, transcendentals=0):
@@ -49,12 +52,29 @@
     return master_old - 0.01 * step, first_new, second_new
 
 
-def pack_body(flag, *refs, places, chunk, count_seen, count_after):
+def column_pieces(lengths, width):
+    moves, column = [], 0
+    for part, length in enumerate(lengths):
+        begin = 0
+        while begin < length:
+            piece, to = divmod(column, width)
+            run = min(length - begin, width - to)
+            moves.append((part, begin, piece, to, run))
+            begin, column = begin + run, column + run
+    return moves
+
+
+def pack_body(flag, targets, *refs, places, chunk, slabs, passed, counts):
     state = refs[0:3]
+    count_seen, count_parts, count_after = counts
     seen = refs[3 : 3 + count_seen]
-    rest = refs[3 + count_seen + count_after :]
+    both = refs[3 + count_seen]
+    parts = refs[4 + count_seen : 4 + count_seen + count_parts]
+    rest = refs[3 + count_seen + (count_parts + 1 if count_parts else 0) + count_after :]
     sends = rest[:2]
-    held, sem = rest[2:]
+    held, sem, passed_sem = rest[2:]
+    width = sends[0].shape[1]
+    size = 3 * chunk
 
     def fetch(j):
         way, k = divmod(j, 3)
@@ -67,46 +87,88 @@
         for j in range(6):
             way, k = divmod(j, 3)
             fetch(j).wait()
-            sends[way][k] = held[j].astype(BF16)
+            sends[way][pl.ds(k * chunk, chunk)] = held[j].astype(BF16)
 
     def relay(way):
-        return pltpu.make_async_copy(seen[way], sends[way], sem.at[way])
+        rows = pl.ds(0, size)
+        return pltpu.make_async_copy(seen[way].at[rows], sends[way].at[rows], sem.at[way])
+
+    def hand_on(way):
+        rows = pl.ds(size, passed[way])
+        return pltpu.make_async_copy(
+            seen[way].at[rows], sends[way].at[rows], passed_sem.at[way]
+        )
+
+    for way in range(2):
+        if passed[way]:
+            hand_on(way).start()
 
     if not seen:
         convert()
-        return
-    pl.when(flag[0] == 1)(convert)
-
-    @pl.when(flag[0] == 0)
-    def _():
-        for way in range(2):
-            relay(way).start()
-        for way in range(2):
-            relay(way).wait()
-
-
-def pack(is_source, state, seen, after, places, chunk):
+    else:
+        pl.when(flag[0] == 1)(convert)
+
+        @pl.when(flag[0] == 0)
+        def _():
+            for way in range(2):
+                relay(way).start()
+            for way in range(2):
+                relay(way).wait()
+
+    n = targets.shape[0]
+    for way in range(2):
+        if slabs[way]:
+            tokens, features = both.shape[0], both.shape[1] // 2
+            keep = flag[1] == 0
+            below = size
+            moves = column_pieces([part.shape[1] for part in parts], width)
+            for part, begin, piece, to, run in moves:
+                units = parts[part][:, begin : begin + run]
+                rows = pl.ds(size + piece * tokens, tokens)
+                sends[way][rows, pl.ds(to, run)] = jnp.where(
+                    keep, units, jnp.zeros_like(units)
+                )
+            below += (1 + moves[-1][2]) * tokens
+            for far in range(slabs[way], 0, -1):
+                target = targets[far if way == 0 else n - far]
+                slab = pl.ds(pl.multiple_of(features + target * width, 128), width)
+                sends[way][pl.ds(below, tokens)] = both[:, slab]
+                below += tokens
+
+    for way in range(2):
+        if passed[way]:
+            hand_on(way).wait()
+
+
+def pack(flag, targets, state, seen, parcel, after, places, chunk, slabs, passed):
     width = state[0].shape[2]
-    shape = jax.ShapeDtypeStruct((3, chunk, width), BF16)
+    extra = list(passed)
+    if parcel:
+        tokens = parcel[0].shape[0]
+        pieces = -(-sum(part.shape[1] for part in parcel[1:]) // width)
+        extra = [tokens * (pieces + count) if count else 0 for count in slabs]
+    counts = (len(seen), max(len(parcel) - 1, 0), len(after))
     return pl.pallas_call(
         functools.partial(
-            pack_body,
-            places=places,
-            chunk=chunk,
-            count_seen=len(seen),
-            count_after=len(after),
+            pack_body, places=places, chunk=chunk, slabs=slabs, passed=passed, counts=counts
         ),
-        in_specs=[SMEM] + [ANY] * (3 + len(seen) + len(after)),
+        in_specs=[SMEM, SMEM]
+        + [ANY] * (3 + len(seen))
+        + [WHOLE] * len(parcel)
+        + [ANY] * len(after),
         out_specs=[WHOLE, WHOLE],
-        out_shape=[shape, shape],
+        out_shape=[
+            jax.ShapeDtypeStruct((3 * chunk + more, width), BF16) for more in extra
+        ],
         scratch_shapes=[
             pltpu.VMEM((6, chunk, width), F32),
             pltpu.SemaphoreType.DMA((6,)),
+            pltpu.SemaphoreType.DMA((2,)),
         ],
         compiler_params=PARAMS,
         cost_estimate=cost(0, 2 * 3 * chunk * width * 6),
         name="pack",
-    )(is_source, *state, *seen, *after)
+    )(flag, targets, *state, *seen, *parcel, *after)
 
 
 def beside_body(*refs):
@@ -261,76 +323,88 @@
         return (self.value,)
 
 
-def parcels_body(where, *refs, count, n, features):
-    both, hidden = refs[0], refs[1 : 1 + count]
-    parcels = refs[-n:]
-    units = sum(part.shape[1] for part in hidden)
-    width = parcels[0].shape[1] - units
-    keep = where[1] == 0
-    for far in range(n):
-        to = lax.rem(where[0] + far, n)
-        first = 0
-        for part in hidden:
-            here = pl.ds(first, part.shape[1])
-            parcels[far][:, here] = jnp.where(keep, part[...], jnp.zeros_like(part))
-            first += part.shape[1]
-        slab = pl.ds(pl.multiple_of(features + to * width, 128), width)
-        parcels[far][:, pl.ds(units, width)] = both[:, slab]
-
-
-def make_parcels(where, both, hidden, after, n, width):
-    rows = both.shape[0]
-    features = both.shape[1] // 2
-    length = sum(part.shape[1] for part in hidden) + width
-    shape = jax.ShapeDtypeStruct((rows, length), BF16)
+def collect_body(flag, targets, both, *refs, places, parts_count, size, pieces):
+    parts = refs[:parts_count]
+    blocks = refs[parts_count : parts_count + len(places)]
+    hidden_t, outs, held, sem = refs[-4:]
+    tokens, features = both.shape[0], both.shape[1] // 2
+    width = outs.shape[1]
+
+    def fetch(j, part):
+        rows = pl.ds(size, pieces * tokens) if part == 0 else pl.ds(places[j], tokens)
+        here = pl.ds(0, pieces * tokens) if part == 0 else pl.ds(pieces * tokens, tokens)
+        return pltpu.make_async_copy(
+            blocks[j].at[rows], held.at[j + 1, here], sem.at[j, part]
+        )
+
+    for j in range(len(places)):
+        for part in range(2):
+            fetch(j, part).start()
+    keep = flag[1] == 0
+    for part, begin, piece, to, run in column_pieces([p.shape[1] for p in parts], width):
+        units = parts[part][:, begin : begin + run]
+        held[0, pl.ds(piece * tokens, tokens), pl.ds(to, run)] = jnp.where(
+            keep, units, jnp.zeros_like(units)
+        )
+    slab = pl.ds(pl.multiple_of(features + targets[0] * width, 128), width)
+    held[0, pl.ds(pieces * tokens, tokens)] = both[:, slab]
+    for j in range(len(places)):
+        for part in range(2):
+            fetch(j, part).wait()
+
+    count = len(places) + 1
+    for j in range(count):
+        outs[pl.ds(j * tokens, tokens)] = held[j, pl.ds(pieces * tokens, tokens)]
+    for piece in range(pieces):
+        run = min(width, hidden_t.shape[0] - piece * width)
+        rows = pl.ds(piece * tokens, tokens)
+        hidden = jnp.concatenate([held[j, rows, :run] for j in range(count)], axis=0)
+        hidden_t[pl.ds(piece * width, run)] = hidden.astype(F32).T.astype(BF16)
+
+
+def collect(flag, targets, both, parts, blocks, places, size, width, after):
+    tokens = both.shape[0]
+    units = sum(part.shape[1] for part in parts)
+    pieces = -(-units // width)
+    depth = tokens * (len(blocks) + 1)
     return pl.pallas_call(
-        functools.partial(parcels_body, count=len(hidden), n=n, features=features),
-        in_specs=[SMEM] + [WHOLE] * (1 + len(hidden)) + [ANY] * len(after),
-        out_specs=[WHOLE] * n,
-        out_shape=[shape] * n,
-        compiler_params=PARAMS,
-        cost_estimate=cost(0, 4 * n * rows * length),
-        name="parcels",
-    )(where, both, *hidden, *after)
-
-
-def collect_body(*refs, count, units):
-    hidden_t, outs = refs[-2:]
-    rows = refs[0].shape[0]
-    for j in range(count):
-        outs[pl.ds(j * rows, rows)] = refs[j][:, units:]
-    hidden = jnp.concatenate([refs[j][:, :units] for j in range(count)], axis=0)
-    hidden_t[...] = hidden.astype(F32).T.astype(BF16)
-
-
-def collect(parcels, units, after):
-    rows, length = parcels[0].shape
-    depth = rows * len(parcels)
-    return pl.pallas_call(
-        functools.partial(collect_body, count=len(parcels), units=units),
-        in_specs=[WHOLE] * len(parcels) + [ANY] * len(after),
+        functools.partial(
+            collect_body,
+            places=places,
+            parts_count=len(parts),
+            size=size,
+            pieces=pieces,
+        ),
+        in_specs=[SMEM, SMEM]
+        + [WHOLE] * (1 + len(parts))
+        + [ANY] * (len(blocks) + len(after)),
         out_specs=[WHOLE, WHOLE],
         out_shape=[
             jax.ShapeDtypeStruct((units, depth), BF16),
-            jax.ShapeDtypeStruct((depth, length - units), BF16),
+            jax.ShapeDtypeStruct((depth, width), BF16),
+        ],
+        scratch_shapes=[
+            pltpu.VMEM((len(blocks) + 1, (pieces + 1) * tokens, width), BF16),
+            pltpu.SemaphoreType.DMA((len(blocks), 2)),
         ],
         compiler_params=PARAMS,
-        cost_estimate=cost(0, 4 * depth * length),
+        cost_estimate=cost(0, 4 * depth * (units + width)),
         name="collect",
-    )(*parcels, *after)
+    )(flag, targets, both, *parts, *blocks, *after)
 
 
 def update_body(info, hid_ref, out_ref, *refs, healthy, block, first, count, unread):
     state, news = refs[:3], refs[3 + unread : 6 + unread]
     total = refs[6 + unread]
     width = out_ref.shape[1]
+    group = row_group(block)
 
     def step(hid, m_ref, a_ref, b_ref, m_new, a_new, b_new):
         total[...] = jnp.dot(hid[...], out_ref[...], preferred_element_type=F32)
 
-        @pl.loop(0, block // GROUP)
+        @pl.loop(0, block // group)
         def _(i):
-            here = pl.ds(pl.multiple_of(i * GROUP, GROUP), GROUP)
+            here = pl.ds(pl.multiple_of(i * group, group), group)
             m_new[here], a_new[here], b_new[here] = updated(
                 m_ref[0, here], a_ref[0, here], b_ref[0, here], total[here], healthy
             )
@@ -388,12 +462,14 @@
     rest = refs[count + 3 + count_after :]
     news = rest[:3]
     held, made, total, in_sem, out_sem = rest[3:]
-    chunk = held.shape[2]
+    chunk = made.shape[2]
+    group = row_group(chunk)
     ahead = info[1]
     lag_of = {True: LAG * (ahead - 1), False: LAG * (n - ahead - 1)}
 
     def fetch(j):
-        return pltpu.make_async_copy(got[j], held.at[j % 2], in_sem.at[j % 2])
+        rows = got[j].at[pl.ds(0, 3 * chunk)]
+        return pltpu.make_async_copy(rows, held.at[j % 2], in_sem.at[j % 2])
 
     def first_row(j):
         step, forward = arrivals[j]
@@ -435,13 +511,16 @@
                 units = hid_ref[pl.ds(first, chunk)]
                 total[...] = jnp.dot(units, out_ref[...], preferred_element_type=F32)
 
-                @pl.loop(0, chunk // TILE)
+                @pl.loop(0, chunk // group)
                 def _(i):
-                    here = pl.ds(pl.multiple_of(i * TILE, TILE), TILE)
-                    old = [held[slot, k, here].astype(F32) for k in range(3)]
-                    new = updated(*old, total[here], n - 1.0)
+                    base = pl.multiple_of(i * group, group)
+                    old = [
+                        held[slot, pl.ds(k * chunk + base, group)].astype(F32)
+                        for k in range(3)
+                    ]
+                    new = updated(*old, total[pl.ds(base, group)], n - 1.0)
                     for k in range(3):
-                        made[slot, k, here] = new[k]
+                        made[slot, k, pl.ds(base, group)] = new[k]
 
                 for k in range(3):
                     store(j, k).start()
@@ -463,7 +542,7 @@
         out_specs=[ANY] * 3,
         out_shape=[shape] * 3,
         scratch_shapes=[
-            pltpu.VMEM((2, 3, chunk, width), BF16),
+            pltpu.VMEM((2, 3 * chunk, width), BF16),
             pltpu.VMEM((2, 3, chunk, width), F32),
             pltpu.VMEM((chunk, width), F32),
             pltpu.SemaphoreType.DMA((2,)),
@@ -491,24 +570,53 @@
     order = ring_order(n)
     place = jnp.array([order.index(i) for i in range(n)], jnp.int32)
     ahead = (place[failed_id] - place[source]) % n
-    is_source = (me == source).astype(jnp.int32)[None]
-    info = jnp.stack([(me == failed_id).astype(jnp.int32), ahead.astype(jnp.int32)])
+    lost = (me == failed_id).astype(jnp.int32)
+    flag = jnp.stack([(me == source).astype(jnp.int32), lost])
+    info = jnp.stack([lost, ahead.astype(jnp.int32)])
+    targets = jnp.array(order, jnp.int32)[(place[me] + jnp.arange(n)) % n]
 
     state = (master, moment1, moment2)
     chunks = largest(
         (c for c in range(2, MOST_CHUNKS + 1, 2) if rows % (TILE * c) == 0), 2
     )
+    chunk = rows // chunks
     steps = (chunks + LAG * (n - 2)) // 2
+    reach = (n // 2, (n - 1) // 2)
     forward = [(order[p], order[(p + 1) % n]) for p in range(n)]
     backward = [(b, a) for a, b in forward]
     sends, got = [], []
-
-    def send(*after):
+    parcel_from = None
+
+    def send(*after, parcel=()):
+        nonlocal parcel_from
         step = len(got)
         seen = got[step - LAG] if step >= LAG else ()
         here = min(step, chunks - 1)
-        places = (here, chunks - 1 - here)
-        sends.append(pack(is_source, state, seen, after, places, rows // chunks))
+        slabs, passed = (0, 0), (0, 0)
+        if parcel:
+            parcel_from, slabs = step, reach
+        elif parcel_from is not None and (step - parcel_from) % LAG == 0:
+            hop = (step - parcel_from) // LAG
+            passed = tuple(
+                seen[way].shape[0] - 3 * chunk - both.shape[0]
+                if hop < reach[way]
+                else 0
+                for way in range(2)
+            )
+        sends.append(
+            pack(
+                flag,
+                targets,
+                state,
+                seen,
+                parcel,
+                after,
+                (here, chunks - 1 - here),
+                chunk,
+                slabs,
+                passed,
+            )
+        )
         got.append(
             (
                 lax.ppermute(sends[-1][0], "replica", forward),
@@ -525,30 +633,29 @@
 
     tile = 128 if units % 128 == 0 else units
     hidden, d_rows = [], None
-    for first, count in shares(units // tile, 4):
+    pieces = shares(units // tile, 4)
+    for first, count in pieces:
         part, d_rows = layer(both, w_gate, w_up, w_down, d_rows, sent, tile, first, count)
         hidden.append(part)
-        sent = send(d_rows)
-
-    where = jnp.stack([me, info[0]])
-    parcels = make_parcels(where, both, hidden, sent, n, width)
-    arrived = [parcels[0]]
-    for far in range(1, n):
-        route = [(i, (i + far) % n) for i in range(n)]
-        arrived.append(lax.ppermute(parcels[far], "replica", route))
+        last = len(hidden) == len(pieces)
+        sent = send(d_rows, parcel=(both, *hidden) if last else ())
     cotangents = ScatteredSum(d_rows, ("fsdp", "tensor"))
-    sent = send(parcels[0], *cotangents.advance((parcels[0],)))
-    sent = send(*cotangents.advance(sent))
-
-    hidden_t, outs = collect(arrived, units, sent)
-    sent = (hidden_t,)
-    block = largest((b for b in range(TILE, 193, TILE) if rows % b == 0), rows)
-    turns = shares(rows // block, 3)
+
     news = ()
     patched = 0
-
-    def update_next(after):
-        first, count = turns.pop(0)
+    hidden_t = outs = None
+
+    def gathered(after):
+        blocks, places = [], []
+        for way in range(2):
+            for hop in range(reach[way]):
+                blocks.append(got[parcel_from + LAG * hop][way])
+                places.append(blocks[-1].shape[0] - both.shape[0])
+        return collect(
+            flag, targets, both, hidden, blocks, places, 3 * chunk, width, after
+        )
+
+    def update_part(first, count, after):
         return update(
             info, hidden_t, outs, state, news, after, n - 1.0, block, first, count
         )
@@ -562,13 +669,20 @@
         patched = step
         return patch(info, hidden_t, outs, blocks, arrivals, news, after, chunks, n)
 
+    block = largest((b for b in range(TILE, 193, TILE) if rows % b == 0), rows)
+    blocks = rows // block
+    early = blocks // 4
+    ready = parcel_from + LAG * reach[0] + 1
     while len(got) < steps:
-        if len(turns) > 1:
-            news = update_next(sent)
-            news = patch_to(len(got) // 2 if patched == 0 else len(got) - 2, ())
-        sent = send(*news[:1], *cotangents.advance(sent))
-    while turns:
-        news = update_next(sent)
+        sent = send(*cotangents.advance(sent), *news[:1])
+        if len(got) == ready and early and len(got) < steps:
+            hidden_t, outs = gathered(sent)
+            news = update_part(0, early, (hidden_t,))
+            news = patch_to(4, ())
+    if hidden_t is None:
+        hidden_t, outs = gathered(sent)
+        early = 0
+    news = update_part(early, blocks - early, sent)
     news = patch_to(steps - 1, sent)
     news = patch_to(steps, ())
     while not cotangents.done:

time: 177 us -> 176 us (level)
  the two profiles are of different devices: /device:TPU:0 before, /device:TPU:16 now
where the time goes in v4:
time: 176 us; the launch traced here: 175 us
  Pallas kernels  81.7 us (46%)
  waiting for transfers between devices  40.7 us (23%)
  starting transfers between devices  30.4 us (17%)
  blocking collectives  12.5 us (7%)
  local copies, waits for them, and re-layouts  6.08 us (3%)
  between operations  3.18 us (2%)
    pallas_call x4, Pallas kernels, layer(): pl.pallas_call(functools.partial(layer_body, resumed=resumed), grid=(coun...  30 us
    pallas_call x12, Pallas kernels, pack(): pl.pallas_call(functools.partial(pack_body, places=places, chunk=chunk, s...  24.4 us
    pallas_call x3, Pallas kernels, patch(): pl.pallas_call(functools.partial(patch_body, arrivals=arrivals, chunks=ch...  24.2 us
    ppermute x12, waiting for transfers between devices, send(): lax.ppermute(sends[-1][1], 'replica', backward)  16.2 us
    ppermute x12, waiting for transfers between devices, send(): lax.ppermute(sends[-1][0], 'replica', forward)  15.9 us
    ppermute x12, starting transfers between devices, send(): lax.ppermute(sends[-1][0], 'replica', forward)  14.7 us
    ppermute x12, starting transfers between devices, send(): lax.ppermute(sends[-1][1], 'replica', backward)  14.1 us
    all_gather x1, blocking collectives, per_device(): both = lax.all_gather(both, ('fsdp', 'tensor'), axis=0, tiled=True)  12.5 us
  transfers between devices with their start and end apart: 27, of which 16 were waited for; matrix products, arithmetic and copies ran while one was open for 0% of the time, Pallas kernels for 43%

profile of v4, /device:TPU:16, one launch (start us, length us, event | category | flops | bytes accessed | tf_op | source)
XLA Modules:
  0.0 175.4 jit_solution(7022446869853031108)
XLA Ops:
  1.3 1.4 fusion.2
  3.4 1.3 gather_fusion
  4.8 3.0 %pack.12 = (bf16[288,1024]{1,0:T(8,128)(2,1)S(1)}, bf16[288,1024]{1,0:T(8,128)(2,1)}) custom-call(s32[2]{0:T(128)S(1)} %pad_add_fusion.flag, s32[4]{0:T(128)S(1)} %gather_fusion, f32[2,1920,1024]{2,1,0:T(8,128)} %refs_0_.27, f32[2,1920,1024]{2,1,0:T(8,128)} %refs_1_.27, f32[2,1920,1024]{2,1,0:T(8,128)} %refs_2_.27), custom_call_target="tpu_custom_call" | custom-call | bytes 3538944 | tf_op jit(solution)/shard_map/pack/pallas_call | solution.py:151
  7.8 1.6 collective-permute-start.1
  9.9 3.2 %pack.13 = (bf16[288,1024]{1,0:T(8,128)(2,1)}, bf16[288,1024]{1,0:T(8,128)(2,1)}) custom-call(s32[2]{0:T(128)S(1)} %pad_add_fusion.flag, s32[4]{0:T(128)S(1)} %gather_fusion, f32[2,1920,1024]{2,1,0:T(8,128)} %refs_0_.27, f32[2,1920,1024]{2,1,0:T(8,128)} %refs_1_.27, f32[2,1920,1024]{2,1,0:T(8,128)} %refs_2_.27, bf16[288,1024]{1,0:T(8,128)(2,1)S(1)} %get-tuple-element.59.refs_3_), custom_call_target="tpu_custom_call" | custom-call | bytes 3538944 | tf_op jit(solution)/shard_map/pack/pallas_call | solution.py:151
  13.1 1.6 collective-permute-start.3
  15.2 12.5 %all-gather = bf16[8,2,8192]{2,1,0:T(2,128)(2,1)S(1)} all-gather(bf16[1,2,8192]{2,1,0:T(2,128)(2,1)S(1)} %bitcast.20), channel_id=1, replica_groups=mesh['replica'=4,'fsdp'=4,'tensor'=2] {'fsdp','tensor'}, dimensions={0}, use_global_device_ids=true | all-gather | bytes 294912 | tf_op jit(solution)/shard_map/all_gather | solution.py:631
  28.9 1.5 collective-permute-start.5
  30.4 1.3 collective-permute-start.4
  31.7 6.4 %layer.4 = (bf16[16,384]{1,0:T(8,128)(2,1)S(1)}, f32[16,4096]{1,0:T(8,128)S(1)}) custom-call(bf16[16,8192]{1,0:T(8,128)(2,1)S(1)} %reshape.69.refs_5_.both, bf16[4096,1920]{1,0:T(8,128)(2,1)} %gate_ref.7, bf16[4096,1920]{1,0:T(8,128)(2,1)} %up_ref.7, bf16[1920,4096]{1,0:T(8,128)(2,1)} %down_ref.7, bf16[288,1024]{1,0:T(8,128)(2,1)S(1)} %get-tuple-element.62.refs_0_), custom_call_target="tpu_custom_call" | custom-call | flops 251658240 | bytes 9437184 | tf_op jit(solution)/shard_map/layer/pallas_call | solution.py:237
  39.2 1.5 collective-permute-start.7
  40.7 1.7 collective-permute-start.6
  42.4 7.9 %layer.5 = (bf16[16,512]{1,0:T(8,128)(2,1)S(1)}, f32[16,4096]{1,0:T(8,128)S(1)}) custom-call(bf16[16,8192]{1,0:T(8,128)(2,1)S(1)} %reshape.69.refs_5_.both, bf16[4096,1920]{1,0:T(8,128)(2,1)} %gate_ref.7, bf16[4096,1920]{1,0:T(8,128)(2,1)} %up_ref.7, bf16[1920,4096]{1,0:T(8,128)(2,1)} %down_ref.7, f32[16,4096]{1,0:T(8,128)S(1)} %get-tuple-element.63.refs_5_.refs_0_, ...), custom_call_target="tpu_custom_call" | custom-call | flops 335544320 | bytes 12582912 | tf_op jit(solution)/shard_map/layer/pallas_call | solution.py:237
  51.8 1.5 collective-permute-start.9
  53.4 1.3 collective-permute-start.8
  54.7 7.9 %layer.6 = (bf16[16,512]{1,0:T(8,128)(2,1)S(1)}, f32[16,4096]{1,0:T(8,128)S(1)}) custom-call(bf16[16,8192]{1,0:T(8,128)(2,1)S(1)} %reshape.69.refs_5_.both, bf16[4096,1920]{1,0:T(8,128)(2,1)} %gate_ref.7, bf16[4096,1920]{1,0:T(8,128)(2,1)} %up_ref.7, bf16[1920,4096]{1,0:T(8,128)(2,1)} %down_ref.7, f32[16,4096]{1,0:T(8,128)S(1)} %get-tuple-element.66.refs_5_.refs_0_, ...), custom_call_target="tpu_custom_call" | custom-call | flops 335544320 | bytes 12582912 | tf_op jit(solution)/shard_map/layer/pallas_call | solution.py:237
  63.6 1.9 %pack.17 = (bf16[288,1024]{1,0:T(8,128)(2,1)}, bf16[288,1024]{1,0:T(8,128)(2,1)}) custom-call(s32[2]{0:T(128)S(1)} %pad_add_fusion.flag, s32[4]{0:T(128)S(1)} %gather_fusion, f32[2,1920,1024]{2,1,0:T(8,128)} %refs_0_.27, f32[2,1920,1024]{2,1,0:T(8,128)} %refs_1_.27, f32[2,1920,1024]{2,1,0:T(8,128)} %refs_2_.27, ...), custom_call_target="tpu_custom_call" | custom-call | bytes 3538944 | tf_op jit(solution)/shard_map/pack/pallas_call | solution.py:151
  65.5 1.5 collective-permute-start.12
  67.9 7.9 %layer.7 = (bf16[16,512]{1,0:T(8,128)(2,1)S(1)}, f32[16,4096]{1,0:T(8,128)S(1)}) custom-call(bf16[16,8192]{1,0:T(8,128)(2,1)S(1)} %reshape.69.refs_5_.both, bf16[4096,1920]{1,0:T(8,128)(2,1)} %gate_ref.7, bf16[4096,1920]{1,0:T(8,128)(2,1)} %up_ref.7, bf16[1920,4096]{1,0:T(8,128)(2,1)} %down_ref.7, f32[16,4096]{1,0:T(8,128)S(1)} %get-tuple-element.69.refs_5_.refs_0_, ...), custom_call_target="tpu_custom_call" | custom-call | flops 335544320 | bytes 12582912 | tf_op jit(solution)/shard_map/layer/pallas_call | solution.py:237
  76.2 2.1 %pack.18 = (bf16[352,1024]{1,0:T(8,128)(2,1)}, bf16[336,1024]{1,0:T(8,128)(2,1)}) custom-call(s32[2]{0:T(128)S(1)} %pad_add_fusion.flag, s32[4]{0:T(128)S(1)} %gather_fusion, f32[2,1920,1024]{2,1,0:T(8,128)} %refs_0_.27, f32[2,1920,1024]{2,1,0:T(8,128)} %refs_1_.27, f32[2,1920,1024]{2,1,0:T(8,128)} %refs_2_.27, ...), custom_call_target="tpu_custom_call" | custom-call | bytes 3538944 | tf_op jit(solution)/shard_map/pack/pallas_call | solution.py:151
  78.3 2.9 %collective-permute-start.14 = (bf16[352,1024]{1,0:T(8,128)(2,1)}, bf16[352,1024]{1,0:T(8,128)(2,1)S(1)}, u32[]{:S(2)}, u32[]{:S(2)}) collective-permute-start(bf16[352,1024]{1,0:T(8,128)(2,1)} %get-tuple-element.78.refs_1_), channel_id=1, source_target_pairs={{0,8},{8,24},{24,16},{16,0},{1,9},{9,25},{25,17},{17,1},{2,10},{10... | collective-permute-start | bytes 2162696 | tf_op jit(solution)/shard_map/ppermute | solution.py:622
  81.3 6.3 %collective-permute-done.12.refs_4_.refs_3_ = bf16[288,1024]{1,0:T(8,128)(2,1)} collective-permute-done((bf16[288,1024]{1,0:T(8,128)(2,1)}, bf16[288,1024]{1,0:T(8,128)(2,1)}, u32[]{:S(2)}, u32[]{:S(2)}) %collective-permute-start.12) | collective-permute-done | bytes 589856 | tf_op jit(solution)/shard_map/ppermute | solution.py:623
  87.6 1.4 collective-permute-done.11.refs_3_.refs_2_
  89.0 2.9 %pack.19 = (bf16[288,1024]{1,0:T(8,128)(2,1)}, bf16[288,1024]{1,0:T(8,128)(2,1)}) custom-call(s32[2]{0:T(128)S(1)} %pad_add_fusion.flag, s32[4]{0:T(128)S(1)} %gather_fusion, f32[2,1920,1024]{2,1,0:T(8,128)} %refs_0_.27, f32[2,1920,1024]{2,1,0:T(8,128)} %refs_1_.27, f32[2,1920,1024]{2,1,0:T(8,128)} %refs_2_.27, ...), custom_call_target="tpu_custom_call" | custom-call | bytes 3538944 | tf_op jit(solution)/shard_map/pack/pallas_call | solution.py:151
  91.8 1.5 collective-permute-start.18
  93.9 6.0 %collective-permute-done.10.refs_1_ = f32[8,4096]{1,0:T(8,128)S(1)} collective-permute-done((f32[8,4096]{1,0:T(8,128)S(1)}, f32[8,4096]{1,0:T(8,128)S(1)}, u32[]{:S(2)}, u32[]{:S(2)}) %collective-permute-start.10) | collective-permute-done | bytes 131104 | tf_op jit(solution)/shard_map/ppermute | solution.py:318
  99.9 2.3 %collective-permute-done.15.refs_4_.refs_6_.refs_5_ = bf16[336,1024]{1,0:T(8,128)(2,1)S(1)} collective-permute-done((bf16[336,1024]{1,0:T(8,128)(2,1)}, bf16[336,1024]{1,0:T(8,128)(2,1)S(1)}, u32[]{:S(2)}, u32[]{:S(2)}) %collective-permute-start.15) | collective-permute-done | bytes 688160 | tf_op jit(solution)/shard_map/ppermute | solution.py:623
  102.2 2.1 %collective-permute-done.14.refs_3_.refs_4_ = bf16[352,1024]{1,0:T(8,128)(2,1)S(1)} collective-permute-done((bf16[352,1024]{1,0:T(8,128)(2,1)}, bf16[352,1024]{1,0:T(8,128)(2,1)S(1)}, u32[]{:S(2)}, u32[]{:S(2)}) %collective-permute-start.14) | collective-permute-done | bytes 720928 | tf_op jit(solution)/shard_map/ppermute | solution.py:622
  104.3 2.0 %pack.20 = (bf16[336,1024]{1,0:T(8,128)(2,1)}, bf16[288,1024]{1,0:T(8,128)(2,1)}) custom-call(s32[2]{0:T(128)S(1)} %pad_add_fusion.flag, s32[4]{0:T(128)S(1)} %gather_fusion, f32[2,1920,1024]{2,1,0:T(8,128)} %refs_0_.27, f32[2,1920,1024]{2,1,0:T(8,128)} %refs_1_.27, f32[2,1920,1024]{2,1,0:T(8,128)} %refs_2_.27, ...), custom_call_target="tpu_custom_call" | custom-call | bytes 3538944 | tf_op jit(solution)/shard_map/pack/pallas_call | solution.py:151
  106.3 1.9 %collective-permute-start.19 = (bf16[336,1024]{1,0:T(8,128)(2,1)}, bf16[336,1024]{1,0:T(8,128)(2,1)S(1)}, u32[]{:S(2)}, u32[]{:S(2)}) collective-permute-start(bf16[336,1024]{1,0:T(8,128)(2,1)} %get-tuple-element.86.refs_2_), channel_id=1, source_target_pairs={{0,8},{8,24},{24,16},{16,0},{1,9},{9,25},{25,17},{17,1},{2,10},{10... | collective-permute-start | bytes 2064392 | tf_op jit(solution)/shard_map/ppermute | solution.py:622
  108.4 1.6 collective-permute-start.13
  110.0 2.7 %collective-permute-done.13.refs_1_ = f32[4,4096]{1,0:T(4,128)S(1)} collective-permute-done((f32[4,4096]{1,0:T(4,128)S(1)}, f32[4,4096]{1,0:T(4,128)S(1)}, u32[]{:S(2)}, u32[]{:S(2)}) %collective-permute-start.13) | collective-permute-done | bytes 65568 | tf_op jit(solution)/shard_map/ppermute | solution.py:318
  112.7 2.3 %collective-permute-done.18.refs_4_.refs_7_ = bf16[288,1024]{1,0:T(8,128)(2,1)} collective-permute-done((bf16[288,1024]{1,0:T(8,128)(2,1)}, bf16[288,1024]{1,0:T(8,128)(2,1)}, u32[]{:S(2)}, u32[]{:S(2)}) %collective-permute-start.18) | collective-permute-done | bytes 589856 | tf_op jit(solution)/shard_map/ppermute | solution.py:623
  115.0 2.1 %collective-permute-done.17.refs_3_.refs_6_ = bf16[288,1024]{1,0:T(8,128)(2,1)} collective-permute-done((bf16[288,1024]{1,0:T(8,128)(2,1)}, bf16[288,1024]{1,0:T(8,128)(2,1)}, u32[]{:S(2)}, u32[]{:S(2)}) %collective-permute-start.17) | collective-permute-done | bytes 589856 | tf_op jit(solution)/shard_map/ppermute | solution.py:622
  117.0 3.0 %pack.21 = (bf16[288,1024]{1,0:T(8,128)(2,1)}, bf16[288,1024]{1,0:T(8,128)(2,1)}) custom-call(s32[2]{0:T(128)S(1)} %pad_add_fusion.flag, s32[4]{0:T(128)S(1)} %gather_fusion, f32[2,1920,1024]{2,1,0:T(8,128)} %refs_0_.27, f32[2,1920,1024]{2,1,0:T(8,128)} %refs_1_.27, f32[2,1920,1024]{2,1,0:T(8,128)} %refs_2_.27, ...), custom_call_target="tpu_custom_call" | custom-call | bytes 3538944 | tf_op jit(solution)/shard_map/pack/pallas_call | solution.py:151
  120.0 1.5 collective-permute-start.22
  123.9 3.7 %collective-permute-done.20.refs_4_.refs_9_ = bf16[288,1024]{1,0:T(8,128)(2,1)} collective-permute-done((bf16[288,1024]{1,0:T(8,128)(2,1)}, bf16[288,1024]{1,0:T(8,128)(2,1)}, u32[]{:S(2)}, u32[]{:S(2)}) %collective-permute-start.20) | collective-permute-done | bytes 589856 | tf_op jit(solution)/shard_map/ppermute | solution.py:623
  127.6 4.1 %collective-permute-done.19.refs_3_.refs_5_.refs_8_ = bf16[336,1024]{1,0:T(8,128)(2,1)S(1)} collective-permute-done((bf16[336,1024]{1,0:T(8,128)(2,1)}, bf16[336,1024]{1,0:T(8,128)(2,1)S(1)}, u32[]{:S(2)}, u32[]{:S(2)}) %collective-permute-start.19) | collective-permute-done | bytes 688160 | tf_op jit(solution)/shard_map/ppermute | solution.py:622
  132.4 1.8 %pack.22 = (bf16[288,1024]{1,0:T(8,128)(2,1)S(1)}, bf16[288,1024]{1,0:T(8,128)(2,1)S(1)}) custom-call(s32[2]{0:T(128)S(1)} %pad_add_fusion.flag, s32[4]{0:T(128)S(1)} %gather_fusion, f32[2,1920,1024]{2,1,0:T(8,128)} %refs_0_.27, f32[2,1920,1024]{2,1,0:T(8,128)} %refs_1_.27, f32[2,1920,1024]{2,1,0:T(8,128)} %refs_2_.27, ...), custom_call_target="tpu_custom_call" | custom-call | bytes 3538944 | tf_op jit(solution)/shard_map/pack/pallas_call | solution.py:151
  134.2 1.5 collective-permute-start.26
  136.4 1.2 collect.1
  139.8 6.8 %patch.3 = (f32[1920,1024]{1,0:T(8,128)}, f32[1920,1024]{1,0:T(8,128)}, f32[1920,1024]{1,0:T(8,128)}) custom-call(s32[2]{0:T(128)S(1)} %pad_add_fusion.1.info, bf16[1920,64]{1,0:T(8,128)(2,1)S(1)} %get-tuple-element.93.hid_ref.refs_3_, bf16[64,1024]{1,0:T(8,128)(2,1)S(1)} %get-tuple-element.94.out_ref, ...), custom_call_target="tpu_custom_call", output_to_operand_aliasing={{0}: (11, {}), {1}: (12, {}), {2}: (13, {})} | custom-call | flops 100663296 | bytes 14155776 | tf_op jit(solution)/shard_map/patch/pallas_call | solution.py:537
  146.5 1.9 %pack.23 = (bf16[288,1024]{1,0:T(8,128)(2,1)S(1)}, bf16[288,1024]{1,0:T(8,128)(2,1)S(1)}) custom-call(s32[2]{0:T(128)S(1)} %pad_add_fusion.flag, s32[4]{0:T(128)S(1)} %gather_fusion, f32[2,1920,1024]{2,1,0:T(8,128)} %refs_0_.27, f32[2,1920,1024]{2,1,0:T(8,128)} %refs_1_.27, f32[2,1920,1024]{2,1,0:T(8,128)} %refs_2_.27, ...), custom_call_target="tpu_custom_call" | custom-call | bytes 3538944 | tf_op jit(solution)/shard_map/pack/pallas_call | solution.py:151
  148.5 2.0 %collective-permute-start.23 = (bf16[288,1024]{1,0:T(8,128)(2,1)S(1)}, bf16[288,1024]{1,0:T(8,128)(2,1)S(1)}, u32[]{:S(2)}, u32[]{:S(2)}) collective-permute-start(bf16[288,1024]{1,0:T(8,128)(2,1)S(1)} %get-tuple-element.100.refs_6_.refs_17_), channel_id=1, source_target_pairs={{0,8},{8,24},{24,16},{16,0},{1,9},{9,25},{25,17},{17,1},{2,10},{10... | collective-permute-start | bytes 1769480 | tf_op jit(solution)/shard_map/ppermute | solution.py:622
  151.3 1.5 collective-permute-done.26.refs_13_
  152.8 4.2 %collective-permute-done.25.refs_12_ = bf16[288,1024]{1,0:T(8,128)(2,1)S(1)} collective-permute-done((bf16[288,1024]{1,0:T(8,128)(2,1)S(1)}, bf16[288,1024]{1,0:T(8,128)(2,1)S(1)}, u32[]{:S(2)}, u32[]{:S(2)}) %collective-permute-start.25) | collective-permute-done | bytes 589856 | tf_op jit(solution)/shard_map/ppermute | solution.py:622
  157.8 14.7 %patch.4 = (f32[1920,1024]{1,0:T(8,128)}, f32[1920,1024]{1,0:T(8,128)}, f32[1920,1024]{1,0:T(8,128)}) custom-call(s32[2]{0:T(128)S(1)} %pad_add_fusion.1.info, bf16[1920,64]{1,0:T(8,128)(2,1)S(1)} %get-tuple-element.93.hid_ref.refs_3_, bf16[64,1024]{1,0:T(8,128)(2,1)S(1)} %get-tuple-element.94.out_ref, ...), custom_call_target="tpu_custom_call", output_to_operand_aliasing={{0}: (17, {}), {1}: (18, {}), {2}: (19, {})} | custom-call | flops 176160768 | bytes 24772608 | tf_op jit(solution)/shard_map/patch/pallas_call | solution.py:537
  172.5 2.7 %patch.5 = (f32[1920,1024]{1,0:T(8,128)}, f32[1920,1024]{1,0:T(8,128)}, f32[1920,1024]{1,0:T(8,128)}) custom-call(s32[2]{0:T(128)S(1)} %pad_add_fusion.1.info, bf16[1920,64]{1,0:T(8,128)(2,1)S(1)} %get-tuple-element.93.hid_ref.refs_3_, bf16[64,1024]{1,0:T(8,128)(2,1)S(1)} %get-tuple-element.94.out_ref, ...), custom_call_target="tpu_custom_call", output_to_operand_aliasing={{0}: (5, {}), {1}: (6, {}), {2}: (7, {})} | custom-call | flops 25165824 | bytes 3538944 | tf_op jit(solution)/shard_map/patch/pallas_call | solution.py:537
  (95 shorter events, 14.8 us)
Async XLA Ops:
  7.8 20.0 %collective-permute-start.1 = (bf16[288,1024]{1,0:T(8,128)(2,1)}, bf16[288,1024]{1,0:T(8,128)(2,1)S(1)}, u32[]{:S(2)}, u32[]{:S(2)}) collective-permute-start(bf16[288,1024]{1,0:T(8,128)(2,1)} %get-tuple-element.61), channel_id=1, source_target_pairs={{8,0},{24,8},{16,24},{0,16},{9,1},{25,9},{17,25},{1,17},{10,2},{26... | collective-permute-start | bytes 1769480 | tf_op jit(solution)/shard_map/ppermute | solution.py:623
  9.4 5.8 %copy-start.23 = (bf16[1,2,4096]{2,1,0:T(2,128)(2,1)S(1)}, bf16[1,2,4096]{2,1,0:T(2,128)(2,1)}, u32[]{:S(2)}) copy-start(bf16[1,2,4096]{2,1,0:T(2,128)(2,1)} %param.11) | copy-start | bytes 49156
  9.4 5.8 %copy-start.24 = (bf16[1,2,4096]{2,1,0:T(2,128)(2,1)S(1)}, bf16[1,2,4096]{2,1,0:T(2,128)(2,1)}, u32[]{:S(2)}) copy-start(bf16[1,2,4096]{2,1,0:T(2,128)(2,1)} %param.12) | copy-start | bytes 49156
  9.4 18.4 %collective-permute-start = (bf16[288,1024]{1,0:T(8,128)(2,1)S(1)}, bf16[288,1024]{1,0:T(8,128)(2,1)S(1)}, u32[]{:S(2)}, u32[]{:S(2)}) collective-permute-start(bf16[288,1024]{1,0:T(8,128)(2,1)S(1)} %get-tuple-element.59.refs_3_), channel_id=1, source_target_pairs={{0,8},{8,24},{24,16},{16,0},{1,9},{9,25},{25,17},{17,1},{2,10},{10... | collective-permute-start | bytes 1769480 | tf_op jit(solution)/shard_map/ppermute | solution.py:622
  13.1 24.9 %collective-permute-start.3 = (bf16[288,1024]{1,0:T(8,128)(2,1)}, bf16[288,1024]{1,0:T(8,128)(2,1)S(1)}, u32[]{:S(2)}, u32[]{:S(2)}) collective-permute-start(bf16[288,1024]{1,0:T(8,128)(2,1)} %get-tuple-element.64), channel_id=1, source_target_pairs={{8,0},{24,8},{16,24},{0,16},{9,1},{25,9},{17,25},{1,17},{10,2},{26... | collective-permute-start | bytes 1769480 | tf_op jit(solution)/shard_map/ppermute | solution.py:623
  14.7 23.6 %collective-permute-start.2 = (bf16[288,1024]{1,0:T(8,128)(2,1)}, bf16[288,1024]{1,0:T(8,128)(2,1)S(1)}, u32[]{:S(2)}, u32[]{:S(2)}) collective-permute-start(bf16[288,1024]{1,0:T(8,128)(2,1)} %get-tuple-element.60.refs_2_), channel_id=1, source_target_pairs={{0,8},{8,24},{24,16},{16,0},{1,9},{9,25},{25,17},{17,1},{2,10},{10... | collective-permute-start | bytes 1769480 | tf_op jit(solution)/shard_map/ppermute | solution.py:622
  28.9 21.5 %collective-permute-start.5 = (bf16[288,1024]{1,0:T(8,128)(2,1)S(1)}, bf16[288,1024]{1,0:T(8,128)(2,1)S(1)}, u32[]{:S(2)}, u32[]{:S(2)}) collective-permute-start(bf16[288,1024]{1,0:T(8,128)(2,1)S(1)} %get-tuple-element.67), channel_id=1, source_target_pairs={{8,0},{24,8},{16,24},{0,16},{9,1},{25,9},{17,25},{1,17},{10,2},{26... | collective-permute-start | bytes 1769480 | tf_op jit(solution)/shard_map/ppermute | solution.py:623
  30.4 20.6 %collective-permute-start.4 = (bf16[288,1024]{1,0:T(8,128)(2,1)S(1)}, bf16[288,1024]{1,0:T(8,128)(2,1)S(1)}, u32[]{:S(2)}, u32[]{:S(2)}) collective-permute-start(bf16[288,1024]{1,0:T(8,128)(2,1)S(1)} %get-tuple-element.62.refs_0_), channel_id=1, source_target_pairs={{0,8},{8,24},{24,16},{16,0},{1,9},{9,25},{25,17},{17,1},{2,10},{10... | collective-permute-start | bytes 1769480 | tf_op jit(solution)/shard_map/ppermute | solution.py:622
  38.1 1.1 copy-start.7
  39.2 23.4 %collective-permute-start.7 = (bf16[288,1024]{1,0:T(8,128)(2,1)S(1)}, bf16[288,1024]{1,0:T(8,128)(2,1)S(1)}, u32[]{:S(2)}, u32[]{:S(2)}) collective-permute-start(bf16[288,1024]{1,0:T(8,128)(2,1)S(1)} %get-tuple-element.70), channel_id=1, source_target_pairs={{8,0},{24,8},{16,24},{0,16},{9,1},{25,9},{17,25},{1,17},{10,2},{26... | collective-permute-start | bytes 1769480 | tf_op jit(solution)/shard_map/ppermute | solution.py:623
  40.7 22.8 %collective-permute-start.6 = (bf16[288,1024]{1,0:T(8,128)(2,1)S(1)}, bf16[288,1024]{1,0:T(8,128)(2,1)S(1)}, u32[]{:S(2)}, u32[]{:S(2)}) collective-permute-start(bf16[288,1024]{1,0:T(8,128)(2,1)S(1)} %get-tuple-element.65.refs_1_), channel_id=1, source_target_pairs={{0,8},{8,24},{24,16},{16,0},{1,9},{9,25},{25,17},{17,1},{2,10},{10... | collective-permute-start | bytes 1769480 | tf_op jit(solution)/shard_map/ppermute | solution.py:622
  51.8 24.0 %collective-permute-start.9 = (bf16[288,1024]{1,0:T(8,128)(2,1)S(1)}, bf16[288,1024]{1,0:T(8,128)(2,1)S(1)}, u32[]{:S(2)}, u32[]{:S(2)}) collective-permute-start(bf16[288,1024]{1,0:T(8,128)(2,1)S(1)} %get-tuple-element.73), channel_id=1, source_target_pairs={{8,0},{24,8},{16,24},{0,16},{9,1},{25,9},{17,25},{1,17},{10,2},{26... | collective-permute-start | bytes 1769480 | tf_op jit(solution)/shard_map/ppermute | solution.py:623
  53.4 22.8 %collective-permute-start.8 = (bf16[288,1024]{1,0:T(8,128)(2,1)S(1)}, bf16[288,1024]{1,0:T(8,128)(2,1)S(1)}, u32[]{:S(2)}, u32[]{:S(2)}) collective-permute-start(bf16[288,1024]{1,0:T(8,128)(2,1)S(1)} %get-tuple-element.68.refs_1_), channel_id=1, source_target_pairs={{0,8},{8,24},{24,16},{16,0},{1,9},{9,25},{25,17},{17,1},{2,10},{10... | collective-permute-start | bytes 1769480 | tf_op jit(solution)/shard_map/ppermute | solution.py:622
  62.6 2.9 %copy-start.13 = (bf16[288,1024]{1,0:T(8,128)(2,1)}, bf16[288,1024]{1,0:T(8,128)(2,1)S(1)}, u32[]{:S(2)}) copy-start(bf16[288,1024]{1,0:T(8,128)(2,1)S(1)} %collective-permute-done.7.refs_4_.refs_7_) | copy-start | bytes 1769476
  63.6 1.9 %copy-start.15 = (bf16[288,1024]{1,0:T(8,128)(2,1)}, bf16[288,1024]{1,0:T(8,128)(2,1)S(1)}, u32[]{:S(2)}) copy-start(bf16[288,1024]{1,0:T(8,128)(2,1)S(1)} %collective-permute-done.6.refs_3_.refs_6_) | copy-start | bytes 1769476
  65.5 22.1 %collective-permute-start.12 = (bf16[288,1024]{1,0:T(8,128)(2,1)}, bf16[288,1024]{1,0:T(8,128)(2,1)}, u32[]{:S(2)}, u32[]{:S(2)}) collective-permute-start(bf16[288,1024]{1,0:T(8,128)(2,1)} %get-tuple-element.81), channel_id=1, source_target_pairs={{8,0},{24,8},{16,24},{0,16},{9,1},{25,9},{17,25},{1,17},{10,2},{26... | collective-permute-start | bytes 1769480 | tf_op jit(solution)/shard_map/ppermute | solution.py:623
  67.0 21.9 %collective-permute-start.11 = (bf16[288,1024]{1,0:T(8,128)(2,1)}, bf16[288,1024]{1,0:T(8,128)(2,1)}, u32[]{:S(2)}, u32[]{:S(2)}) collective-permute-start(bf16[288,1024]{1,0:T(8,128)(2,1)} %get-tuple-element.71.refs_1_), channel_id=1, source_target_pairs={{0,8},{8,24},{24,16},{16,0},{1,9},{9,25},{25,17},{17,1},{2,10},{10... | collective-permute-start | bytes 1769480 | tf_op jit(solution)/shard_map/ppermute | solution.py:622
  75.8 2.5 %copy-start.18 = (bf16[288,1024]{1,0:T(8,128)(2,1)}, bf16[288,1024]{1,0:T(8,128)(2,1)S(1)}, u32[]{:S(2)}) copy-start(bf16[288,1024]{1,0:T(8,128)(2,1)S(1)} %collective-permute-done.9.refs_4_.refs_1_) | copy-start | bytes 1769476
  76.2 2.1 %copy-start.20 = (bf16[288,1024]{1,0:T(8,128)(2,1)}, bf16[288,1024]{1,0:T(8,128)(2,1)S(1)}, u32[]{:S(2)}) copy-start(bf16[288,1024]{1,0:T(8,128)(2,1)S(1)} %collective-permute-done.8.refs_3_.refs_0_) | copy-start | bytes 1769476
  78.3 26.0 %collective-permute-start.14 = (bf16[352,1024]{1,0:T(8,128)(2,1)}, bf16[352,1024]{1,0:T(8,128)(2,1)S(1)}, u32[]{:S(2)}, u32[]{:S(2)}) collective-permute-start(bf16[352,1024]{1,0:T(8,128)(2,1)} %get-tuple-element.78.refs_1_), channel_id=1, source_target_pairs={{0,8},{8,24},{24,16},{16,0},{1,9},{9,25},{25,17},{17,1},{2,10},{10... | collective-permute-start | bytes 2162696 | tf_op jit(solution)/shard_map/ppermute | solution.py:622
  81.2 21.0 %collective-permute-start.15 = (bf16[336,1024]{1,0:T(8,128)(2,1)}, bf16[336,1024]{1,0:T(8,128)(2,1)S(1)}, u32[]{:S(2)}, u32[]{:S(2)}) collective-permute-start(bf16[336,1024]{1,0:T(8,128)(2,1)} %get-tuple-element.85), channel_id=1, source_target_pairs={{8,0},{24,8},{16,24},{0,16},{9,1},{25,9},{17,25},{1,17},{10,2},{26... | collective-permute-start | bytes 2064392 | tf_op jit(solution)/shard_map/ppermute | solution.py:623
  91.8 23.1 %collective-permute-start.18 = (bf16[288,1024]{1,0:T(8,128)(2,1)}, bf16[288,1024]{1,0:T(8,128)(2,1)}, u32[]{:S(2)}, u32[]{:S(2)}) collective-permute-start(bf16[288,1024]{1,0:T(8,128)(2,1)} %get-tuple-element.89), channel_id=1, source_target_pairs={{8,0},{24,8},{16,24},{0,16},{9,1},{25,9},{17,25},{1,17},{10,2},{26... | collective-permute-start | bytes 1769480 | tf_op jit(solution)/shard_map/ppermute | solution.py:623
  93.4 23.7 %collective-permute-start.17 = (bf16[288,1024]{1,0:T(8,128)(2,1)}, bf16[288,1024]{1,0:T(8,128)(2,1)}, u32[]{:S(2)}, u32[]{:S(2)}) collective-permute-start(bf16[288,1024]{1,0:T(8,128)(2,1)} %get-tuple-element.82.refs_2_), channel_id=1, source_target_pairs={{0,8},{8,24},{24,16},{16,0},{1,9},{9,25},{25,17},{17,1},{2,10},{10... | collective-permute-start | bytes 1769480 | tf_op jit(solution)/shard_map/ppermute | solution.py:622
  93.9 6.0 %collective-permute-start.10 = (f32[8,4096]{1,0:T(8,128)S(1)}, f32[8,4096]{1,0:T(8,128)S(1)}, u32[]{:S(2)}, u32[]{:S(2)}) collective-permute-start(f32[8,4096]{1,0:T(8,128)S(1)} %get-tuple-element.80), channel_id=1, source_target_pairs={{0,4},{2,6},{4,0},{6,2},{1,5},{3,7},{5,1},{7,3},{8,12},{10,14},{12... | collective-permute-start | bytes 393224 | tf_op jit(solution)/shard_map/ppermute | solution.py:318
  102.2 34.1 %copy-start.1 = (bf16[336,1024]{1,0:T(8,128)(2,1)}, bf16[336,1024]{1,0:T(8,128)(2,1)S(1)}, u32[]{:S(2)}) copy-start(bf16[336,1024]{1,0:T(8,128)(2,1)S(1)} %collective-permute-done.15.refs_4_.refs_6_.refs_5_) | copy-start | bytes 2064388
  104.3 32.1 %copy-start = (bf16[352,1024]{1,0:T(8,128)(2,1)}, bf16[352,1024]{1,0:T(8,128)(2,1)S(1)}, u32[]{:S(2)}) copy-start(bf16[352,1024]{1,0:T(8,128)(2,1)S(1)} %collective-permute-done.14.refs_3_.refs_4_) | copy-start | bytes 2162692
  106.3 25.3 %collective-permute-start.19 = (bf16[336,1024]{1,0:T(8,128)(2,1)}, bf16[336,1024]{1,0:T(8,128)(2,1)S(1)}, u32[]{:S(2)}, u32[]{:S(2)}) collective-permute-start(bf16[336,1024]{1,0:T(8,128)(2,1)} %get-tuple-element.86.refs_2_), channel_id=1, source_target_pairs={{0,8},{8,24},{24,16},{16,0},{1,9},{9,25},{25,17},{17,1},{2,10},{10... | collective-permute-start | bytes 2064392 | tf_op jit(solution)/shard_map/ppermute | solution.py:622
  108.3 19.4 %collective-permute-start.20 = (bf16[288,1024]{1,0:T(8,128)(2,1)}, bf16[288,1024]{1,0:T(8,128)(2,1)}, u32[]{:S(2)}, u32[]{:S(2)}) collective-permute-start(bf16[288,1024]{1,0:T(8,128)(2,1)} %get-tuple-element.91), channel_id=1, source_target_pairs={{8,0},{24,8},{16,24},{0,16},{9,1},{25,9},{17,25},{1,17},{10,2},{26... | collective-permute-start | bytes 1769480 | tf_op jit(solution)/shard_map/ppermute | solution.py:623
  108.4 4.3 %collective-permute-start.13 = (f32[4,4096]{1,0:T(4,128)S(1)}, f32[4,4096]{1,0:T(4,128)S(1)}, u32[]{:S(2)}, u32[]{:S(2)}) collective-permute-start(f32[4,4096]{1,0:T(4,128)S(1)} %get-tuple-element.84), channel_id=1, source_target_pairs={{0,2},{2,0},{4,6},{6,4},{1,3},{3,1},{5,7},{7,5},{8,10},{10,8},{12,... | collective-permute-start | bytes 196616 | tf_op jit(solution)/shard_map/ppermute | solution.py:318
  120.0 26.5 %collective-permute-start.22 = (bf16[288,1024]{1,0:T(8,128)(2,1)}, bf16[288,1024]{1,0:T(8,128)(2,1)}, u32[]{:S(2)}, u32[]{:S(2)}) collective-permute-start(bf16[288,1024]{1,0:T(8,128)(2,1)} %get-tuple-element.95), channel_id=1, source_target_pairs={{8,0},{24,8},{16,24},{0,16},{9,1},{25,9},{17,25},{1,17},{10,2},{26... | collective-permute-start | bytes 1769480 | tf_op jit(solution)/shard_map/ppermute | solution.py:623
  121.5 25.0 %collective-permute-start.21 = (bf16[288,1024]{1,0:T(8,128)(2,1)}, bf16[288,1024]{1,0:T(8,128)(2,1)}, u32[]{:S(2)}, u32[]{:S(2)}) collective-permute-start(bf16[288,1024]{1,0:T(8,128)(2,1)} %get-tuple-element.90.refs_2_), channel_id=1, source_target_pairs={{0,8},{8,24},{24,16},{16,0},{1,9},{9,25},{25,17},{17,1},{2,10},{10... | collective-permute-start | bytes 1769480 | tf_op jit(solution)/shard_map/ppermute | solution.py:622
  122.1 1.2 collective-permute-start.16
  132.4 4.0 %copy-start.2 = (bf16[336,1024]{1,0:T(8,128)(2,1)}, bf16[336,1024]{1,0:T(8,128)(2,1)S(1)}, u32[]{:S(2)}) copy-start(bf16[336,1024]{1,0:T(8,128)(2,1)S(1)} %collective-permute-done.19.refs_3_.refs_5_.refs_8_) | copy-start | bytes 2064388
  134.2 18.6 %collective-permute-start.26 = (bf16[288,1024]{1,0:T(8,128)(2,1)S(1)}, bf16[288,1024]{1,0:T(8,128)(2,1)S(1)}, u32[]{:S(2)}, u32[]{:S(2)}) collective-permute-start(bf16[288,1024]{1,0:T(8,128)(2,1)S(1)} %get-tuple-element.102), channel_id=1, source_target_pairs={{8,0},{24,8},{16,24},{0,16},{9,1},{25,9},{17,25},{1,17},{10,2},{26... | collective-permute-start | bytes 1769480 | tf_op jit(solution)/shard_map/ppermute | solution.py:623
  135.8 21.2 %collective-permute-start.25 = (bf16[288,1024]{1,0:T(8,128)(2,1)S(1)}, bf16[288,1024]{1,0:T(8,128)(2,1)S(1)}, u32[]{:S(2)}, u32[]{:S(2)}) collective-permute-start(bf16[288,1024]{1,0:T(8,128)(2,1)S(1)} %get-tuple-element.92.refs_7_), channel_id=1, source_target_pairs={{0,8},{8,24},{24,16},{16,0},{1,9},{9,25},{25,17},{17,1},{2,10},{10... | collective-permute-start | bytes 1769480 | tf_op jit(solution)/shard_map/ppermute | solution.py:622
  137.6 1.1 copy-start.4
  137.6 1.2 copy-start.6
  137.6 1.4 copy-start.8
  137.6 1.6 copy-start.10
  137.7 1.7 copy-start.12
  137.7 1.9 %copy-start.14 = (bf16[288,1024]{1,0:T(8,128)(2,1)S(1)}, bf16[288,1024]{1,0:T(8,128)(2,1)}, u32[]{:S(2)}) copy-start(bf16[288,1024]{1,0:T(8,128)(2,1)} %copy-done.13) | copy-start | bytes 1769476
  137.7 2.1 %copy-start.16 = (bf16[288,1024]{1,0:T(8,128)(2,1)S(1)}, bf16[288,1024]{1,0:T(8,128)(2,1)}, u32[]{:S(2)}) copy-start(bf16[288,1024]{1,0:T(8,128)(2,1)} %copy-done.15) | copy-start | bytes 1769476
  148.4 2.8 %copy-start.17 = (bf16[288,1024]{1,0:T(8,128)(2,1)}, bf16[288,1024]{1,0:T(8,128)(2,1)S(1)}, u32[]{:S(2)}) copy-start(bf16[288,1024]{1,0:T(8,128)(2,1)S(1)} %get-tuple-element.100.refs_6_.refs_17_) | copy-start | bytes 1769476
  148.4 24.1 %collective-permute-start.24 = (bf16[288,1024]{1,0:T(8,128)(2,1)S(1)}, bf16[288,1024]{1,0:T(8,128)(2,1)S(1)}, u32[]{:S(2)}, u32[]{:S(2)}) collective-permute-start(bf16[288,1024]{1,0:T(8,128)(2,1)S(1)} %get-tuple-element.101), channel_id=1, source_target_pairs={{8,0},{24,8},{16,24},{0,16},{9,1},{25,9},{17,25},{1,17},{10,2},{26... | collective-permute-start | bytes 1769480 | tf_op jit(solution)/shard_map/ppermute | solution.py:623
  148.5 24.0 %collective-permute-start.23 = (bf16[288,1024]{1,0:T(8,128)(2,1)S(1)}, bf16[288,1024]{1,0:T(8,128)(2,1)S(1)}, u32[]{:S(2)}, u32[]{:S(2)}) collective-permute-start(bf16[288,1024]{1,0:T(8,128)(2,1)S(1)} %get-tuple-element.100.refs_6_.refs_17_), channel_id=1, source_target_pairs={{0,8},{8,24},{24,16},{16,0},{1,9},{9,25},{25,17},{17,1},{2,10},{10... | collective-permute-start | bytes 1769480 | tf_op jit(solution)/shard_map/ppermute | solution.py:622
  150.5 7.3 %copy-start.19 = (bf16[288,1024]{1,0:T(8,128)(2,1)S(1)}, bf16[288,1024]{1,0:T(8,128)(2,1)}, u32[]{:S(2)}) copy-start(bf16[288,1024]{1,0:T(8,128)(2,1)} %copy-done.18) | copy-start | bytes 1769476
  150.5 7.3 %copy-start.21 = (bf16[288,1024]{1,0:T(8,128)(2,1)S(1)}, bf16[288,1024]{1,0:T(8,128)(2,1)}, u32[]{:S(2)}) copy-start(bf16[288,1024]{1,0:T(8,128)(2,1)} %copy-done.20) | copy-start | bytes 1769476
  152.8 4.2 %copy-start.25 = (bf16[288,1024]{1,0:T(8,128)(2,1)}, bf16[288,1024]{1,0:T(8,128)(2,1)S(1)}, u32[]{:S(2)}) copy-start(bf16[288,1024]{1,0:T(8,128)(2,1)S(1)} %collective-permute-done.26.refs_13_) | copy-start | bytes 1769476
  (6 other events, 5.3 us)

commit v5 on v4

--- a/solution.py
+++ b/solution.py
@@ -11,6 +11,8 @@
 LAG = 2
 MOST_CHUNKS = 20
 TILE = 16
+BUFFERS = 3
+FETCHED = 4
 VMEM = 48 << 20
 
 ANY = pl.BlockSpec(memory_space=pl.ANY)
@@ -64,22 +66,31 @@
     return moves
 
 
-def pack_body(flag, targets, *refs, places, chunk, slabs, passed, counts):
+def pack_body(*refs, places, chunk, slabs, passed, counts):
+    count_flags, count_seen, count_parts, count_after = counts
+    flag, targets = refs[:2] if count_flags else (None, None)
+    refs = refs[count_flags:]
     state = refs[0:3]
-    count_seen, count_parts, count_after = counts
     seen = refs[3 : 3 + count_seen]
-    both = refs[3 + count_seen]
-    parts = refs[4 + count_seen : 4 + count_seen + count_parts]
-    rest = refs[3 + count_seen + (count_parts + 1 if count_parts else 0) + count_after :]
-    sends = rest[:2]
-    held, sem, passed_sem = rest[2:]
-    width = sends[0].shape[1]
+    rest = refs[3 + count_seen :]
+    if count_parts:
+        both, parts, rest = rest[0], rest[1 : 1 + count_parts], rest[1 + count_parts :]
+    sends = rest[count_after : count_after + 2]
+    held, made, sem, out_sem, below_sem = rest[count_after + 2 :]
+    width = held.shape[2]
     size = 3 * chunk
 
     def fetch(j):
         way, k = divmod(j, 3)
         rows = pl.ds(places[way] * chunk, chunk)
         return pltpu.make_async_copy(state[k].at[1, rows], held.at[j], sem.at[j])
+
+    def store(j):
+        way, k = divmod(j, 3)
+        rows = pl.ds(k * chunk, chunk)
+        return pltpu.make_async_copy(
+            made.at[way, rows], sends[way].at[rows], out_sem.at[j]
+        )
 
     def convert():
         for j in range(6):
@@ -87,21 +98,40 @@
         for j in range(6):
             way, k = divmod(j, 3)
             fetch(j).wait()
-            sends[way][pl.ds(k * chunk, chunk)] = held[j].astype(BF16)
+            made[way, pl.ds(k * chunk, chunk)] = held[j].astype(BF16)
+            store(j).start()
+        for j in range(6):
+            store(j).wait()
 
     def relay(way):
         rows = pl.ds(0, size)
         return pltpu.make_async_copy(seen[way].at[rows], sends[way].at[rows], sem.at[way])
 
-    def hand_on(way):
-        rows = pl.ds(size, passed[way])
-        return pltpu.make_async_copy(
-            seen[way].at[rows], sends[way].at[rows], passed_sem.at[way]
-        )
+    def below(way):
+        count = passed[way] or sends[way].shape[0] - size
+        rows = pl.ds(size, count)
+        origin = seen[way].at[rows] if passed[way] else made.at[way, rows]
+        return pltpu.make_async_copy(origin, sends[way].at[rows], below_sem.at[way])
 
     for way in range(2):
-        if passed[way]:
-            hand_on(way).start()
+        if slabs[way]:
+            n = targets.shape[0]
+            tokens, features = both.shape[0], both.shape[1] // 2
+            keep = flag[1] == 0
+            moves = column_pieces([part.shape[1] for part in parts], width)
+            for part, begin, piece, to, run in moves:
+                units = parts[part][:, begin : begin + run]
+                made[way, pl.ds(size + piece * tokens, tokens), pl.ds(to, run)] = (
+                    jnp.where(keep, units, jnp.zeros_like(units))
+                )
+            row = size + (1 + moves[-1][2]) * tokens
+            for far in range(slabs[way], 0, -1):
+                target = targets[far if way == 0 else n - far]
+                slab = pl.ds(pl.multiple_of(features + target * width, 128), width)
+                made[way, pl.ds(row, tokens)] = both[:, slab]
+                row += tokens
+        if slabs[way] or passed[way]:
+            below(way).start()
 
     if not seen:
         convert()
@@ -115,60 +145,42 @@
             for way in range(2):
                 relay(way).wait()
 
-    n = targets.shape[0]
     for way in range(2):
-        if slabs[way]:
-            tokens, features = both.shape[0], both.shape[1] // 2
-            keep = flag[1] == 0
-            below = size
-            moves = column_pieces([part.shape[1] for part in parts], width)
-            for part, begin, piece, to, run in moves:
-                units = parts[part][:, begin : begin + run]
-                rows = pl.ds(size + piece * tokens, tokens)
-                sends[way][rows, pl.ds(to, run)] = jnp.where(
-                    keep, units, jnp.zeros_like(units)
-                )
-            below += (1 + moves[-1][2]) * tokens
-            for far in range(slabs[way], 0, -1):
-                target = targets[far if way == 0 else n - far]
-                slab = pl.ds(pl.multiple_of(features + target * width, 128), width)
-                sends[way][pl.ds(below, tokens)] = both[:, slab]
-                below += tokens
-
-    for way in range(2):
-        if passed[way]:
-            hand_on(way).wait()
-
-
-def pack(flag, targets, state, seen, parcel, after, places, chunk, slabs, passed):
+        if slabs[way] or passed[way]:
+            below(way).wait()
+
+
+def pack(flags, state, seen, parcel, after, places, chunk, slabs, passed):
     width = state[0].shape[2]
     extra = list(passed)
     if parcel:
         tokens = parcel[0].shape[0]
         pieces = -(-sum(part.shape[1] for part in parcel[1:]) // width)
         extra = [tokens * (pieces + count) if count else 0 for count in slabs]
-    counts = (len(seen), max(len(parcel) - 1, 0), len(after))
+    counts = (len(flags), len(seen), max(len(parcel) - 1, 0), len(after))
     return pl.pallas_call(
         functools.partial(
             pack_body, places=places, chunk=chunk, slabs=slabs, passed=passed, counts=counts
         ),
-        in_specs=[SMEM, SMEM]
+        in_specs=[SMEM] * len(flags)
         + [ANY] * (3 + len(seen))
         + [WHOLE] * len(parcel)
         + [ANY] * len(after),
-        out_specs=[WHOLE, WHOLE],
+        out_specs=[ANY, ANY],
         out_shape=[
             jax.ShapeDtypeStruct((3 * chunk + more, width), BF16) for more in extra
         ],
         scratch_shapes=[
             pltpu.VMEM((6, chunk, width), F32),
+            pltpu.VMEM((2, 3 * chunk + max(extra), width), BF16),
+            pltpu.SemaphoreType.DMA((6,)),
             pltpu.SemaphoreType.DMA((6,)),
             pltpu.SemaphoreType.DMA((2,)),
         ],
         compiler_params=PARAMS,
         cost_estimate=cost(0, 2 * 3 * chunk * width * 6),
         name="pack",
-    )(flag, targets, *state, *seen, *parcel, *after)
+    )(*flags, *state, *seen, *parcel, *after)
 
 
 def beside_body(*refs):
@@ -195,57 +207,56 @@
     return lax.dot_general(a, b, (((1,), (1,)), ((), ())), preferred_element_type=F32)
 
 
-def layer_body(both, gate_ref, up_ref, down_ref, *refs, resumed):
+def layer_body(both, *refs, resumed, tile, first, count):
+    weights = refs[:3]
     hidden_ref, sum_ref = refs[-2:]
-    features = gate_ref.shape[0]
-    tile = gate_ref.shape[1]
-    x, dy = both[:, :features], both[:, features:]
-    w_gate, w_up = gate_ref[...], up_ref[...]
+    features = weights[0].shape[0]
+    rows = both.shape[0]
     joined = tile % 128 == 0
-    if joined:
-        w_both = jnp.concatenate([w_gate, w_up], axis=1)
-        gate_up = jnp.dot(x, w_both, preferred_element_type=F32)
-        gate, up = gate_up[:, :tile], gate_up[:, tile:]
-    else:
-        gate = jnp.dot(x, w_gate, preferred_element_type=F32)
-        up = jnp.dot(x, w_up, preferred_element_type=F32)
-    d_hidden = by_rows(dy, down_ref[...])
-    sig = 1.0 / (1.0 + jnp.exp(-gate))
-    hidden_ref[...] = (gate * sig * up).astype(BF16)
-    d_gate = (d_hidden * up * sig * (1.0 + gate * (1.0 - sig))).astype(BF16)
-    d_up = (d_hidden * gate * sig).astype(BF16)
-    if joined:
-        term = by_rows(jnp.concatenate([d_gate, d_up], axis=1), w_both)
-    else:
-        term = by_rows(d_gate, w_gate) + by_rows(d_up, w_up)
-
-    @pl.when(pl.program_id(0) == 0)
-    def _():
-        sum_ref[...] = (refs[0][...] + term) if resumed else term
-
-    @pl.when(pl.program_id(0) > 0)
-    def _():
-        sum_ref[...] += term
+    sum_ref[...] = refs[3][...] if resumed else jnp.zeros_like(sum_ref)
+
+    def step(gate_ref, up_ref, down_ref, hidden):
+        x, dy = both[:, :features], both[:, features:]
+        w_gate, w_up = gate_ref[...], up_ref[...]
+        if joined:
+            w_both = jnp.concatenate([w_gate, w_up], axis=1)
+            gate_up = jnp.dot(x, w_both, preferred_element_type=F32)
+            gate, up = gate_up[:, :tile], gate_up[:, tile:]
+        else:
+            gate = jnp.dot(x, w_gate, preferred_element_type=F32)
+            up = jnp.dot(x, w_up, preferred_element_type=F32)
+        d_hidden = by_rows(dy, down_ref[...])
+        sig = 1.0 / (1.0 + jnp.exp(-gate))
+        hidden[...] = (gate * sig * up).astype(BF16)
+        d_gate = (d_hidden * up * sig * (1.0 + gate * (1.0 - sig))).astype(BF16)
+        d_up = (d_hidden * gate * sig).astype(BF16)
+        if joined:
+            sum_ref[...] += by_rows(jnp.concatenate([d_gate, d_up], axis=1), w_both)
+        else:
+            sum_ref[...] += by_rows(d_gate, w_gate) + by_rows(d_up, w_up)
+
+    deep = pl.Buffered(min(BUFFERS, count + 1))
+    across = pl.BlockSpec((features, tile), lambda i: (0, first + i), pipeline_mode=deep)
+    pltpu.emit_pipeline(
+        step,
+        grid=(count,),
+        in_specs=[
+            across,
+            across,
+            pl.BlockSpec((tile, features), lambda i: (first + i, 0), pipeline_mode=deep),
+        ],
+        out_specs=[pl.BlockSpec((rows, tile), lambda i: (0, i))],
+    )(*weights, hidden_ref)
 
 
 def layer(both, w_gate, w_up, w_down, partial_sum, after, tile, first, count):
     rows = both.shape[0]
     features = w_gate.shape[0]
-    across = pl.BlockSpec((features, tile), lambda i: (0, first + i))
     resumed = partial_sum is not None
-    fixed = pl.BlockSpec((rows, features), lambda i: (0, 0))
     return pl.pallas_call(
-        functools.partial(layer_body, resumed=resumed),
-        grid=(count,),
-        in_specs=[
-            pl.BlockSpec(both.shape, lambda i: (0, 0)),
-            across,
-            across,
-            pl.BlockSpec((tile, features), lambda i: (first + i, 0)),
-        ]
-        + [fixed] * resumed
-        + [ANY] * len(after),
-        out_specs=[pl.BlockSpec((rows, tile), lambda i: (0, i)), fixed],
+        functools.partial(layer_body, resumed=resumed, tile=tile, first=first, count=count),
+        in_specs=[WHOLE] + [ANY] * 3 + [WHOLE] * resumed + [ANY] * len(after),
+        out_specs=[ANY, WHOLE],
         out_shape=[
             jax.ShapeDtypeStruct((rows, count * tile), BF16),
             jax.ShapeDtypeStruct((rows, features), F32),
@@ -409,7 +420,10 @@
                 m_ref[0, here], a_ref[0, here], b_ref[0, here], total[here], healthy
             )
 
-    old = pl.BlockSpec((1, block, width), lambda i: (0, first + i, 0))
+    deep = pl.Buffered(min(BUFFERS, count + 1))
+    old = pl.BlockSpec(
+        (1, block, width), lambda i: (0, first + i, 0), pipeline_mode=deep
+    )
     new = pl.BlockSpec((block, width), lambda i: (first + i, 0))
 
     @pl.when(info[0] == 0)
@@ -469,7 +483,7 @@
 
     def fetch(j):
         rows = got[j].at[pl.ds(0, 3 * chunk)]
-        return pltpu.make_async_copy(rows, held.at[j % 2], in_sem.at[j % 2])
+        return pltpu.make_async_copy(rows, held.at[j % FETCHED], in_sem.at[j % FETCHED])
 
     def first_row(j):
         step, forward = arrivals[j]
@@ -480,7 +494,9 @@
 
     def store(j, k):
         return pltpu.make_async_copy(
-            made.at[j % 2, k], news[k].at[pl.ds(first_row(j), chunk)], out_sem.at[j % 2, k]
+            made.at[j % BUFFERS, k],
+            news[k].at[pl.ds(first_row(j), chunk)],
+            out_sem.at[j % BUFFERS, k],
         )
 
     def valid(j):
@@ -495,17 +511,17 @@
 
     @pl.when(info[0] == 1)
     def _():
-        fetch(0).start()
+        for j in range(min(FETCHED - 1, count)):
+            fetch(j).start()
         for j in range(count):
-            slot = j % 2
-            if j + 1 < count:
-                fetch(j + 1).start()
+            if j + FETCHED - 1 < count:
+                fetch(j + FETCHED - 1).start()
             fetch(j).wait()
-            if j >= 2:
-                finish(j - 2)
+            if j >= BUFFERS:
+                finish(j - BUFFERS)
 
             @pl.when(valid(j))
-            def _(j=j, slot=slot):
+            def _(j=j, slot=j % FETCHED, out_slot=j % BUFFERS):
                 first = first_row(j)
 
                 units = hid_ref[pl.ds(first, chunk)]
@@ -520,12 +536,12 @@
                     ]
                     new = updated(*old, total[pl.ds(base, group)], n - 1.0)
                     for k in range(3):
-                        made[slot, k, pl.ds(base, group)] = new[k]
+                        made[out_slot, k, pl.ds(base, group)] = new[k]
 
                 for k in range(3):
                     store(j, k).start()
 
-        for j in range(max(count - 2, 0), count):
+        for j in range(max(count - BUFFERS, 0), count):
             finish(j)
 
 
@@ -542,11 +558,11 @@
         out_specs=[ANY] * 3,
         out_shape=[shape] * 3,
         scratch_shapes=[
-            pltpu.VMEM((2, 3 * chunk, width), BF16),
-            pltpu.VMEM((2, 3, chunk, width), F32),
+            pltpu.VMEM((FETCHED, 3 * chunk, width), BF16),
+            pltpu.VMEM((BUFFERS, 3, chunk, width), F32),
             pltpu.VMEM((chunk, width), F32),
-            pltpu.SemaphoreType.DMA((2,)),
-            pltpu.SemaphoreType.DMA((2, 3)),
+            pltpu.SemaphoreType.DMA((FETCHED,)),
+            pltpu.SemaphoreType.DMA((BUFFERS, 3)),
         ],
         input_output_aliases={3 + count + k: k for k in range(3)},
         compiler_params=PARAMS,
@@ -605,8 +621,7 @@
             )
         sends.append(
             pack(
-                flag,
-                targets,
+                (flag, targets) if seen else (),
                 state,
                 seen,
                 parcel,
@@ -678,13 +693,13 @@
         if len(got) == ready and early and len(got) < steps:
             hidden_t, outs = gathered(sent)
             news = update_part(0, early, (hidden_t,))
-            news = patch_to(4, ())
+            news = patch_to(len(got) // 2, ())
     if hidden_t is None:
         hidden_t, outs = gathered(sent)
         early = 0
     news = update_part(early, blocks - early, sent)
-    news = patch_to(steps - 1, sent)
-    news = patch_to(steps, ())
+    for step in (steps - 2, steps - 1, steps):
+        news = patch_to(step, ())
     while not cotangents.done:
         cotangents.advance(sent)
     return (cotangents.value[None], *news)

time: 176 us -> 205 us (1.16)
  the two profiles are of different devices: /device:TPU:16 before, /device:TPU:0 now
where the time goes in v5:
time: 205 us; the launch traced here: 204 us
  Pallas kernels  126 us (61%)
  starting transfers between devices  33.1 us (16%)
  waiting for transfers between devices  21.8 us (11%)
  blocking collectives  16 us (8%)
  between operations  3.36 us (2%)
  local copies, waits for them, and re-layouts  3.27 us (2%)
    pallas_call x12, Pallas kernels, pack(): pl.pallas_call(functools.partial(pack_body, places=places, chunk=chunk, s...  74.4 us
    pallas_call x4, Pallas kernels, layer(): pl.pallas_call(functools.partial(layer_body, resumed=resumed, tile=tile,...  26.7 us
    ppermute x12, starting transfers between devices, send(): lax.ppermute(sends[-1][1], 'replica', backward)  23.1 us
    pallas_call x2, Pallas kernels, update(): pl.pallas_call(functools.partial(update_body, healthy=healthy, block=bloc...  19.9 us
    all_gather x1, blocking collectives, per_device(): both = lax.all_gather(both, ('fsdp', 'tensor'), axis=0, tiled=True)  16 us
    ppermute x3, waiting for transfers between devices, advance(): self.arrived = (lax.ppermute(sent, axis, route),)  11.4 us
    ppermute x12, starting transfers between devices, send(): lax.ppermute(sends[-1][0], 'replica', forward)  8.75 us
    ppermute x12, waiting for transfers between devices, send(): lax.ppermute(sends[-1][0], 'replica', forward)  6.48 us
  transfers between devices with their start and end apart: 27, of which 8 were waited for; matrix products, arithmetic and copies ran while one was open for 2% of the time, Pallas kernels for 60%

profile of v5, /device:TPU:0, one launch (start us, length us, event | category | flops | bytes accessed | tf_op | source)
XLA Modules:
  0.0 203.9 jit_solution(10385004562301572805)
XLA Ops:
  0.6 2.8 %pack.12 = (bf16[288,1024]{1,0:T(8,128)(2,1)S(1)}, bf16[288,1024]{1,0:T(8,128)(2,1)}) custom-call(f32[2,1920,1024]{2,1,0:T(8,128)} %refs_0_.15, f32[2,1920,1024]{2,1,0:T(8,128)} %refs_1_.15, f32[2,1920,1024]{2,1,0:T(8,128)} %refs_2_.35), custom_call_target="tpu_custom_call" | custom-call | bytes 3538944 | tf_op jit(solution)/shard_map/pack/pallas_call | solution.py:161
  3.4 3.0 %collective-permute-start.1 = (bf16[288,1024]{1,0:T(8,128)(2,1)}, bf16[288,1024]{1,0:T(8,128)(2,1)S(1)}, u32[]{:S(2)}, u32[]{:S(2)}) collective-permute-start(bf16[288,1024]{1,0:T(8,128)(2,1)} %get-tuple-element.64), channel_id=1, source_target_pairs={{8,0},{24,8},{16,24},{0,16},{9,1},{25,9},{17,25},{1,17},{10,2},{26... | collective-permute-start | bytes 1769480 | tf_op jit(solution)/shard_map/ppermute | solution.py:638
  6.5 2.4 %pack.13 = (bf16[288,1024]{1,0:T(8,128)(2,1)}, bf16[288,1024]{1,0:T(8,128)(2,1)}) custom-call(f32[2,1920,1024]{2,1,0:T(8,128)} %refs_0_.15, f32[2,1920,1024]{2,1,0:T(8,128)} %refs_1_.15, f32[2,1920,1024]{2,1,0:T(8,128)} %refs_2_.35, bf16[288,1024]{1,0:T(8,128)(2,1)S(1)} %get-tuple-element.62.refs_3_), custom_call_target="tpu_custom_call" | custom-call | bytes 3538944 | tf_op jit(solution)/shard_map/pack/pallas_call | solution.py:161
  8.9 2.0 collective-permute-start.3
  11.7 0.7 fusion.2
  13.0 0.6 gather_fusion
  13.6 16.0 %all-gather = bf16[8,2,8192]{2,1,0:T(2,128)(2,1)} all-gather(bf16[1,2,8192]{2,1,0:T(2,128)(2,1)S(1)} %bitcast.20), channel_id=1, replica_groups=mesh['replica'=4,'fsdp'=4,'tensor'=2] {'fsdp','tensor'}, dimensions={0}, use_global_device_ids=true | all-gather | bytes 294912 | tf_op jit(solution)/shard_map/all_gather | solution.py:646
  29.6 1.0 reshape.69.refs_7_.both
  30.7 0.9 pack.14
  31.7 1.5 collective-permute-start.5
  33.8 5.7 %layer.4 = (bf16[16,384]{1,0:T(8,128)(2,1)S(1)}, f32[16,4096]{1,0:T(8,128)S(1)}) custom-call(bf16[16,8192]{1,0:T(8,128)(2,1)S(1)} %reshape.69.refs_7_.both, bf16[4096,1920]{1,0:T(8,128)(2,1)} %refs_0_.13, bf16[4096,1920]{1,0:T(8,128)(2,1)} %refs_1_.13, bf16[1920,4096]{1,0:T(8,128)(2,1)} %refs_2_.27, bf16[288,1024]{1,0:T(8,128)(2,1)S(1)} %get-tuple-element.65.refs_3_), custom_call_target="tpu_custom_call" | custom-call | flops 251658240 | bytes 9437184 | tf_op jit(solution)/shard_map/layer/pallas_call | solution.py:256
  39.5 0.9 pack.15
  40.5 3.4 %collective-permute-start.7 = (bf16[288,1024]{1,0:T(8,128)(2,1)S(1)}, bf16[288,1024]{1,0:T(8,128)(2,1)S(1)}, u32[]{:S(2)}, u32[]{:S(2)}) collective-permute-start(bf16[288,1024]{1,0:T(8,128)(2,1)S(1)} %get-tuple-element.73), channel_id=1, source_target_pairs={{8,0},{24,8},{16,24},{0,16},{9,1},{25,9},{17,25},{1,17},{10,2},{26... | collective-permute-start | bytes 1769480 | tf_op jit(solution)/shard_map/ppermute | solution.py:638
  44.0 7.0 %layer.5 = (bf16[16,512]{1,0:T(8,128)(2,1)S(1)}, f32[16,4096]{1,0:T(8,128)S(1)}) custom-call(bf16[16,8192]{1,0:T(8,128)(2,1)S(1)} %reshape.69.refs_7_.both, bf16[4096,1920]{1,0:T(8,128)(2,1)} %refs_0_.13, bf16[4096,1920]{1,0:T(8,128)(2,1)} %refs_1_.13, bf16[1920,4096]{1,0:T(8,128)(2,1)} %refs_2_.27, f32[16,4096]{1,0:T(8,128)S(1)} %get-tuple-element.66.refs_7_.refs_3_, ...), custom_call_target="tpu_custom_call" | custom-call | flops 335544320 | bytes 12582912 | tf_op jit(solution)/shard_map/layer/pallas_call | solution.py:256
  51.3 0.9 pack.16
  52.2 4.2 %collective-permute-start.9 = (bf16[288,1024]{1,0:T(8,128)(2,1)S(1)}, bf16[288,1024]{1,0:T(8,128)(2,1)S(1)}, u32[]{:S(2)}, u32[]{:S(2)}) collective-permute-start(bf16[288,1024]{1,0:T(8,128)(2,1)S(1)} %get-tuple-element.76), channel_id=1, source_target_pairs={{8,0},{24,8},{16,24},{0,16},{9,1},{25,9},{17,25},{1,17},{10,2},{26... | collective-permute-start | bytes 1769480 | tf_op jit(solution)/shard_map/ppermute | solution.py:638
  56.5 7.0 %layer.6 = (bf16[16,512]{1,0:T(8,128)(2,1)S(1)}, f32[16,4096]{1,0:T(8,128)S(1)}) custom-call(bf16[16,8192]{1,0:T(8,128)(2,1)S(1)} %reshape.69.refs_7_.both, bf16[4096,1920]{1,0:T(8,128)(2,1)} %refs_0_.13, bf16[4096,1920]{1,0:T(8,128)(2,1)} %refs_1_.13, bf16[1920,4096]{1,0:T(8,128)(2,1)} %refs_2_.27, f32[16,4096]{1,0:T(8,128)S(1)} %get-tuple-element.69.refs_7_.refs_3_, ...), custom_call_target="tpu_custom_call" | custom-call | flops 335544320 | bytes 12582912 | tf_op jit(solution)/shard_map/layer/pallas_call | solution.py:256
  63.9 1.8 pack.17
  65.7 4.0 %collective-permute-start.12 = (bf16[288,1024]{1,0:T(8,128)(2,1)}, bf16[288,1024]{1,0:T(8,128)(2,1)S(1)}, u32[]{:S(2)}, u32[]{:S(2)}) collective-permute-start(bf16[288,1024]{1,0:T(8,128)(2,1)} %get-tuple-element.84), channel_id=1, source_target_pairs={{8,0},{24,8},{16,24},{0,16},{9,1},{25,9},{17,25},{1,17},{10,2},{26... | collective-permute-start | bytes 1769480 | tf_op jit(solution)/shard_map/ppermute | solution.py:638
  69.8 7.0 %layer.7 = (bf16[16,512]{1,0:T(8,128)(2,1)S(1)}, f32[16,4096]{1,0:T(8,128)S(1)}) custom-call(bf16[16,8192]{1,0:T(8,128)(2,1)S(1)} %reshape.69.refs_7_.both, bf16[4096,1920]{1,0:T(8,128)(2,1)} %refs_0_.13, bf16[4096,1920]{1,0:T(8,128)(2,1)} %refs_1_.13, bf16[1920,4096]{1,0:T(8,128)(2,1)} %refs_2_.27, f32[16,4096]{1,0:T(8,128)S(1)} %get-tuple-element.72.refs_7_.refs_3_, ...), custom_call_target="tpu_custom_call" | custom-call | flops 335544320 | bytes 12582912 | tf_op jit(solution)/shard_map/layer/pallas_call | solution.py:256
  76.9 1.8 pack.18
  78.7 3.2 %collective-permute-start.14 = (bf16[352,1024]{1,0:T(8,128)(2,1)}, bf16[352,1024]{1,0:T(8,128)(2,1)S(1)}, u32[]{:S(2)}, u32[]{:S(2)}) collective-permute-start(bf16[352,1024]{1,0:T(8,128)(2,1)} %get-tuple-element.81.refs_1_), channel_id=1, source_target_pairs={{0,8},{8,24},{24,16},{16,0},{1,9},{9,25},{25,17},{17,1},{2,10},{10... | collective-permute-start | bytes 2162696 | tf_op jit(solution)/shard_map/ppermute | solution.py:637
  81.9 3.9 %collective-permute-done.12.refs_6_.refs_1_ = bf16[288,1024]{1,0:T(8,128)(2,1)S(1)} collective-permute-done((bf16[288,1024]{1,0:T(8,128)(2,1)}, bf16[288,1024]{1,0:T(8,128)(2,1)S(1)}, u32[]{:S(2)}, u32[]{:S(2)}) %collective-permute-start.12) | collective-permute-done | bytes 589856 | tf_op jit(solution)/shard_map/ppermute | solution.py:638
  85.8 3.5 %collective-permute-done.11.refs_5_.refs_0_ = bf16[288,1024]{1,0:T(8,128)(2,1)} collective-permute-done((bf16[288,1024]{1,0:T(8,128)(2,1)}, bf16[288,1024]{1,0:T(8,128)(2,1)}, u32[]{:S(2)}, u32[]{:S(2)}) %collective-permute-start.11) | collective-permute-done | bytes 589856 | tf_op jit(solution)/shard_map/ppermute | solution.py:637
  89.3 19.6 %pack.19 = (bf16[288,1024]{1,0:T(8,128)(2,1)}, bf16[288,1024]{1,0:T(8,128)(2,1)}) custom-call(s32[2]{0:T(128)S(1)} %pad_add_fusion.refs_0_.flag, s32[4]{0:T(128)S(1)} %gather_fusion, f32[2,1920,1024]{2,1,0:T(8,128)} %refs_0_.15, f32[2,1920,1024]{2,1,0:T(8,128)} %refs_1_.15, f32[2,1920,1024]{2,1,0:T(8,128)} %refs_2_.35, ...), custom_call_target="tpu_custom_call" | custom-call | bytes 3538944 | tf_op jit(solution)/shard_map/pack/pallas_call | solution.py:161
  109.0 2.1 %collective-permute-start.18 = (bf16[288,1024]{1,0:T(8,128)(2,1)}, bf16[288,1024]{1,0:T(8,128)(2,1)}, u32[]{:S(2)}, u32[]{:S(2)}) collective-permute-start(bf16[288,1024]{1,0:T(8,128)(2,1)} %get-tuple-element.92), channel_id=1, source_target_pairs={{8,0},{24,8},{16,24},{0,16},{9,1},{25,9},{17,25},{1,17},{10,2},{26... | collective-permute-start | bytes 1769480 | tf_op jit(solution)/shard_map/ppermute | solution.py:638
  111.1 7.5 %collective-permute-done.10.refs_1_ = f32[8,4096]{1,0:T(8,128)S(1)} collective-permute-done((f32[8,4096]{1,0:T(8,128)S(1)}, f32[8,4096]{1,0:T(8,128)S(1)}, u32[]{:S(2)}, u32[]{:S(2)}) %collective-permute-start.10) | collective-permute-done | bytes 131104 | tf_op jit(solution)/shard_map/ppermute | solution.py:329
  118.6 1.7 pack.20
  120.3 0.6 collective-permute-start.19
  121.0 1.2 collective-permute-start.13
  122.4 2.8 %collective-permute-done.13.refs_1_ = f32[4,4096]{1,0:T(4,128)S(1)} collective-permute-done((f32[4,4096]{1,0:T(4,128)S(1)}, f32[4,4096]{1,0:T(4,128)S(1)}, u32[]{:S(2)}, u32[]{:S(2)}) %collective-permute-start.13) | collective-permute-done | bytes 65568 | tf_op jit(solution)/shard_map/ppermute | solution.py:329
  125.3 2.4 %collective-permute-done.17.refs_5_.refs_4_ = bf16[288,1024]{1,0:T(8,128)(2,1)} collective-permute-done((bf16[288,1024]{1,0:T(8,128)(2,1)}, bf16[288,1024]{1,0:T(8,128)(2,1)}, u32[]{:S(2)}, u32[]{:S(2)}) %collective-permute-start.17) | collective-permute-done | bytes 589856 | tf_op jit(solution)/shard_map/ppermute | solution.py:637
  127.6 37.5 %pack.21 = (bf16[288,1024]{1,0:T(8,128)(2,1)}, bf16[288,1024]{1,0:T(8,128)(2,1)}) custom-call(s32[2]{0:T(128)S(1)} %pad_add_fusion.refs_0_.flag, s32[4]{0:T(128)S(1)} %gather_fusion, f32[2,1920,1024]{2,1,0:T(8,128)} %refs_0_.15, f32[2,1920,1024]{2,1,0:T(8,128)} %refs_1_.15, f32[2,1920,1024]{2,1,0:T(8,128)} %refs_2_.35, ...), custom_call_target="tpu_custom_call" | custom-call | bytes 3538944 | tf_op jit(solution)/shard_map/pack/pallas_call | solution.py:161
  165.3 2.0 collective-permute-start.21
  168.7 1.1 collective-permute-done.16.refs_1_
  169.8 0.6 halve.7.refs_7_
  170.5 0.7 copy-done.20
  171.2 1.9 pack.22
  173.2 2.0 collective-permute-start.25
  175.2 1.2 collect.1
  176.5 5.4 %update.2 = (f32[1920,1024]{1,0:T(8,128)}, f32[1920,1024]{1,0:T(8,128)}, f32[1920,1024]{1,0:T(8,128)}) custom-call(s32[2]{0:T(128)S(1)} %pad_add_fusion.1.info, bf16[1920,64]{1,0:T(8,128)(2,1)S(1)} %get-tuple-element.96.hid_ref.refs_3_, bf16[64,1024]{1,0:T(8,128)(2,1)S(1)} %get-tuple-element.97.out_ref, f32[2,1920,1024]{2,1,0:T(8,128)} %refs_0_.15, ...), custom_call_target="tpu_custom_call" | custom-call | flops 50331648 | bytes 9437184 | tf_op jit(solution)/shard_map/update/pallas_call | solution.py:449
  181.9 0.7 patch.4
  182.6 2.1 %pack.23 = (bf16[288,1024]{1,0:T(8,128)(2,1)S(1)}, bf16[288,1024]{1,0:T(8,128)(2,1)S(1)}) custom-call(s32[2]{0:T(128)S(1)} %pad_add_fusion.refs_0_.flag, s32[4]{0:T(128)S(1)} %gather_fusion, f32[2,1920,1024]{2,1,0:T(8,128)} %refs_0_.15, f32[2,1920,1024]{2,1,0:T(8,128)} %refs_1_.15, f32[2,1920,1024]{2,1,0:T(8,128)} %refs_2_.35, ...), custom_call_target="tpu_custom_call" | custom-call | bytes 3538944 | tf_op jit(solution)/shard_map/pack/pallas_call | solution.py:161
  184.8 2.4 %collective-permute-start.24 = (bf16[288,1024]{1,0:T(8,128)(2,1)S(1)}, bf16[288,1024]{1,0:T(8,128)(2,1)S(1)}, u32[]{:S(2)}, u32[]{:S(2)}) collective-permute-start(bf16[288,1024]{1,0:T(8,128)(2,1)S(1)} %get-tuple-element.104), channel_id=1, source_target_pairs={{8,0},{24,8},{16,24},{0,16},{9,1},{25,9},{17,25},{1,17},{10,2},{26... | collective-permute-start | bytes 1769480 | tf_op jit(solution)/shard_map/ppermute | solution.py:638
  187.1 14.5 %update.3 = (f32[1920,1024]{1,0:T(8,128)}, f32[1920,1024]{1,0:T(8,128)}, f32[1920,1024]{1,0:T(8,128)}) custom-call(s32[2]{0:T(128)S(1)} %pad_add_fusion.1.info, bf16[1920,64]{1,0:T(8,128)(2,1)S(1)} %get-tuple-element.96.hid_ref.refs_3_, bf16[64,1024]{1,0:T(8,128)(2,1)S(1)} %get-tuple-element.97.out_ref, ...), custom_call_target="tpu_custom_call", output_to_operand_aliasing={{0}: (6, {}), {1}: (7, {}), {2}: (8, {})} | custom-call | flops 201326592 | bytes 37748736 | tf_op jit(solution)/shard_map/update/pallas_call | solution.py:449
  201.6 0.7 patch.5
  202.3 0.7 patch.6
  203.0 0.7 patch.7
  (90 shorter events, 3.3 us)
Async XLA Ops:
  3.4 27.3 %collective-permute-start.1 = (bf16[288,1024]{1,0:T(8,128)(2,1)}, bf16[288,1024]{1,0:T(8,128)(2,1)S(1)}, u32[]{:S(2)}, u32[]{:S(2)}) collective-permute-start(bf16[288,1024]{1,0:T(8,128)(2,1)} %get-tuple-element.64), channel_id=1, source_target_pairs={{8,0},{24,8},{16,24},{0,16},{9,1},{25,9},{17,25},{1,17},{10,2},{26... | collective-permute-start | bytes 1769480 | tf_op jit(solution)/shard_map/ppermute | solution.py:638
  6.4 5.2 %copy-start.23 = (s32[4]{0:T(128)S(1)}, s32[4]{0:T(128)}, u32[]{:S(2)}) copy-start(s32[4]{0:T(128)} %constant.88.clone) | copy-start | bytes 52
  6.4 7.2 %copy-start.21 = (bf16[1,2,4096]{2,1,0:T(2,128)(2,1)S(1)}, bf16[1,2,4096]{2,1,0:T(2,128)(2,1)}, u32[]{:S(2)}) copy-start(bf16[1,2,4096]{2,1,0:T(2,128)(2,1)} %param.11) | copy-start | bytes 49156
  6.4 7.2 %copy-start.22 = (bf16[1,2,4096]{2,1,0:T(2,128)(2,1)S(1)}, bf16[1,2,4096]{2,1,0:T(2,128)(2,1)}, u32[]{:S(2)}) copy-start(bf16[1,2,4096]{2,1,0:T(2,128)(2,1)} %param.12) | copy-start | bytes 49156
  6.4 24.3 %collective-permute-start = (bf16[288,1024]{1,0:T(8,128)(2,1)S(1)}, bf16[288,1024]{1,0:T(8,128)(2,1)S(1)}, u32[]{:S(2)}, u32[]{:S(2)}) collective-permute-start(bf16[288,1024]{1,0:T(8,128)(2,1)S(1)} %get-tuple-element.62.refs_3_), channel_id=1, source_target_pairs={{0,8},{8,24},{24,16},{16,0},{1,9},{9,25},{25,17},{17,1},{2,10},{10... | collective-permute-start | bytes 1769480 | tf_op jit(solution)/shard_map/ppermute | solution.py:637
  8.9 30.6 %collective-permute-start.3 = (bf16[288,1024]{1,0:T(8,128)(2,1)}, bf16[288,1024]{1,0:T(8,128)(2,1)S(1)}, u32[]{:S(2)}, u32[]{:S(2)}) collective-permute-start(bf16[288,1024]{1,0:T(8,128)(2,1)} %get-tuple-element.67), channel_id=1, source_target_pairs={{8,0},{24,8},{16,24},{0,16},{9,1},{25,9},{17,25},{1,17},{10,2},{26... | collective-permute-start | bytes 1769480 | tf_op jit(solution)/shard_map/ppermute | solution.py:638
  10.9 28.6 %collective-permute-start.2 = (bf16[288,1024]{1,0:T(8,128)(2,1)}, bf16[288,1024]{1,0:T(8,128)(2,1)S(1)}, u32[]{:S(2)}, u32[]{:S(2)}) collective-permute-start(bf16[288,1024]{1,0:T(8,128)(2,1)} %get-tuple-element.63.refs_2_), channel_id=1, source_target_pairs={{0,8},{8,24},{24,16},{16,0},{1,9},{9,25},{25,17},{17,1},{2,10},{10... | collective-permute-start | bytes 1769480 | tf_op jit(solution)/shard_map/ppermute | solution.py:637
  30.7 1.0 copy-start.3
  31.7 19.3 %collective-permute-start.5 = (bf16[288,1024]{1,0:T(8,128)(2,1)S(1)}, bf16[288,1024]{1,0:T(8,128)(2,1)S(1)}, u32[]{:S(2)}, u32[]{:S(2)}) collective-permute-start(bf16[288,1024]{1,0:T(8,128)(2,1)S(1)} %get-tuple-element.70), channel_id=1, source_target_pairs={{8,0},{24,8},{16,24},{0,16},{9,1},{25,9},{17,25},{1,17},{10,2},{26... | collective-permute-start | bytes 1769480 | tf_op jit(solution)/shard_map/ppermute | solution.py:638
  33.3 18.0 %collective-permute-start.4 = (bf16[288,1024]{1,0:T(8,128)(2,1)S(1)}, bf16[288,1024]{1,0:T(8,128)(2,1)S(1)}, u32[]{:S(2)}, u32[]{:S(2)}) collective-permute-start(bf16[288,1024]{1,0:T(8,128)(2,1)S(1)} %get-tuple-element.65.refs_3_), channel_id=1, source_target_pairs={{0,8},{8,24},{24,16},{16,0},{1,9},{9,25},{25,17},{17,1},{2,10},{10... | collective-permute-start | bytes 1769480 | tf_op jit(solution)/shard_map/ppermute | solution.py:637
  39.5 1.0 copy-start.5
  39.5 1.0 copy-start.7
  40.5 23.0 %collective-permute-start.7 = (bf16[288,1024]{1,0:T(8,128)(2,1)S(1)}, bf16[288,1024]{1,0:T(8,128)(2,1)S(1)}, u32[]{:S(2)}, u32[]{:S(2)}) collective-permute-start(bf16[288,1024]{1,0:T(8,128)(2,1)S(1)} %get-tuple-element.73), channel_id=1, source_target_pairs={{8,0},{24,8},{16,24},{0,16},{9,1},{25,9},{17,25},{1,17},{10,2},{26... | collective-permute-start | bytes 1769480 | tf_op jit(solution)/shard_map/ppermute | solution.py:638
  43.9 20.0 %collective-permute-start.6 = (bf16[288,1024]{1,0:T(8,128)(2,1)S(1)}, bf16[288,1024]{1,0:T(8,128)(2,1)S(1)}, u32[]{:S(2)}, u32[]{:S(2)}) collective-permute-start(bf16[288,1024]{1,0:T(8,128)(2,1)S(1)} %get-tuple-element.68.refs_4_), channel_id=1, source_target_pairs={{0,8},{8,24},{24,16},{16,0},{1,9},{9,25},{25,17},{17,1},{2,10},{10... | collective-permute-start | bytes 1769480 | tf_op jit(solution)/shard_map/ppermute | solution.py:637
  52.2 24.6 %collective-permute-start.9 = (bf16[288,1024]{1,0:T(8,128)(2,1)S(1)}, bf16[288,1024]{1,0:T(8,128)(2,1)S(1)}, u32[]{:S(2)}, u32[]{:S(2)}) collective-permute-start(bf16[288,1024]{1,0:T(8,128)(2,1)S(1)} %get-tuple-element.76), channel_id=1, source_target_pairs={{8,0},{24,8},{16,24},{0,16},{9,1},{25,9},{17,25},{1,17},{10,2},{26... | collective-permute-start | bytes 1769480 | tf_op jit(solution)/shard_map/ppermute | solution.py:638
  56.4 20.5 %collective-permute-start.8 = (bf16[288,1024]{1,0:T(8,128)(2,1)S(1)}, bf16[288,1024]{1,0:T(8,128)(2,1)S(1)}, u32[]{:S(2)}, u32[]{:S(2)}) collective-permute-start(bf16[288,1024]{1,0:T(8,128)(2,1)S(1)} %get-tuple-element.71.refs_4_), channel_id=1, source_target_pairs={{0,8},{8,24},{24,16},{16,0},{1,9},{9,25},{25,17},{17,1},{2,10},{10... | collective-permute-start | bytes 1769480 | tf_op jit(solution)/shard_map/ppermute | solution.py:637
  63.5 2.2 %copy-start.11 = (bf16[288,1024]{1,0:T(8,128)(2,1)}, bf16[288,1024]{1,0:T(8,128)(2,1)S(1)}, u32[]{:S(2)}) copy-start(bf16[288,1024]{1,0:T(8,128)(2,1)S(1)} %collective-permute-done.7.refs_6_.refs_7_) | copy-start | bytes 1769476
  63.9 1.8 copy-start.13
  65.7 20.1 %collective-permute-start.12 = (bf16[288,1024]{1,0:T(8,128)(2,1)}, bf16[288,1024]{1,0:T(8,128)(2,1)S(1)}, u32[]{:S(2)}, u32[]{:S(2)}) collective-permute-start(bf16[288,1024]{1,0:T(8,128)(2,1)} %get-tuple-element.84), channel_id=1, source_target_pairs={{8,0},{24,8},{16,24},{0,16},{9,1},{25,9},{17,25},{1,17},{10,2},{26... | collective-permute-start | bytes 1769480 | tf_op jit(solution)/shard_map/ppermute | solution.py:638
  69.7 19.6 %collective-permute-start.11 = (bf16[288,1024]{1,0:T(8,128)(2,1)}, bf16[288,1024]{1,0:T(8,128)(2,1)}, u32[]{:S(2)}, u32[]{:S(2)}) collective-permute-start(bf16[288,1024]{1,0:T(8,128)(2,1)} %get-tuple-element.74.refs_4_), channel_id=1, source_target_pairs={{0,8},{8,24},{24,16},{16,0},{1,9},{9,25},{25,17},{17,1},{2,10},{10... | collective-permute-start | bytes 1769480 | tf_op jit(solution)/shard_map/ppermute | solution.py:637
  76.8 1.8 copy-start.17
  76.9 1.8 copy-start.18
  78.7 39.9 %collective-permute-start.14 = (bf16[352,1024]{1,0:T(8,128)(2,1)}, bf16[352,1024]{1,0:T(8,128)(2,1)S(1)}, u32[]{:S(2)}, u32[]{:S(2)}) collective-permute-start(bf16[352,1024]{1,0:T(8,128)(2,1)} %get-tuple-element.81.refs_1_), channel_id=1, source_target_pairs={{0,8},{8,24},{24,16},{16,0},{1,9},{9,25},{25,17},{17,1},{2,10},{10... | collective-permute-start | bytes 2162696 | tf_op jit(solution)/shard_map/ppermute | solution.py:637
  81.9 36.7 %collective-permute-start.15 = (bf16[336,1024]{1,0:T(8,128)(2,1)}, bf16[336,1024]{1,0:T(8,128)(2,1)S(1)}, u32[]{:S(2)}, u32[]{:S(2)}) collective-permute-start(bf16[336,1024]{1,0:T(8,128)(2,1)} %get-tuple-element.88), channel_id=1, source_target_pairs={{8,0},{24,8},{16,24},{0,16},{9,1},{25,9},{17,25},{1,17},{10,2},{26... | collective-permute-start | bytes 2064392 | tf_op jit(solution)/shard_map/ppermute | solution.py:638
  85.8 23.1 %copy-start.15 = (bf16[288,1024]{1,0:T(8,128)(2,1)}, bf16[288,1024]{1,0:T(8,128)(2,1)S(1)}, u32[]{:S(2)}) copy-start(bf16[288,1024]{1,0:T(8,128)(2,1)S(1)} %collective-permute-done.12.refs_6_.refs_1_) | copy-start | bytes 1769476
  109.0 16.3 %collective-permute-start.18 = (bf16[288,1024]{1,0:T(8,128)(2,1)}, bf16[288,1024]{1,0:T(8,128)(2,1)}, u32[]{:S(2)}, u32[]{:S(2)}) collective-permute-start(bf16[288,1024]{1,0:T(8,128)(2,1)} %get-tuple-element.92), channel_id=1, source_target_pairs={{8,0},{24,8},{16,24},{0,16},{9,1},{25,9},{17,25},{1,17},{10,2},{26... | collective-permute-start | bytes 1769480 | tf_op jit(solution)/shard_map/ppermute | solution.py:638
  111.1 16.6 %collective-permute-start.17 = (bf16[288,1024]{1,0:T(8,128)(2,1)}, bf16[288,1024]{1,0:T(8,128)(2,1)}, u32[]{:S(2)}, u32[]{:S(2)}) collective-permute-start(bf16[288,1024]{1,0:T(8,128)(2,1)} %get-tuple-element.85.refs_2_), channel_id=1, source_target_pairs={{0,8},{8,24},{24,16},{16,0},{1,9},{9,25},{25,17},{17,1},{2,10},{10... | collective-permute-start | bytes 1769480 | tf_op jit(solution)/shard_map/ppermute | solution.py:637
  111.1 7.5 %collective-permute-start.10 = (f32[8,4096]{1,0:T(8,128)S(1)}, f32[8,4096]{1,0:T(8,128)S(1)}, u32[]{:S(2)}, u32[]{:S(2)}) collective-permute-start(f32[8,4096]{1,0:T(8,128)S(1)} %get-tuple-element.83), channel_id=1, source_target_pairs={{0,4},{2,6},{4,0},{6,2},{1,5},{3,7},{5,1},{7,3},{8,12},{10,14},{12... | collective-permute-start | bytes 393224 | tf_op jit(solution)/shard_map/ppermute | solution.py:329
  118.6 56.6 %copy-start = (bf16[352,1024]{1,0:T(8,128)(2,1)}, bf16[352,1024]{1,0:T(8,128)(2,1)S(1)}, u32[]{:S(2)}) copy-start(bf16[352,1024]{1,0:T(8,128)(2,1)S(1)} %collective-permute-done.14.refs_5_.refs_4_.refs_2_) | copy-start | bytes 2162692
  120.3 50.1 %collective-permute-start.19 = (bf16[336,1024]{1,0:T(8,128)(2,1)}, bf16[336,1024]{1,0:T(8,128)(2,1)S(1)}, u32[]{:S(2)}, u32[]{:S(2)}) collective-permute-start(bf16[336,1024]{1,0:T(8,128)(2,1)} %get-tuple-element.89.refs_2_), channel_id=1, source_target_pairs={{0,8},{8,24},{24,16},{16,0},{1,9},{9,25},{25,17},{17,1},{2,10},{10... | collective-permute-start | bytes 2064392 | tf_op jit(solution)/shard_map/ppermute | solution.py:637
  121.0 4.3 %collective-permute-start.13 = (f32[4,4096]{1,0:T(4,128)S(1)}, f32[4,4096]{1,0:T(4,128)S(1)}, u32[]{:S(2)}, u32[]{:S(2)}) collective-permute-start(f32[4,4096]{1,0:T(4,128)S(1)} %get-tuple-element.87), channel_id=1, source_target_pairs={{0,2},{2,0},{4,6},{6,4},{1,3},{3,1},{5,7},{7,5},{8,10},{10,8},{12,... | collective-permute-start | bytes 196616 | tf_op jit(solution)/shard_map/ppermute | solution.py:329
  122.1 48.4 %collective-permute-start.20 = (bf16[288,1024]{1,0:T(8,128)(2,1)}, bf16[288,1024]{1,0:T(8,128)(2,1)}, u32[]{:S(2)}, u32[]{:S(2)}) collective-permute-start(bf16[288,1024]{1,0:T(8,128)(2,1)} %get-tuple-element.94), channel_id=1, source_target_pairs={{8,0},{24,8},{16,24},{0,16},{9,1},{25,9},{17,25},{1,17},{10,2},{26... | collective-permute-start | bytes 1769480 | tf_op jit(solution)/shard_map/ppermute | solution.py:638
  165.2 17.5 %collective-permute-start.22 = (bf16[288,1024]{1,0:T(8,128)(2,1)}, bf16[288,1024]{1,0:T(8,128)(2,1)}, u32[]{:S(2)}, u32[]{:S(2)}) collective-permute-start(bf16[288,1024]{1,0:T(8,128)(2,1)} %get-tuple-element.98), channel_id=1, source_target_pairs={{8,0},{24,8},{16,24},{0,16},{9,1},{25,9},{17,25},{1,17},{10,2},{26... | collective-permute-start | bytes 1769480 | tf_op jit(solution)/shard_map/ppermute | solution.py:638
  165.3 17.3 %collective-permute-start.21 = (bf16[288,1024]{1,0:T(8,128)(2,1)}, bf16[288,1024]{1,0:T(8,128)(2,1)}, u32[]{:S(2)}, u32[]{:S(2)}) collective-permute-start(bf16[288,1024]{1,0:T(8,128)(2,1)} %get-tuple-element.93.refs_2_), channel_id=1, source_target_pairs={{0,8},{8,24},{24,16},{16,0},{1,9},{9,25},{25,17},{17,1},{2,10},{10... | collective-permute-start | bytes 1769480 | tf_op jit(solution)/shard_map/ppermute | solution.py:637
  168.6 1.3 collective-permute-start.16
  173.1 29.2 %collective-permute-start.26 = (bf16[288,1024]{1,0:T(8,128)(2,1)S(1)}, bf16[288,1024]{1,0:T(8,128)(2,1)S(1)}, u32[]{:S(2)}, u32[]{:S(2)}) collective-permute-start(bf16[288,1024]{1,0:T(8,128)(2,1)S(1)} %get-tuple-element.105), channel_id=1, source_target_pairs={{8,0},{24,8},{16,24},{0,16},{9,1},{25,9},{17,25},{1,17},{10,2},{26... | collective-permute-start | bytes 1769480 | tf_op jit(solution)/shard_map/ppermute | solution.py:638
  173.2 29.1 %collective-permute-start.25 = (bf16[288,1024]{1,0:T(8,128)(2,1)S(1)}, bf16[288,1024]{1,0:T(8,128)(2,1)S(1)}, u32[]{:S(2)}, u32[]{:S(2)}) collective-permute-start(bf16[288,1024]{1,0:T(8,128)(2,1)S(1)} %get-tuple-element.95.refs_7_), channel_id=1, source_target_pairs={{0,8},{8,24},{24,16},{16,0},{1,9},{9,25},{25,17},{17,1},{2,10},{10... | collective-permute-start | bytes 1769480 | tf_op jit(solution)/shard_map/ppermute | solution.py:637
  176.4 5.5 %copy-start.2 = (bf16[288,1024]{1,0:T(8,128)(2,1)S(1)}, bf16[288,1024]{1,0:T(8,128)(2,1)}, u32[]{:S(2)}) copy-start(bf16[288,1024]{1,0:T(8,128)(2,1)} %copy-done.1) | copy-start | bytes 1769476
  176.4 5.5 %copy-start.4 = (bf16[288,1024]{1,0:T(8,128)(2,1)S(1)}, bf16[288,1024]{1,0:T(8,128)(2,1)}, u32[]{:S(2)}) copy-start(bf16[288,1024]{1,0:T(8,128)(2,1)} %copy-done.3) | copy-start | bytes 1769476
  176.4 5.5 %copy-start.6 = (bf16[288,1024]{1,0:T(8,128)(2,1)S(1)}, bf16[288,1024]{1,0:T(8,128)(2,1)}, u32[]{:S(2)}) copy-start(bf16[288,1024]{1,0:T(8,128)(2,1)} %copy-done.5) | copy-start | bytes 1769476
  176.4 5.5 %copy-start.8 = (bf16[288,1024]{1,0:T(8,128)(2,1)S(1)}, bf16[288,1024]{1,0:T(8,128)(2,1)}, u32[]{:S(2)}) copy-start(bf16[288,1024]{1,0:T(8,128)(2,1)} %copy-done.7) | copy-start | bytes 1769476
  176.4 5.5 %copy-start.10 = (bf16[288,1024]{1,0:T(8,128)(2,1)S(1)}, bf16[288,1024]{1,0:T(8,128)(2,1)}, u32[]{:S(2)}) copy-start(bf16[288,1024]{1,0:T(8,128)(2,1)} %copy-done.9) | copy-start | bytes 1769476
  176.4 5.5 %copy-start.12 = (bf16[288,1024]{1,0:T(8,128)(2,1)S(1)}, bf16[288,1024]{1,0:T(8,128)(2,1)}, u32[]{:S(2)}) copy-start(bf16[288,1024]{1,0:T(8,128)(2,1)} %copy-done.11) | copy-start | bytes 1769476
  176.4 5.5 %copy-start.14 = (bf16[288,1024]{1,0:T(8,128)(2,1)S(1)}, bf16[288,1024]{1,0:T(8,128)(2,1)}, u32[]{:S(2)}) copy-start(bf16[288,1024]{1,0:T(8,128)(2,1)} %copy-done.13) | copy-start | bytes 1769476
  176.5 5.5 %copy-start.19 = (bf16[288,1024]{1,0:T(8,128)(2,1)S(1)}, bf16[288,1024]{1,0:T(8,128)(2,1)}, u32[]{:S(2)}) copy-start(bf16[288,1024]{1,0:T(8,128)(2,1)} %copy-done.18) | copy-start | bytes 1769476
  184.8 18.3 %collective-permute-start.24 = (bf16[288,1024]{1,0:T(8,128)(2,1)S(1)}, bf16[288,1024]{1,0:T(8,128)(2,1)S(1)}, u32[]{:S(2)}, u32[]{:S(2)}) collective-permute-start(bf16[288,1024]{1,0:T(8,128)(2,1)S(1)} %get-tuple-element.104), channel_id=1, source_target_pairs={{8,0},{24,8},{16,24},{0,16},{9,1},{25,9},{17,25},{1,17},{10,2},{26... | collective-permute-start | bytes 1769480 | tf_op jit(solution)/shard_map/ppermute | solution.py:638
  187.1 15.9 %collective-permute-start.23 = (bf16[288,1024]{1,0:T(8,128)(2,1)S(1)}, bf16[288,1024]{1,0:T(8,128)(2,1)S(1)}, u32[]{:S(2)}, u32[]{:S(2)}) collective-permute-start(bf16[288,1024]{1,0:T(8,128)(2,1)S(1)} %get-tuple-element.103.refs_6_), channel_id=1, source_target_pairs={{0,8},{8,24},{24,16},{16,0},{1,9},{9,25},{25,17},{17,1},{2,10},{10... | collective-permute-start | bytes 1769480 | tf_op jit(solution)/shard_map/ppermute | solution.py:637
  187.1 14.5 %copy-start.16 = (bf16[288,1024]{1,0:T(8,128)(2,1)S(1)}, bf16[288,1024]{1,0:T(8,128)(2,1)}, u32[]{:S(2)}) copy-start(bf16[288,1024]{1,0:T(8,128)(2,1)} %copy-done.15) | copy-start | bytes 1769476
  (3 other events, 2.6 us)

commit v6 on v5

--- a/solution.py
+++ b/solution.py
@@ -23,6 +23,32 @@
 
 def ring_order(n):
     return [0, 1, 3, 2] if n == 4 else list(range(n))
+
+
+def entry(table, index):
+    found = jnp.int32(0)
+    for at, value in enumerate(table):
+        found = jnp.where(index == at, jnp.int32(value), found)
+    return found
+
+
+class Roles:
+    def __init__(self, failed, n):
+        self.n = n
+        self.order = ring_order(n)
+        self.spots = [self.order.index(i) for i in range(n)]
+        self.me = lax.axis_index("replica").astype(jnp.int32)
+        self.failed = failed[0]
+        self.source = lax.rem(self.failed + 1, n)
+        self.lost = self.me == self.failed
+
+    def ahead(self):
+        apart = entry(self.spots, self.failed) - entry(self.spots, self.source)
+        return lax.rem(apart + self.n, self.n)
+
+    def neighbour(self, hops):
+        spot = lax.rem(entry(self.spots, self.me) + hops, self.n)
+        return entry(self.order, spot)
 
 
 def largest(options, default):
@@ -66,10 +92,10 @@
     return moves
 
 
-def pack_body(*refs, places, chunk, slabs, passed, counts):
-    count_flags, count_seen, count_parts, count_after = counts
-    flag, targets = refs[:2] if count_flags else (None, None)
-    refs = refs[count_flags:]
+def pack_body(*refs, n, places, chunk, slabs, passed, counts):
+    count_seen, count_parts, count_after = counts
+    if count_seen:
+        roles, refs = Roles(refs[0], n), refs[1:]
     state = refs[0:3]
     seen = refs[3 : 3 + count_seen]
     rest = refs[3 + count_seen :]
@@ -80,14 +106,21 @@
     width = held.shape[2]
     size = 3 * chunk
 
+    def rows_of(j):
+        way, k = divmod(j, 3)
+        return way, pl.ds(k * chunk, chunk)
+
     def fetch(j):
         way, k = divmod(j, 3)
         rows = pl.ds(places[way] * chunk, chunk)
         return pltpu.make_async_copy(state[k].at[1, rows], held.at[j], sem.at[j])
 
+    def take(j):
+        way, rows = rows_of(j)
+        return pltpu.make_async_copy(seen[way].at[rows], made.at[way, rows], sem.at[j])
+
     def store(j):
-        way, k = divmod(j, 3)
-        rows = pl.ds(k * chunk, chunk)
+        way, rows = rows_of(j)
         return pltpu.make_async_copy(
             made.at[way, rows], sends[way].at[rows], out_sem.at[j]
         )
@@ -96,73 +129,83 @@
         for j in range(6):
             fetch(j).start()
         for j in range(6):
-            way, k = divmod(j, 3)
+            way, rows = rows_of(j)
             fetch(j).wait()
-            made[way, pl.ds(k * chunk, chunk)] = held[j].astype(BF16)
+            made[way, rows] = held[j].astype(BF16)
             store(j).start()
         for j in range(6):
             store(j).wait()
 
-    def relay(way):
-        rows = pl.ds(0, size)
-        return pltpu.make_async_copy(seen[way].at[rows], sends[way].at[rows], sem.at[way])
-
-    def below(way):
-        count = passed[way] or sends[way].shape[0] - size
-        rows = pl.ds(size, count)
-        origin = seen[way].at[rows] if passed[way] else made.at[way, rows]
-        return pltpu.make_async_copy(origin, sends[way].at[rows], below_sem.at[way])
+    def relay():
+        for j in range(6):
+            take(j).start()
+        for j in range(6):
+            take(j).wait()
+            store(j).start()
+        for j in range(6):
+            store(j).wait()
+
+    def below(way, inward):
+        rows = pl.ds(size, passed[way] or sends[way].shape[0] - size)
+        here = made.at[way, rows]
+        if inward:
+            return pltpu.make_async_copy(seen[way].at[rows], here, below_sem.at[way])
+        return pltpu.make_async_copy(here, sends[way].at[rows], below_sem.at[way])
 
     for way in range(2):
+        if passed[way]:
+            below(way, True).start()
         if slabs[way]:
-            n = targets.shape[0]
             tokens, features = both.shape[0], both.shape[1] // 2
-            keep = flag[1] == 0
             moves = column_pieces([part.shape[1] for part in parts], width)
             for part, begin, piece, to, run in moves:
                 units = parts[part][:, begin : begin + run]
                 made[way, pl.ds(size + piece * tokens, tokens), pl.ds(to, run)] = (
-                    jnp.where(keep, units, jnp.zeros_like(units))
+                    jnp.where(roles.lost, jnp.zeros_like(units), units)
                 )
             row = size + (1 + moves[-1][2]) * tokens
             for far in range(slabs[way], 0, -1):
-                target = targets[far if way == 0 else n - far]
+                target = roles.neighbour(far if way == 0 else n - far)
                 slab = pl.ds(pl.multiple_of(features + target * width, 128), width)
                 made[way, pl.ds(row, tokens)] = both[:, slab]
                 row += tokens
-        if slabs[way] or passed[way]:
-            below(way).start()
-
-    if not seen:
+            below(way, False).start()
+
+    for way in range(2):
+        if passed[way]:
+            below(way, True).wait()
+            below(way, False).start()
+
+    if seen:
+        pl.when(roles.me == roles.source)(convert)
+        pl.when(roles.me != roles.source)(relay)
+    else:
         convert()
-    else:
-        pl.when(flag[0] == 1)(convert)
-
-        @pl.when(flag[0] == 0)
-        def _():
-            for way in range(2):
-                relay(way).start()
-            for way in range(2):
-                relay(way).wait()
 
     for way in range(2):
         if slabs[way] or passed[way]:
-            below(way).wait()
-
-
-def pack(flags, state, seen, parcel, after, places, chunk, slabs, passed):
+            below(way, False).wait()
+
+
+def pack(failed, n, state, seen, parcel, after, places, chunk, slabs, passed):
     width = state[0].shape[2]
     extra = list(passed)
     if parcel:
         tokens = parcel[0].shape[0]
         pieces = -(-sum(part.shape[1] for part in parcel[1:]) // width)
         extra = [tokens * (pieces + count) if count else 0 for count in slabs]
-    counts = (len(flags), len(seen), max(len(parcel) - 1, 0), len(after))
+    counts = (len(seen), max(len(parcel) - 1, 0), len(after))
     return pl.pallas_call(
         functools.partial(
-            pack_body, places=places, chunk=chunk, slabs=slabs, passed=passed, counts=counts
+            pack_body,
+            n=n,
+            places=places,
+            chunk=chunk,
+            slabs=slabs,
+            passed=passed,
+            counts=counts,
         ),
-        in_specs=[SMEM] * len(flags)
+        in_specs=[SMEM] * bool(seen)
         + [ANY] * (3 + len(seen))
         + [WHOLE] * len(parcel)
         + [ANY] * len(after),
@@ -180,7 +223,7 @@
         compiler_params=PARAMS,
         cost_estimate=cost(0, 2 * 3 * chunk * width * 6),
         name="pack",
-    )(*flags, *state, *seen, *parcel, *after)
+    )(*([failed] if seen else []), *state, *seen, *parcel, *after)
 
 
 def beside_body(*refs):
@@ -334,7 +377,8 @@
         return (self.value,)
 
 
-def collect_body(flag, targets, both, *refs, places, parts_count, size, pieces):
+def collect_body(failed, both, *refs, n, places, parts_count, size, pieces):
+    roles = Roles(failed, n)
     parts = refs[:parts_count]
     blocks = refs[parts_count : parts_count + len(places)]
     hidden_t, outs, held, sem = refs[-4:]
@@ -351,13 +395,12 @@
     for j in range(len(places)):
         for part in range(2):
             fetch(j, part).start()
-    keep = flag[1] == 0
     for part, begin, piece, to, run in column_pieces([p.shape[1] for p in parts], width):
         units = parts[part][:, begin : begin + run]
         held[0, pl.ds(piece * tokens, tokens), pl.ds(to, run)] = jnp.where(
-            keep, units, jnp.zeros_like(units)
+            roles.lost, jnp.zeros_like(units), units
         )
-    slab = pl.ds(pl.multiple_of(features + targets[0] * width, 128), width)
+    slab = pl.ds(pl.multiple_of(features + roles.me * width, 128), width)
     held[0, pl.ds(pieces * tokens, tokens)] = both[:, slab]
     for j in range(len(places)):
         for part in range(2):
@@ -373,7 +416,7 @@
         hidden_t[pl.ds(piece * width, run)] = hidden.astype(F32).T.astype(BF16)
 
 
-def collect(flag, targets, both, parts, blocks, places, size, width, after):
+def collect(failed, n, both, parts, blocks, places, size, width, after):
     tokens = both.shape[0]
     units = sum(part.shape[1] for part in parts)
     pieces = -(-units // width)
@@ -381,12 +424,13 @@
     return pl.pallas_call(
         functools.partial(
             collect_body,
+            n=n,
             places=places,
             parts_count=len(parts),
             size=size,
             pieces=pieces,
         ),
-        in_specs=[SMEM, SMEM]
+        in_specs=[SMEM]
         + [WHOLE] * (1 + len(parts))
         + [ANY] * (len(blocks) + len(after)),
         out_specs=[WHOLE, WHOLE],
@@ -401,10 +445,10 @@
         compiler_params=PARAMS,
         cost_estimate=cost(0, 4 * depth * (units + width)),
         name="collect",
-    )(flag, targets, both, *parts, *blocks, *after)
-
-
-def update_body(info, hid_ref, out_ref, *refs, healthy, block, first, count, unread):
+    )(failed, both, *parts, *blocks, *after)
+
+
+def update_body(failed, hid_ref, out_ref, *refs, n, block, first, count, unread):
     state, news = refs[:3], refs[3 + unread : 6 + unread]
     total = refs[6 + unread]
     width = out_ref.shape[1]
@@ -417,7 +461,7 @@
         def _(i):
             here = pl.ds(pl.multiple_of(i * group, group), group)
             m_new[here], a_new[here], b_new[here] = updated(
-                m_ref[0, here], a_ref[0, here], b_ref[0, here], total[here], healthy
+                m_ref[0, here], a_ref[0, here], b_ref[0, here], total[here], n - 1.0
             )
 
     deep = pl.Buffered(min(BUFFERS, count + 1))
@@ -426,7 +470,7 @@
     )
     new = pl.BlockSpec((block, width), lambda i: (first + i, 0))
 
-    @pl.when(info[0] == 0)
+    @pl.when(jnp.logical_not(Roles(failed, n).lost))
     def _():
         pltpu.emit_pipeline(
             step,
@@ -441,7 +485,7 @@
         )(hid_ref, *state, *news)
 
 
-def update(info, hidden_t, outs, state, news, after, healthy, block, first, count):
+def update(failed, n, hidden_t, outs, state, news, after, block, first, count):
     _, rows, width = state[0].shape
     depth = hidden_t.shape[1]
     shape = jax.ShapeDtypeStruct((rows, width), F32)
@@ -449,7 +493,7 @@
     return pl.pallas_call(
         functools.partial(
             update_body,
-            healthy=healthy,
+            n=n,
             block=block,
             first=first,
             count=count,
@@ -467,10 +511,10 @@
             2 * count * block * width,
         ),
         name="update",
-    )(info, hidden_t, outs, *state, *news, *after)
-
-
-def patch_body(info, hid_ref, out_ref, *refs, arrivals, chunks, n, count_after):
+    )(failed, hidden_t, outs, *state, *news, *after)
+
+
+def patch_body(failed, hid_ref, out_ref, *refs, arrivals, chunks, n, count_after):
     count = len(arrivals)
     got = refs[:count]
     rest = refs[count + 3 + count_after :]
@@ -478,7 +522,8 @@
     held, made, total, in_sem, out_sem = rest[3:]
     chunk = made.shape[2]
     group = row_group(chunk)
-    ahead = info[1]
+    roles = Roles(failed, n)
+    ahead = roles.ahead()
     lag_of = {True: LAG * (ahead - 1), False: LAG * (n - ahead - 1)}
 
     def fetch(j):
@@ -509,7 +554,7 @@
             for k in range(3):
                 store(j, k).wait()
 
-    @pl.when(info[0] == 1)
+    @pl.when(roles.lost)
     def _():
         for j in range(min(FETCHED - 1, count)):
             fetch(j).start()
@@ -545,7 +590,7 @@
             finish(j)
 
 
-def patch(info, hidden_t, outs, got, arrivals, news, after, chunks, n):
+def patch(failed, n, hidden_t, outs, got, arrivals, news, after, chunks):
     rows, width = news[0].shape
     chunk = rows // chunks
     count = len(got)
@@ -572,24 +617,15 @@
             2 * count * chunk * width,
         ),
         name="patch",
-    )(info, hidden_t, outs, *got, *news, *after)
+    )(failed, hidden_t, outs, *got, *news, *after)
 
 
 def per_device(tokens, d_out, w_gate, w_up, w_down, failed, master, moment1, moment2):
     n = lax.axis_size("replica")
-    me = lax.axis_index("replica")
     _, rows, width = master.shape
     features, units = w_gate.shape
 
-    failed_id = failed[0]
-    source = (failed_id + 1) % n
     order = ring_order(n)
-    place = jnp.array([order.index(i) for i in range(n)], jnp.int32)
-    ahead = (place[failed_id] - place[source]) % n
-    lost = (me == failed_id).astype(jnp.int32)
-    flag = jnp.stack([(me == source).astype(jnp.int32), lost])
-    info = jnp.stack([lost, ahead.astype(jnp.int32)])
-    targets = jnp.array(order, jnp.int32)[(place[me] + jnp.arange(n)) % n]
 
     state = (master, moment1, moment2)
     chunks = largest(
@@ -621,7 +657,8 @@
             )
         sends.append(
             pack(
-                (flag, targets) if seen else (),
+                failed,
+                n,
                 state,
                 seen,
                 parcel,
@@ -667,12 +704,12 @@
                 blocks.append(got[parcel_from + LAG * hop][way])
                 places.append(blocks[-1].shape[0] - both.shape[0])
         return collect(
-            flag, targets, both, hidden, blocks, places, 3 * chunk, width, after
+            failed, n, both, hidden, blocks, places, 3 * chunk, width, after
         )
 
     def update_part(first, count, after):
         return update(
-            info, hidden_t, outs, state, news, after, n - 1.0, block, first, count
+            failed, n, hidden_t, outs, state, news, after, block, first, count
         )
 
     def patch_to(step, after):
@@ -682,7 +719,7 @@
             return news
         blocks = [b for s in range(patched, step) for b in got[s]]
         patched = step
-        return patch(info, hidden_t, outs, blocks, arrivals, news, after, chunks, n)
+        return patch(failed, n, hidden_t, outs, blocks, arrivals, news, after, chunks)
 
     block = largest((b for b in range(TILE, 193, TILE) if rows % b == 0), rows)
     blocks = rows // block

time: 205 us -> 167 us (0.81)
  Pallas kernels: 126 us -> 81.5 us
  waiting for transfers between devices: 21.8 us -> 36 us
  starting transfers between devices: 33.1 us -> 30.4 us
  local copies, waits for them, and re-layouts: 3.27 us -> 0.91 us
    pallas_call x15, Pallas kernels: 95.5 us -> 52.8 us  [the longest x12 33.5 us: pack(): pl.pallas_call(functools.partial(pack_body, n=n, places=places, chunk=chu...]
    ppermute x12, waiting for transfers between devices: 6.48 us -> 16.2 us  [send(): lax.ppermute(sends[-1][0], 'replica', forward)]
    ppermute x12, waiting for transfers between devices: 3.96 us -> 12.9 us  [send(): lax.ppermute(sends[-1][1], 'replica', backward)]
    ppermute x3, waiting for transfers between devices: 11.4 us -> 6.88 us  [advance(): self.arrived = (lax.ppermute(sent, axis, route),)]
    ppermute x3, starting transfers between devices: 1.23 us -> 4.52 us  [advance(): self.arrived = (lax.ppermute(sent, axis, route),)]
    ppermute x12, starting transfers between devices: 23.1 us -> 20.1 us  [send(): lax.ppermute(sends[-1][1], 'replica', backward)]
    ppermute x12, starting transfers between devices: 8.75 us -> 5.78 us  [send(): lax.ppermute(sends[-1][0], 'replica', forward)]
  transfers between devices with their start and end apart: 27 -> 27, of which waited for: 8 -> 14; matrix products, arithmetic and copies ran while one was open for 2% -> 0% of each run, Pallas kernels for 60% -> 47%
where the time goes in v6:
time: 167 us; the launch traced here: 166 us
  Pallas kernels  81.5 us (49%)
  waiting for transfers between devices  36 us (22%)
  starting transfers between devices  30.4 us (18%)
  blocking collectives  14.9 us (9%)
  between operations  1.99 us (1%)
    pallas_call x12, Pallas kernels, pack(): pl.pallas_call(functools.partial(pack_body, n=n, places=places, chunk=chu...  33.5 us
    pallas_call x4, Pallas kernels, layer(): pl.pallas_call(functools.partial(layer_body, resumed=resumed, tile=tile,...  26.7 us
    ppermute x12, starting transfers between devices, send(): lax.ppermute(sends[-1][1], 'replica', backward)  20.1 us
    pallas_call x2, Pallas kernels, update(): pl.pallas_call(functools.partial(update_body, n=n, block=block, first=fir...  18.7 us
    ppermute x12, waiting for transfers between devices, send(): lax.ppermute(sends[-1][0], 'replica', forward)  16.2 us
    all_gather x1, blocking collectives, per_device(): both = lax.all_gather(both, ('fsdp', 'tensor'), axis=0, tiled=True)  14.9 us
    ppermute x12, waiting for transfers between devices, send(): lax.ppermute(sends[-1][1], 'replica', backward)  12.9 us
    ppermute x3, waiting for transfers between devices, advance(): self.arrived = (lax.ppermute(sent, axis, route),)  6.88 us
  transfers between devices with their start and end apart: 27, of which 14 were waited for; matrix products, arithmetic and copies ran while one was open for 0% of the time, Pallas kernels for 47%

profile of v6, /device:TPU:0, one launch (start us, length us, event | category | flops | bytes accessed | tf_op | source)
XLA Modules:
  0.0 165.6 jit_solution(17576423948157844714)
XLA Ops:
  0.6 2.8 %pack.12 = (bf16[288,1024]{1,0:T(8,128)(2,1)S(1)}, bf16[288,1024]{1,0:T(8,128)(2,1)}) custom-call(f32[2,1920,1024]{2,1,0:T(8,128)} %refs_0_.25, f32[2,1920,1024]{2,1,0:T(8,128)} %refs_1_.35, f32[2,1920,1024]{2,1,0:T(8,128)} %refs_2_.35), custom_call_target="tpu_custom_call" | custom-call | bytes 3538944 | tf_op jit(solution)/shard_map/pack/pallas_call | solution.py:198
  3.4 3.0 %collective-permute-start.1 = (bf16[288,1024]{1,0:T(8,128)(2,1)}, bf16[288,1024]{1,0:T(8,128)(2,1)S(1)}, u32[]{:S(2)}, u32[]{:S(2)}) collective-permute-start(bf16[288,1024]{1,0:T(8,128)(2,1)} %get-tuple-element.64), channel_id=1, source_target_pairs={{8,0},{24,8},{16,24},{0,16},{9,1},{25,9},{17,25},{1,17},{10,2},{26... | collective-permute-start | bytes 1769480 | tf_op jit(solution)/shard_map/ppermute | solution.py:675
  6.5 2.4 %pack.13 = (bf16[288,1024]{1,0:T(8,128)(2,1)}, bf16[288,1024]{1,0:T(8,128)(2,1)}) custom-call(f32[2,1920,1024]{2,1,0:T(8,128)} %refs_0_.25, f32[2,1920,1024]{2,1,0:T(8,128)} %refs_1_.35, f32[2,1920,1024]{2,1,0:T(8,128)} %refs_2_.35, bf16[288,1024]{1,0:T(8,128)(2,1)S(1)} %get-tuple-element.62.refs_3_), custom_call_target="tpu_custom_call" | custom-call | bytes 3538944 | tf_op jit(solution)/shard_map/pack/pallas_call | solution.py:198
  8.9 2.0 %collective-permute-start.3 = (bf16[288,1024]{1,0:T(8,128)(2,1)}, bf16[288,1024]{1,0:T(8,128)(2,1)S(1)}, u32[]{:S(2)}, u32[]{:S(2)}) collective-permute-start(bf16[288,1024]{1,0:T(8,128)(2,1)} %get-tuple-element.67), channel_id=1, source_target_pairs={{8,0},{24,8},{16,24},{0,16},{9,1},{25,9},{17,25},{1,17},{10,2},{26... | collective-permute-start | bytes 1769480 | tf_op jit(solution)/shard_map/ppermute | solution.py:675
  11.7 14.9 %all-gather = bf16[8,2,8192]{2,1,0:T(2,128)(2,1)S(1)} all-gather(bf16[1,2,8192]{2,1,0:T(2,128)(2,1)S(1)} %bitcast.7), channel_id=1, replica_groups=mesh['replica'=4,'fsdp'=4,'tensor'=2] {'fsdp','tensor'}, dimensions={0}, use_global_device_ids=true | all-gather | bytes 294912 | tf_op jit(solution)/shard_map/all_gather | solution.py:683
  26.7 3.1 %pack.14 = (bf16[288,1024]{1,0:T(8,128)(2,1)S(1)}, bf16[288,1024]{1,0:T(8,128)(2,1)S(1)}) custom-call(s32[1]{0:T(128)S(6)} %copy.43.refs_0_.failed, f32[2,1920,1024]{2,1,0:T(8,128)} %refs_0_.25, f32[2,1920,1024]{2,1,0:T(8,128)} %refs_1_.35, f32[2,1920,1024]{2,1,0:T(8,128)} %refs_2_.35, bf16[288,1024]{1,0:T(8,128)(2,1)S(1)} %collective-permute-done.refs_4_.refs_0_, ...), custom_call_target="tpu_custom_call" | custom-call | bytes 3538944 | tf_op jit(solution)/shard_map/pack/pallas_call | solution.py:198
  29.8 1.7 %collective-permute-start.5 = (bf16[288,1024]{1,0:T(8,128)(2,1)S(1)}, bf16[288,1024]{1,0:T(8,128)(2,1)S(1)}, u32[]{:S(2)}, u32[]{:S(2)}) collective-permute-start(bf16[288,1024]{1,0:T(8,128)(2,1)S(1)} %get-tuple-element.70), channel_id=1, source_target_pairs={{8,0},{24,8},{16,24},{0,16},{9,1},{25,9},{17,25},{1,17},{10,2},{26... | collective-permute-start | bytes 1769480 | tf_op jit(solution)/shard_map/ppermute | solution.py:675
  31.9 5.7 %layer.4 = (bf16[16,384]{1,0:T(8,128)(2,1)S(1)}, f32[16,4096]{1,0:T(8,128)S(1)}) custom-call(bf16[16,8192]{1,0:T(8,128)(2,1)S(1)} %reshape.9.refs_6_.both, bf16[4096,1920]{1,0:T(8,128)(2,1)} %refs_0_.23, bf16[4096,1920]{1,0:T(8,128)(2,1)} %refs_1_.27, bf16[1920,4096]{1,0:T(8,128)(2,1)} %refs_2_.27, bf16[288,1024]{1,0:T(8,128)(2,1)S(1)} %get-tuple-element.65.refs_3_), custom_call_target="tpu_custom_call" | custom-call | flops 251658240 | bytes 9437184 | tf_op jit(solution)/shard_map/layer/pallas_call | solution.py:299
  37.6 3.1 %pack.15 = (bf16[288,1024]{1,0:T(8,128)(2,1)S(1)}, bf16[288,1024]{1,0:T(8,128)(2,1)S(1)}) custom-call(s32[1]{0:T(128)S(6)} %copy.43.refs_0_.failed, f32[2,1920,1024]{2,1,0:T(8,128)} %refs_0_.25, f32[2,1920,1024]{2,1,0:T(8,128)} %refs_1_.35, f32[2,1920,1024]{2,1,0:T(8,128)} %refs_2_.35, bf16[288,1024]{1,0:T(8,128)(2,1)S(1)} %collective-permute-done.2.refs_4_.refs_2_, ...), custom_call_target="tpu_custom_call" | custom-call | bytes 3538944 | tf_op jit(solution)/shard_map/pack/pallas_call | solution.py:198
  40.8 1.8 %collective-permute-start.7 = (bf16[288,1024]{1,0:T(8,128)(2,1)S(1)}, bf16[288,1024]{1,0:T(8,128)(2,1)S(1)}, u32[]{:S(2)}, u32[]{:S(2)}) collective-permute-start(bf16[288,1024]{1,0:T(8,128)(2,1)S(1)} %get-tuple-element.73), channel_id=1, source_target_pairs={{8,0},{24,8},{16,24},{0,16},{9,1},{25,9},{17,25},{1,17},{10,2},{26... | collective-permute-start | bytes 1769480 | tf_op jit(solution)/shard_map/ppermute | solution.py:675
  42.8 7.0 %layer.5 = (bf16[16,512]{1,0:T(8,128)(2,1)S(1)}, f32[16,4096]{1,0:T(8,128)S(1)}) custom-call(bf16[16,8192]{1,0:T(8,128)(2,1)S(1)} %reshape.9.refs_6_.both, bf16[4096,1920]{1,0:T(8,128)(2,1)} %refs_0_.23, bf16[4096,1920]{1,0:T(8,128)(2,1)} %refs_1_.27, bf16[1920,4096]{1,0:T(8,128)(2,1)} %refs_2_.27, f32[16,4096]{1,0:T(8,128)S(1)} %get-tuple-element.66.refs_6_.refs_3_, ...), custom_call_target="tpu_custom_call" | custom-call | flops 335544320 | bytes 12582912 | tf_op jit(solution)/shard_map/layer/pallas_call | solution.py:299
  49.9 3.0 %pack.16 = (bf16[288,1024]{1,0:T(8,128)(2,1)S(1)}, bf16[288,1024]{1,0:T(8,128)(2,1)S(1)}) custom-call(s32[1]{0:T(128)S(6)} %copy.43.refs_0_.failed, f32[2,1920,1024]{2,1,0:T(8,128)} %refs_0_.25, f32[2,1920,1024]{2,1,0:T(8,128)} %refs_1_.35, f32[2,1920,1024]{2,1,0:T(8,128)} %refs_2_.35, bf16[288,1024]{1,0:T(8,128)(2,1)S(1)} %collective-permute-done.4.refs_4_, ...), custom_call_target="tpu_custom_call" | custom-call | bytes 3538944 | tf_op jit(solution)/shard_map/pack/pallas_call | solution.py:198
  52.9 2.0 %collective-permute-start.9 = (bf16[288,1024]{1,0:T(8,128)(2,1)S(1)}, bf16[288,1024]{1,0:T(8,128)(2,1)S(1)}, u32[]{:S(2)}, u32[]{:S(2)}) collective-permute-start(bf16[288,1024]{1,0:T(8,128)(2,1)S(1)} %get-tuple-element.76), channel_id=1, source_target_pairs={{8,0},{24,8},{16,24},{0,16},{9,1},{25,9},{17,25},{1,17},{10,2},{26... | collective-permute-start | bytes 1769480 | tf_op jit(solution)/shard_map/ppermute | solution.py:675
  55.0 7.0 %layer.6 = (bf16[16,512]{1,0:T(8,128)(2,1)S(1)}, f32[16,4096]{1,0:T(8,128)S(1)}) custom-call(bf16[16,8192]{1,0:T(8,128)(2,1)S(1)} %reshape.9.refs_6_.both, bf16[4096,1920]{1,0:T(8,128)(2,1)} %refs_0_.23, bf16[4096,1920]{1,0:T(8,128)(2,1)} %refs_1_.27, bf16[1920,4096]{1,0:T(8,128)(2,1)} %refs_2_.27, f32[16,4096]{1,0:T(8,128)S(1)} %get-tuple-element.69.refs_6_.refs_3_, ...), custom_call_target="tpu_custom_call" | custom-call | flops 335544320 | bytes 12582912 | tf_op jit(solution)/shard_map/layer/pallas_call | solution.py:299
  62.0 2.8 %pack.17 = (bf16[288,1024]{1,0:T(8,128)(2,1)}, bf16[288,1024]{1,0:T(8,128)(2,1)}) custom-call(s32[1]{0:T(128)S(6)} %copy.43.refs_0_.failed, f32[2,1920,1024]{2,1,0:T(8,128)} %refs_0_.25, f32[2,1920,1024]{2,1,0:T(8,128)} %refs_1_.35, f32[2,1920,1024]{2,1,0:T(8,128)} %refs_2_.35, bf16[288,1024]{1,0:T(8,128)(2,1)S(1)} %collective-permute-done.6.refs_4_.refs_6_, ...), custom_call_target="tpu_custom_call" | custom-call | bytes 3538944 | tf_op jit(solution)/shard_map/pack/pallas_call | solution.py:198
  64.8 1.8 %collective-permute-start.12 = (bf16[288,1024]{1,0:T(8,128)(2,1)}, bf16[288,1024]{1,0:T(8,128)(2,1)S(1)}, u32[]{:S(2)}, u32[]{:S(2)}) collective-permute-start(bf16[288,1024]{1,0:T(8,128)(2,1)} %get-tuple-element.84), channel_id=1, source_target_pairs={{8,0},{24,8},{16,24},{0,16},{9,1},{25,9},{17,25},{1,17},{10,2},{26... | collective-permute-start | bytes 1769480 | tf_op jit(solution)/shard_map/ppermute | solution.py:675
  66.9 7.0 %layer.7 = (bf16[16,512]{1,0:T(8,128)(2,1)S(1)}, f32[16,4096]{1,0:T(8,128)S(1)}) custom-call(bf16[16,8192]{1,0:T(8,128)(2,1)S(1)} %reshape.9.refs_6_.both, bf16[4096,1920]{1,0:T(8,128)(2,1)} %refs_0_.23, bf16[4096,1920]{1,0:T(8,128)(2,1)} %refs_1_.27, bf16[1920,4096]{1,0:T(8,128)(2,1)} %refs_2_.27, f32[16,4096]{1,0:T(8,128)S(1)} %get-tuple-element.72.refs_6_.refs_3_, ...), custom_call_target="tpu_custom_call" | custom-call | flops 335544320 | bytes 12582912 | tf_op jit(solution)/shard_map/layer/pallas_call | solution.py:299
  74.0 2.9 %pack.18 = (bf16[352,1024]{1,0:T(8,128)(2,1)}, bf16[336,1024]{1,0:T(8,128)(2,1)}) custom-call(s32[1]{0:T(128)S(6)} %copy.43.refs_0_.failed, f32[2,1920,1024]{2,1,0:T(8,128)} %refs_0_.25, f32[2,1920,1024]{2,1,0:T(8,128)} %refs_1_.35, f32[2,1920,1024]{2,1,0:T(8,128)} %refs_2_.35, bf16[288,1024]{1,0:T(8,128)(2,1)S(1)} %collective-permute-done.8.refs_4_.refs_8_, ...), custom_call_target="tpu_custom_call" | custom-call | bytes 3538944 | tf_op jit(solution)/shard_map/pack/pallas_call | solution.py:198
  76.9 1.6 collective-permute-start.14
  79.6 4.3 %collective-permute-done.12.refs_5_.refs_1_ = bf16[288,1024]{1,0:T(8,128)(2,1)S(1)} collective-permute-done((bf16[288,1024]{1,0:T(8,128)(2,1)}, bf16[288,1024]{1,0:T(8,128)(2,1)S(1)}, u32[]{:S(2)}, u32[]{:S(2)}) %collective-permute-start.12) | collective-permute-done | bytes 589856 | tf_op jit(solution)/shard_map/ppermute | solution.py:675
  83.9 1.8 %collective-permute-done.11.refs_4_.refs_0_ = bf16[288,1024]{1,0:T(8,128)(2,1)} collective-permute-done((bf16[288,1024]{1,0:T(8,128)(2,1)}, bf16[288,1024]{1,0:T(8,128)(2,1)}, u32[]{:S(2)}, u32[]{:S(2)}) %collective-permute-start.11) | collective-permute-done | bytes 589856 | tf_op jit(solution)/shard_map/ppermute | solution.py:674
  85.7 2.4 %pack.19 = (bf16[288,1024]{1,0:T(8,128)(2,1)}, bf16[288,1024]{1,0:T(8,128)(2,1)}) custom-call(s32[1]{0:T(128)S(6)} %copy.43.refs_0_.failed, f32[2,1920,1024]{2,1,0:T(8,128)} %refs_0_.25, f32[2,1920,1024]{2,1,0:T(8,128)} %refs_1_.35, f32[2,1920,1024]{2,1,0:T(8,128)} %refs_2_.35, bf16[288,1024]{1,0:T(8,128)(2,1)} %collective-permute-done.11.refs_4_.refs_0_, ...), custom_call_target="tpu_custom_call" | custom-call | bytes 3538944 | tf_op jit(solution)/shard_map/pack/pallas_call | solution.py:198
  88.2 1.2 collective-permute-start.18
  89.4 0.8 collective-permute-start.17
  90.2 2.9 %collective-permute-start.10 = (f32[8,4096]{1,0:T(8,128)}, f32[8,4096]{1,0:T(8,128)S(1)}, u32[]{:S(2)}, u32[]{:S(2)}) collective-permute-start(f32[8,4096]{1,0:T(8,128)} %get-tuple-element.83), channel_id=1, source_target_pairs={{0,4},{2,6},{4,0},{6,2},{1,5},{3,7},{5,1},{7,3},{8,12},{10,14},{12... | collective-permute-start | bytes 393224 | tf_op jit(solution)/shard_map/ppermute | solution.py:372
  93.1 4.6 %collective-permute-done.10.refs_1_ = f32[8,4096]{1,0:T(8,128)S(1)} collective-permute-done((f32[8,4096]{1,0:T(8,128)}, f32[8,4096]{1,0:T(8,128)S(1)}, u32[]{:S(2)}, u32[]{:S(2)}) %collective-permute-start.10) | collective-permute-done | bytes 131104 | tf_op jit(solution)/shard_map/ppermute | solution.py:372
  97.7 0.9 collective-permute-done.15.refs_5_.refs_6_.refs_3_
  98.7 2.4 %collective-permute-done.14.refs_4_.refs_2_ = bf16[352,1024]{1,0:T(8,128)(2,1)S(1)} collective-permute-done((bf16[352,1024]{1,0:T(8,128)(2,1)}, bf16[352,1024]{1,0:T(8,128)(2,1)S(1)}, u32[]{:S(2)}, u32[]{:S(2)}) %collective-permute-start.14) | collective-permute-done | bytes 720928 | tf_op jit(solution)/shard_map/ppermute | solution.py:674
  101.1 2.7 %pack.20 = (bf16[336,1024]{1,0:T(8,128)(2,1)}, bf16[288,1024]{1,0:T(8,128)(2,1)}) custom-call(s32[1]{0:T(128)S(6)} %copy.43.refs_0_.failed, f32[2,1920,1024]{2,1,0:T(8,128)} %refs_0_.25, f32[2,1920,1024]{2,1,0:T(8,128)} %refs_1_.35, f32[2,1920,1024]{2,1,0:T(8,128)} %refs_2_.35, bf16[352,1024]{1,0:T(8,128)(2,1)S(1)} %collective-permute-done.14.refs_4_.refs_2_, ...), custom_call_target="tpu_custom_call" | custom-call | bytes 3538944 | tf_op jit(solution)/shard_map/pack/pallas_call | solution.py:198
  104.2 1.7 %collective-permute-start.13 = (f32[4,4096]{1,0:T(4,128)S(1)}, f32[4,4096]{1,0:T(4,128)S(1)}, u32[]{:S(2)}, u32[]{:S(2)}) collective-permute-start(f32[4,4096]{1,0:T(4,128)S(1)} %get-tuple-element.87), channel_id=1, source_target_pairs={{0,2},{2,0},{4,6},{6,4},{1,3},{3,1},{5,7},{7,5},{8,10},{10,8},{12,... | collective-permute-start | bytes 196616 | tf_op jit(solution)/shard_map/ppermute | solution.py:372
  105.9 1.5 collective-permute-start.20
  107.5 1.1 collective-permute-done.13.refs_1_
  108.5 2.9 %collective-permute-done.18.refs_5_ = bf16[288,1024]{1,0:T(8,128)(2,1)} collective-permute-done((bf16[288,1024]{1,0:T(8,128)(2,1)}, bf16[288,1024]{1,0:T(8,128)(2,1)}, u32[]{:S(2)}, u32[]{:S(2)}) %collective-permute-start.18) | collective-permute-done | bytes 589856 | tf_op jit(solution)/shard_map/ppermute | solution.py:675
  111.4 2.4 %collective-permute-done.17.refs_4_ = bf16[288,1024]{1,0:T(8,128)(2,1)} collective-permute-done((bf16[288,1024]{1,0:T(8,128)(2,1)}, bf16[288,1024]{1,0:T(8,128)(2,1)}, u32[]{:S(2)}, u32[]{:S(2)}) %collective-permute-start.17) | collective-permute-done | bytes 589856 | tf_op jit(solution)/shard_map/ppermute | solution.py:674
  113.8 2.8 %pack.21 = (bf16[288,1024]{1,0:T(8,128)(2,1)S(1)}, bf16[288,1024]{1,0:T(8,128)(2,1)S(1)}) custom-call(s32[1]{0:T(128)S(6)} %copy.43.refs_0_.failed, f32[2,1920,1024]{2,1,0:T(8,128)} %refs_0_.25, f32[2,1920,1024]{2,1,0:T(8,128)} %refs_1_.35, f32[2,1920,1024]{2,1,0:T(8,128)} %refs_2_.35, bf16[288,1024]{1,0:T(8,128)(2,1)} %collective-permute-done.17.refs_4_, ...), custom_call_target="tpu_custom_call" | custom-call | bytes 3538944 | tf_op jit(solution)/shard_map/pack/pallas_call | solution.py:198
  116.6 1.3 collective-permute-start.22
  118.7 1.2 collective-permute-done.16.refs_1_
  120.5 3.5 %collective-permute-done.20.refs_5_.refs_7_ = bf16[288,1024]{1,0:T(8,128)(2,1)} collective-permute-done((bf16[288,1024]{1,0:T(8,128)(2,1)}, bf16[288,1024]{1,0:T(8,128)(2,1)}, u32[]{:S(2)}, u32[]{:S(2)}) %collective-permute-start.20) | collective-permute-done | bytes 589856 | tf_op jit(solution)/shard_map/ppermute | solution.py:675
  124.0 4.4 %collective-permute-done.19.refs_4_.refs_5_.refs_6_ = bf16[336,1024]{1,0:T(8,128)(2,1)S(1)} collective-permute-done((bf16[336,1024]{1,0:T(8,128)(2,1)}, bf16[336,1024]{1,0:T(8,128)(2,1)S(1)}, u32[]{:S(2)}, u32[]{:S(2)}) %collective-permute-start.19) | collective-permute-done | bytes 688160 | tf_op jit(solution)/shard_map/ppermute | solution.py:674
  129.2 2.8 %pack.22 = (bf16[288,1024]{1,0:T(8,128)(2,1)S(1)}, bf16[288,1024]{1,0:T(8,128)(2,1)S(1)}) custom-call(s32[1]{0:T(128)S(6)} %copy.43.refs_0_.failed, f32[2,1920,1024]{2,1,0:T(8,128)} %refs_0_.25, f32[2,1920,1024]{2,1,0:T(8,128)} %refs_1_.35, f32[2,1920,1024]{2,1,0:T(8,128)} %refs_2_.35, bf16[336,1024]{1,0:T(8,128)(2,1)S(1)} %collective-permute-done.19.refs_4_.refs_5_.refs_6_, ...), custom_call_target="tpu_custom_call" | custom-call | bytes 3538944 | tf_op jit(solution)/shard_map/pack/pallas_call | solution.py:198
  131.9 1.3 collective-permute-start.26
  134.8 4.7 %update.2 = (f32[1920,1024]{1,0:T(8,128)}, f32[1920,1024]{1,0:T(8,128)}, f32[1920,1024]{1,0:T(8,128)}) custom-call(s32[1]{0:T(128)S(6)} %copy.43.refs_0_.failed, bf16[1920,64]{1,0:T(8,128)(2,1)S(1)} %get-tuple-element.96.hid_ref.refs_3_, bf16[64,1024]{1,0:T(8,128)(2,1)S(1)} %get-tuple-element.97.out_ref, f32[2,1920,1024]{2,1,0:T(8,128)} %refs_0_.25, ...), custom_call_target="tpu_custom_call" | custom-call | flops 50331648 | bytes 9437184 | tf_op jit(solution)/shard_map/update/pallas_call | solution.py:493
  139.8 1.2 collective-permute-done.21.refs_4_.refs_8_
  141.1 2.8 %pack.23 = (bf16[288,1024]{1,0:T(8,128)(2,1)S(1)}, bf16[288,1024]{1,0:T(8,128)(2,1)S(1)}) custom-call(s32[1]{0:T(128)S(6)} %copy.43.refs_0_.failed, f32[2,1920,1024]{2,1,0:T(8,128)} %refs_0_.25, f32[2,1920,1024]{2,1,0:T(8,128)} %refs_1_.35, f32[2,1920,1024]{2,1,0:T(8,128)} %refs_2_.35, bf16[288,1024]{1,0:T(8,128)(2,1)S(1)} %collective-permute-done.21.refs_4_.refs_8_, ...), custom_call_target="tpu_custom_call" | custom-call | bytes 3538944 | tf_op jit(solution)/shard_map/pack/pallas_call | solution.py:198
  143.9 1.9 %collective-permute-start.24 = (bf16[288,1024]{1,0:T(8,128)(2,1)S(1)}, bf16[288,1024]{1,0:T(8,128)(2,1)S(1)}, u32[]{:S(2)}, u32[]{:S(2)}) collective-permute-start(bf16[288,1024]{1,0:T(8,128)(2,1)S(1)} %get-tuple-element.104), channel_id=1, source_target_pairs={{8,0},{24,8},{16,24},{0,16},{9,1},{25,9},{17,25},{1,17},{10,2},{26... | collective-permute-start | bytes 1769480 | tf_op jit(solution)/shard_map/ppermute | solution.py:675
  145.9 14.0 %update.3 = (f32[1920,1024]{1,0:T(8,128)}, f32[1920,1024]{1,0:T(8,128)}, f32[1920,1024]{1,0:T(8,128)}) custom-call(s32[1]{0:T(128)S(6)} %copy.43.refs_0_.failed, bf16[1920,64]{1,0:T(8,128)(2,1)S(1)} %get-tuple-element.96.hid_ref.refs_3_, bf16[64,1024]{1,0:T(8,128)(2,1)S(1)} %get-tuple-element.97.out_ref, ...), custom_call_target="tpu_custom_call", output_to_operand_aliasing={{0}: (6, {}), {1}: (7, {}), {2}: (8, {})} | custom-call | flops 201326592 | bytes 37748736 | tf_op jit(solution)/shard_map/update/pallas_call | solution.py:493
  160.2 1.2 collective-permute-done.24.refs_1_
  161.4 3.9 %collective-permute-done.23.refs_0_ = bf16[288,1024]{1,0:T(8,128)(2,1)S(1)} collective-permute-done((bf16[288,1024]{1,0:T(8,128)(2,1)S(1)}, bf16[288,1024]{1,0:T(8,128)(2,1)S(1)}, u32[]{:S(2)}, u32[]{:S(2)}) %collective-permute-start.23) | collective-permute-done | bytes 589856 | tf_op jit(solution)/shard_map/ppermute | solution.py:674
  (82 shorter events, 7.5 us)
Async XLA Ops:
  3.4 23.3 %collective-permute-start.1 = (bf16[288,1024]{1,0:T(8,128)(2,1)}, bf16[288,1024]{1,0:T(8,128)(2,1)S(1)}, u32[]{:S(2)}, u32[]{:S(2)}) collective-permute-start(bf16[288,1024]{1,0:T(8,128)(2,1)} %get-tuple-element.64), channel_id=1, source_target_pairs={{8,0},{24,8},{16,24},{0,16},{9,1},{25,9},{17,25},{1,17},{10,2},{26... | collective-permute-start | bytes 1769480 | tf_op jit(solution)/shard_map/ppermute | solution.py:675
  6.4 5.2 %copy-start.21 = (bf16[1,2,4096]{2,1,0:T(2,128)(2,1)S(1)}, bf16[1,2,4096]{2,1,0:T(2,128)(2,1)}, u32[]{:S(2)}) copy-start(bf16[1,2,4096]{2,1,0:T(2,128)(2,1)} %param.9) | copy-start | bytes 49156
  6.4 5.2 %copy-start.22 = (bf16[1,2,4096]{2,1,0:T(2,128)(2,1)S(1)}, bf16[1,2,4096]{2,1,0:T(2,128)(2,1)}, u32[]{:S(2)}) copy-start(bf16[1,2,4096]{2,1,0:T(2,128)(2,1)} %param.10) | copy-start | bytes 49156
  6.4 20.2 %collective-permute-start = (bf16[288,1024]{1,0:T(8,128)(2,1)S(1)}, bf16[288,1024]{1,0:T(8,128)(2,1)S(1)}, u32[]{:S(2)}, u32[]{:S(2)}) collective-permute-start(bf16[288,1024]{1,0:T(8,128)(2,1)S(1)} %get-tuple-element.62.refs_3_), channel_id=1, source_target_pairs={{0,8},{8,24},{24,16},{16,0},{1,9},{9,25},{25,17},{17,1},{2,10},{10... | collective-permute-start | bytes 1769480 | tf_op jit(solution)/shard_map/ppermute | solution.py:674
  8.9 28.7 %collective-permute-start.3 = (bf16[288,1024]{1,0:T(8,128)(2,1)}, bf16[288,1024]{1,0:T(8,128)(2,1)S(1)}, u32[]{:S(2)}, u32[]{:S(2)}) collective-permute-start(bf16[288,1024]{1,0:T(8,128)(2,1)} %get-tuple-element.67), channel_id=1, source_target_pairs={{8,0},{24,8},{16,24},{0,16},{9,1},{25,9},{17,25},{1,17},{10,2},{26... | collective-permute-start | bytes 1769480 | tf_op jit(solution)/shard_map/ppermute | solution.py:675
  10.9 26.7 %collective-permute-start.2 = (bf16[288,1024]{1,0:T(8,128)(2,1)}, bf16[288,1024]{1,0:T(8,128)(2,1)S(1)}, u32[]{:S(2)}, u32[]{:S(2)}) collective-permute-start(bf16[288,1024]{1,0:T(8,128)(2,1)} %get-tuple-element.63.refs_2_), channel_id=1, source_target_pairs={{0,8},{8,24},{24,16},{16,0},{1,9},{9,25},{25,17},{17,1},{2,10},{10... | collective-permute-start | bytes 1769480 | tf_op jit(solution)/shard_map/ppermute | solution.py:674
  26.7 3.1 %copy-start.1 = (bf16[288,1024]{1,0:T(8,128)(2,1)}, bf16[288,1024]{1,0:T(8,128)(2,1)S(1)}, u32[]{:S(2)}) copy-start(bf16[288,1024]{1,0:T(8,128)(2,1)S(1)} %collective-permute-done.1.refs_5_.refs_1_) | copy-start | bytes 1769476
  26.7 3.1 %copy-start.3 = (bf16[288,1024]{1,0:T(8,128)(2,1)}, bf16[288,1024]{1,0:T(8,128)(2,1)S(1)}, u32[]{:S(2)}) copy-start(bf16[288,1024]{1,0:T(8,128)(2,1)S(1)} %collective-permute-done.refs_4_.refs_0_) | copy-start | bytes 1769476
  29.8 20.0 %collective-permute-start.5 = (bf16[288,1024]{1,0:T(8,128)(2,1)S(1)}, bf16[288,1024]{1,0:T(8,128)(2,1)S(1)}, u32[]{:S(2)}, u32[]{:S(2)}) collective-permute-start(bf16[288,1024]{1,0:T(8,128)(2,1)S(1)} %get-tuple-element.70), channel_id=1, source_target_pairs={{8,0},{24,8},{16,24},{0,16},{9,1},{25,9},{17,25},{1,17},{10,2},{26... | collective-permute-start | bytes 1769480 | tf_op jit(solution)/shard_map/ppermute | solution.py:675
  31.5 18.4 %collective-permute-start.4 = (bf16[288,1024]{1,0:T(8,128)(2,1)S(1)}, bf16[288,1024]{1,0:T(8,128)(2,1)S(1)}, u32[]{:S(2)}, u32[]{:S(2)}) collective-permute-start(bf16[288,1024]{1,0:T(8,128)(2,1)S(1)} %get-tuple-element.65.refs_3_), channel_id=1, source_target_pairs={{0,8},{8,24},{24,16},{16,0},{1,9},{9,25},{25,17},{17,1},{2,10},{10... | collective-permute-start | bytes 1769480 | tf_op jit(solution)/shard_map/ppermute | solution.py:674
  37.6 3.1 %copy-start.5 = (bf16[288,1024]{1,0:T(8,128)(2,1)}, bf16[288,1024]{1,0:T(8,128)(2,1)S(1)}, u32[]{:S(2)}) copy-start(bf16[288,1024]{1,0:T(8,128)(2,1)S(1)} %collective-permute-done.3.refs_5_.refs_3_) | copy-start | bytes 1769476
  37.6 3.1 %copy-start.7 = (bf16[288,1024]{1,0:T(8,128)(2,1)}, bf16[288,1024]{1,0:T(8,128)(2,1)S(1)}, u32[]{:S(2)}) copy-start(bf16[288,1024]{1,0:T(8,128)(2,1)S(1)} %collective-permute-done.2.refs_4_.refs_2_) | copy-start | bytes 1769476
  40.8 21.2 %collective-permute-start.7 = (bf16[288,1024]{1,0:T(8,128)(2,1)S(1)}, bf16[288,1024]{1,0:T(8,128)(2,1)S(1)}, u32[]{:S(2)}, u32[]{:S(2)}) collective-permute-start(bf16[288,1024]{1,0:T(8,128)(2,1)S(1)} %get-tuple-element.73), channel_id=1, source_target_pairs={{8,0},{24,8},{16,24},{0,16},{9,1},{25,9},{17,25},{1,17},{10,2},{26... | collective-permute-start | bytes 1769480 | tf_op jit(solution)/shard_map/ppermute | solution.py:675
  42.6 19.4 %collective-permute-start.6 = (bf16[288,1024]{1,0:T(8,128)(2,1)S(1)}, bf16[288,1024]{1,0:T(8,128)(2,1)S(1)}, u32[]{:S(2)}, u32[]{:S(2)}) collective-permute-start(bf16[288,1024]{1,0:T(8,128)(2,1)S(1)} %get-tuple-element.68.refs_4_), channel_id=1, source_target_pairs={{0,8},{8,24},{24,16},{16,0},{1,9},{9,25},{25,17},{17,1},{2,10},{10... | collective-permute-start | bytes 1769480 | tf_op jit(solution)/shard_map/ppermute | solution.py:674
  49.9 3.0 %copy-start.9 = (bf16[288,1024]{1,0:T(8,128)(2,1)}, bf16[288,1024]{1,0:T(8,128)(2,1)S(1)}, u32[]{:S(2)}) copy-start(bf16[288,1024]{1,0:T(8,128)(2,1)S(1)} %collective-permute-done.4.refs_4_) | copy-start | bytes 1769476
  52.9 21.0 %collective-permute-start.9 = (bf16[288,1024]{1,0:T(8,128)(2,1)S(1)}, bf16[288,1024]{1,0:T(8,128)(2,1)S(1)}, u32[]{:S(2)}, u32[]{:S(2)}) collective-permute-start(bf16[288,1024]{1,0:T(8,128)(2,1)S(1)} %get-tuple-element.76), channel_id=1, source_target_pairs={{8,0},{24,8},{16,24},{0,16},{9,1},{25,9},{17,25},{1,17},{10,2},{26... | collective-permute-start | bytes 1769480 | tf_op jit(solution)/shard_map/ppermute | solution.py:675
  54.9 19.1 %collective-permute-start.8 = (bf16[288,1024]{1,0:T(8,128)(2,1)S(1)}, bf16[288,1024]{1,0:T(8,128)(2,1)S(1)}, u32[]{:S(2)}, u32[]{:S(2)}) collective-permute-start(bf16[288,1024]{1,0:T(8,128)(2,1)S(1)} %get-tuple-element.71.refs_4_), channel_id=1, source_target_pairs={{0,8},{8,24},{24,16},{16,0},{1,9},{9,25},{25,17},{17,1},{2,10},{10... | collective-permute-start | bytes 1769480 | tf_op jit(solution)/shard_map/ppermute | solution.py:674
  62.0 2.9 %copy-start.11 = (bf16[288,1024]{1,0:T(8,128)(2,1)}, bf16[288,1024]{1,0:T(8,128)(2,1)S(1)}, u32[]{:S(2)}) copy-start(bf16[288,1024]{1,0:T(8,128)(2,1)S(1)} %collective-permute-done.7.refs_5_.refs_7_) | copy-start | bytes 1769476
  64.8 19.1 %collective-permute-start.12 = (bf16[288,1024]{1,0:T(8,128)(2,1)}, bf16[288,1024]{1,0:T(8,128)(2,1)S(1)}, u32[]{:S(2)}, u32[]{:S(2)}) collective-permute-start(bf16[288,1024]{1,0:T(8,128)(2,1)} %get-tuple-element.84), channel_id=1, source_target_pairs={{8,0},{24,8},{16,24},{0,16},{9,1},{25,9},{17,25},{1,17},{10,2},{26... | collective-permute-start | bytes 1769480 | tf_op jit(solution)/shard_map/ppermute | solution.py:675
  66.7 19.0 %collective-permute-start.11 = (bf16[288,1024]{1,0:T(8,128)(2,1)}, bf16[288,1024]{1,0:T(8,128)(2,1)}, u32[]{:S(2)}, u32[]{:S(2)}) collective-permute-start(bf16[288,1024]{1,0:T(8,128)(2,1)} %get-tuple-element.74.refs_4_), channel_id=1, source_target_pairs={{0,8},{8,24},{24,16},{16,0},{1,9},{9,25},{25,17},{17,1},{2,10},{10... | collective-permute-start | bytes 1769480 | tf_op jit(solution)/shard_map/ppermute | solution.py:674
  73.9 2.9 %copy-start.17 = (bf16[288,1024]{1,0:T(8,128)(2,1)}, bf16[288,1024]{1,0:T(8,128)(2,1)S(1)}, u32[]{:S(2)}) copy-start(bf16[288,1024]{1,0:T(8,128)(2,1)S(1)} %collective-permute-done.9.refs_5_.refs_9_) | copy-start | bytes 1769476
  73.9 2.9 %copy-start.18 = (bf16[288,1024]{1,0:T(8,128)(2,1)}, bf16[288,1024]{1,0:T(8,128)(2,1)S(1)}, u32[]{:S(2)}) copy-start(bf16[288,1024]{1,0:T(8,128)(2,1)S(1)} %collective-permute-done.8.refs_4_.refs_8_) | copy-start | bytes 1769476
  76.9 24.2 %collective-permute-start.14 = (bf16[352,1024]{1,0:T(8,128)(2,1)}, bf16[352,1024]{1,0:T(8,128)(2,1)S(1)}, u32[]{:S(2)}, u32[]{:S(2)}) collective-permute-start(bf16[352,1024]{1,0:T(8,128)(2,1)} %get-tuple-element.81.refs_1_), channel_id=1, source_target_pairs={{0,8},{8,24},{24,16},{16,0},{1,9},{9,25},{25,17},{17,1},{2,10},{10... | collective-permute-start | bytes 2162696 | tf_op jit(solution)/shard_map/ppermute | solution.py:674
  78.5 20.2 %collective-permute-start.15 = (bf16[336,1024]{1,0:T(8,128)(2,1)}, bf16[336,1024]{1,0:T(8,128)(2,1)S(1)}, u32[]{:S(2)}, u32[]{:S(2)}) collective-permute-start(bf16[336,1024]{1,0:T(8,128)(2,1)} %get-tuple-element.88), channel_id=1, source_target_pairs={{8,0},{24,8},{16,24},{0,16},{9,1},{25,9},{17,25},{1,17},{10,2},{26... | collective-permute-start | bytes 2064392 | tf_op jit(solution)/shard_map/ppermute | solution.py:675
  83.9 4.2 %copy-start.15 = (bf16[288,1024]{1,0:T(8,128)(2,1)}, bf16[288,1024]{1,0:T(8,128)(2,1)S(1)}, u32[]{:S(2)}) copy-start(bf16[288,1024]{1,0:T(8,128)(2,1)S(1)} %collective-permute-done.12.refs_5_.refs_1_) | copy-start | bytes 1769476
  88.2 23.3 %collective-permute-start.18 = (bf16[288,1024]{1,0:T(8,128)(2,1)}, bf16[288,1024]{1,0:T(8,128)(2,1)}, u32[]{:S(2)}, u32[]{:S(2)}) collective-permute-start(bf16[288,1024]{1,0:T(8,128)(2,1)} %get-tuple-element.92), channel_id=1, source_target_pairs={{8,0},{24,8},{16,24},{0,16},{9,1},{25,9},{17,25},{1,17},{10,2},{26... | collective-permute-start | bytes 1769480 | tf_op jit(solution)/shard_map/ppermute | solution.py:675
  89.4 24.4 %collective-permute-start.17 = (bf16[288,1024]{1,0:T(8,128)(2,1)}, bf16[288,1024]{1,0:T(8,128)(2,1)}, u32[]{:S(2)}, u32[]{:S(2)}) collective-permute-start(bf16[288,1024]{1,0:T(8,128)(2,1)} %get-tuple-element.85.refs_2_), channel_id=1, source_target_pairs={{0,8},{8,24},{24,16},{16,0},{1,9},{9,25},{25,17},{17,1},{2,10},{10... | collective-permute-start | bytes 1769480 | tf_op jit(solution)/shard_map/ppermute | solution.py:674
  90.2 7.5 %collective-permute-start.10 = (f32[8,4096]{1,0:T(8,128)}, f32[8,4096]{1,0:T(8,128)S(1)}, u32[]{:S(2)}, u32[]{:S(2)}) collective-permute-start(f32[8,4096]{1,0:T(8,128)} %get-tuple-element.83), channel_id=1, source_target_pairs={{0,4},{2,6},{4,0},{6,2},{1,5},{3,7},{5,1},{7,3},{8,12},{10,14},{12... | collective-permute-start | bytes 393224 | tf_op jit(solution)/shard_map/ppermute | solution.py:372
  101.1 33.0 %copy-start = (bf16[352,1024]{1,0:T(8,128)(2,1)}, bf16[352,1024]{1,0:T(8,128)(2,1)S(1)}, u32[]{:S(2)}) copy-start(bf16[352,1024]{1,0:T(8,128)(2,1)S(1)} %collective-permute-done.14.refs_4_.refs_2_) | copy-start | bytes 2162692
  103.8 24.7 %collective-permute-start.19 = (bf16[336,1024]{1,0:T(8,128)(2,1)}, bf16[336,1024]{1,0:T(8,128)(2,1)S(1)}, u32[]{:S(2)}, u32[]{:S(2)}) collective-permute-start(bf16[336,1024]{1,0:T(8,128)(2,1)} %get-tuple-element.89.refs_2_), channel_id=1, source_target_pairs={{0,8},{8,24},{24,16},{16,0},{1,9},{9,25},{25,17},{17,1},{2,10},{10... | collective-permute-start | bytes 2064392 | tf_op jit(solution)/shard_map/ppermute | solution.py:674
  104.2 4.3 %collective-permute-start.13 = (f32[4,4096]{1,0:T(4,128)S(1)}, f32[4,4096]{1,0:T(4,128)S(1)}, u32[]{:S(2)}, u32[]{:S(2)}) collective-permute-start(f32[4,4096]{1,0:T(4,128)S(1)} %get-tuple-element.87), channel_id=1, source_target_pairs={{0,2},{2,0},{4,6},{6,4},{1,3},{3,1},{5,7},{7,5},{8,10},{10,8},{12,... | collective-permute-start | bytes 196616 | tf_op jit(solution)/shard_map/ppermute | solution.py:372
  105.9 18.1 %collective-permute-start.20 = (bf16[288,1024]{1,0:T(8,128)(2,1)}, bf16[288,1024]{1,0:T(8,128)(2,1)}, u32[]{:S(2)}, u32[]{:S(2)}) collective-permute-start(bf16[288,1024]{1,0:T(8,128)(2,1)} %get-tuple-element.94), channel_id=1, source_target_pairs={{8,0},{24,8},{16,24},{0,16},{9,1},{25,9},{17,25},{1,17},{10,2},{26... | collective-permute-start | bytes 1769480 | tf_op jit(solution)/shard_map/ppermute | solution.py:675
  116.6 23.2 %collective-permute-start.22 = (bf16[288,1024]{1,0:T(8,128)(2,1)S(1)}, bf16[288,1024]{1,0:T(8,128)(2,1)S(1)}, u32[]{:S(2)}, u32[]{:S(2)}) collective-permute-start(bf16[288,1024]{1,0:T(8,128)(2,1)S(1)} %get-tuple-element.98), channel_id=1, source_target_pairs={{8,0},{24,8},{16,24},{0,16},{9,1},{25,9},{17,25},{1,17},{10,2},{26... | collective-permute-start | bytes 1769480 | tf_op jit(solution)/shard_map/ppermute | solution.py:675
  117.9 23.2 %collective-permute-start.21 = (bf16[288,1024]{1,0:T(8,128)(2,1)S(1)}, bf16[288,1024]{1,0:T(8,128)(2,1)S(1)}, u32[]{:S(2)}, u32[]{:S(2)}) collective-permute-start(bf16[288,1024]{1,0:T(8,128)(2,1)S(1)} %get-tuple-element.93.refs_2_), channel_id=1, source_target_pairs={{0,8},{8,24},{24,16},{16,0},{1,9},{9,25},{25,17},{17,1},{2,10},{10... | collective-permute-start | bytes 1769480 | tf_op jit(solution)/shard_map/ppermute | solution.py:674
  118.7 1.2 collective-permute-start.16
  131.9 28.1 %collective-permute-start.26 = (bf16[288,1024]{1,0:T(8,128)(2,1)S(1)}, bf16[288,1024]{1,0:T(8,128)(2,1)S(1)}, u32[]{:S(2)}, u32[]{:S(2)}) collective-permute-start(bf16[288,1024]{1,0:T(8,128)(2,1)S(1)} %get-tuple-element.105), channel_id=1, source_target_pairs={{8,0},{24,8},{16,24},{0,16},{9,1},{25,9},{17,25},{1,17},{10,2},{26... | collective-permute-start | bytes 1769480 | tf_op jit(solution)/shard_map/ppermute | solution.py:675
  133.2 26.9 %collective-permute-start.25 = (bf16[288,1024]{1,0:T(8,128)(2,1)S(1)}, bf16[288,1024]{1,0:T(8,128)(2,1)S(1)}, u32[]{:S(2)}, u32[]{:S(2)}) collective-permute-start(bf16[288,1024]{1,0:T(8,128)(2,1)S(1)} %get-tuple-element.95.refs_7_), channel_id=1, source_target_pairs={{0,8},{8,24},{24,16},{16,0},{1,9},{9,25},{25,17},{17,1},{2,10},{10... | collective-permute-start | bytes 1769480 | tf_op jit(solution)/shard_map/ppermute | solution.py:674
  134.7 4.8 %copy-start.2 = (bf16[288,1024]{1,0:T(8,128)(2,1)S(1)}, bf16[288,1024]{1,0:T(8,128)(2,1)}, u32[]{:S(2)}) copy-start(bf16[288,1024]{1,0:T(8,128)(2,1)} %copy-done.1) | copy-start | bytes 1769476
  134.7 4.8 %copy-start.4 = (bf16[288,1024]{1,0:T(8,128)(2,1)S(1)}, bf16[288,1024]{1,0:T(8,128)(2,1)}, u32[]{:S(2)}) copy-start(bf16[288,1024]{1,0:T(8,128)(2,1)} %copy-done.3) | copy-start | bytes 1769476
  134.7 4.7 %copy-start.6 = (bf16[288,1024]{1,0:T(8,128)(2,1)S(1)}, bf16[288,1024]{1,0:T(8,128)(2,1)}, u32[]{:S(2)}) copy-start(bf16[288,1024]{1,0:T(8,128)(2,1)} %copy-done.5) | copy-start | bytes 1769476
  134.7 4.7 %copy-start.8 = (bf16[288,1024]{1,0:T(8,128)(2,1)S(1)}, bf16[288,1024]{1,0:T(8,128)(2,1)}, u32[]{:S(2)}) copy-start(bf16[288,1024]{1,0:T(8,128)(2,1)} %copy-done.7) | copy-start | bytes 1769476
  134.7 4.7 %copy-start.10 = (bf16[288,1024]{1,0:T(8,128)(2,1)S(1)}, bf16[288,1024]{1,0:T(8,128)(2,1)}, u32[]{:S(2)}) copy-start(bf16[288,1024]{1,0:T(8,128)(2,1)} %copy-done.9) | copy-start | bytes 1769476
  134.7 4.7 %copy-start.12 = (bf16[288,1024]{1,0:T(8,128)(2,1)S(1)}, bf16[288,1024]{1,0:T(8,128)(2,1)}, u32[]{:S(2)}) copy-start(bf16[288,1024]{1,0:T(8,128)(2,1)} %copy-done.11) | copy-start | bytes 1769476
  134.7 4.7 %copy-start.14 = (bf16[288,1024]{1,0:T(8,128)(2,1)S(1)}, bf16[288,1024]{1,0:T(8,128)(2,1)}, u32[]{:S(2)}) copy-start(bf16[288,1024]{1,0:T(8,128)(2,1)} %copy-done.13) | copy-start | bytes 1769476
  134.8 4.7 %copy-start.19 = (bf16[288,1024]{1,0:T(8,128)(2,1)S(1)}, bf16[288,1024]{1,0:T(8,128)(2,1)}, u32[]{:S(2)}) copy-start(bf16[288,1024]{1,0:T(8,128)(2,1)} %copy-done.18) | copy-start | bytes 1769476
  143.9 17.5 %collective-permute-start.24 = (bf16[288,1024]{1,0:T(8,128)(2,1)S(1)}, bf16[288,1024]{1,0:T(8,128)(2,1)S(1)}, u32[]{:S(2)}, u32[]{:S(2)}) collective-permute-start(bf16[288,1024]{1,0:T(8,128)(2,1)S(1)} %get-tuple-element.104), channel_id=1, source_target_pairs={{8,0},{24,8},{16,24},{0,16},{9,1},{25,9},{17,25},{1,17},{10,2},{26... | collective-permute-start | bytes 1769480 | tf_op jit(solution)/shard_map/ppermute | solution.py:675
  145.8 19.6 %collective-permute-start.23 = (bf16[288,1024]{1,0:T(8,128)(2,1)S(1)}, bf16[288,1024]{1,0:T(8,128)(2,1)S(1)}, u32[]{:S(2)}, u32[]{:S(2)}) collective-permute-start(bf16[288,1024]{1,0:T(8,128)(2,1)S(1)} %get-tuple-element.103.refs_6_), channel_id=1, source_target_pairs={{0,8},{8,24},{24,16},{16,0},{1,9},{9,25},{25,17},{17,1},{2,10},{10... | collective-permute-start | bytes 1769480 | tf_op jit(solution)/shard_map/ppermute | solution.py:674
  145.9 14.0 %copy-start.16 = (bf16[288,1024]{1,0:T(8,128)(2,1)S(1)}, bf16[288,1024]{1,0:T(8,128)(2,1)}, u32[]{:S(2)}) copy-start(bf16[288,1024]{1,0:T(8,128)(2,1)} %copy-done.15) | copy-start | bytes 1769476
  (2 other events, 3.6 us)
